TPU v7x, 32 devices: a whole 2x2x4 slice. The times are simulated.
32 devices in a mesh: group: 2 (over x), wide: 16 (over z, y, core).
Axes of the slice: x: 2, y: 2, z: 4, core: 2. Of those that a mesh axis runs over, the one named last changes fastest.
Arguments:
- tokens: bfloat16 [4096, 4096], P(('group', 'wide')), parts along dimension 0, may hold values from -6 to 6
- cotangent: bfloat16 [4096, 4096], P(('group', 'wide')), parts along dimension 0, may hold values from -18 to 18
- expert_ids: int32 [4096, 4], P(('group', 'wide')), parts along dimension 0, may hold values from 0 to 15, all different within a row; in each aligned block of 128 rows (0 to 127, 128 to 255, ...) at most 48 rows name the same one
- gate_codes: int32 [4096, 4], P(('group', 'wide')), parts along dimension 0, may hold values from 1 to 1023
- w_gate: bfloat16 [16, 4096, 768], P('wide'), may hold values from -0.09375 to 0.09375
- w_up: bfloat16 [16, 4096, 768], P('wide'), may hold values from -0.09375 to 0.09375
- w_down: bfloat16 [16, 768, 4096], P('wide'), may hold values from -0.21875 to 0.21875
Outputs:
- moe_out: bfloat16 [4096, 4096], P(('group', 'wide')), parts along dimension 0
- token_grad: bfloat16 [4096, 4096], P(('group', 'wide')), parts along dimension 0
There are 2 independent parts, one for each index of `group`. A program takes and returns all parts, laid end to end along the dimension named above; an argument that names none is the same for every part. Nothing has to cross between parts.
Inputs may be any that keep to these rules, and one draw needn't show every extreme that they name: `expert_ids`: each token names 4 different experts; among the routes of the tokens of one device no expert is named more than 48 times.
All inputs are finite; a program needn't handle non-finite values.
Results may differ from a plain program's by a relative error of at most 0.0064.
Values may be sent and summed in bfloat16 or wider, within the bound.
No kernel may reach another device: no remote copies, remote signals or barrier semaphores. Data moves between devices by JAX's collectives and lax.ppermute only.
A program may use at most 128 MiB of HBM per device.

v0:
```python
import jax
import jax.numpy as jnp
from jax import lax
from jax.sharding import PartitionSpec as P

contract_last = (((1,), (1,)), ((), ()))


def per_device(tokens, cotangent, expert_ids, gate_codes, w_gate, w_up, w_down):
    axis_size = lax.axis_size("wide")
    tok_rows, model_width = tokens.shape
    route_top = expert_ids.shape[1]
    capacity = 3 * tok_rows * route_top // (2 * axis_size)
    gate_values = gate_codes.astype(jnp.float32)
    gate_share = gate_values / jnp.sum(gate_values, axis=1, keepdims=True)
    flat_ids = expert_ids.reshape(-1)
    route_count = flat_ids.shape[0]
    onehot = (flat_ids[:, None] == jnp.arange(axis_size, dtype=jnp.int32)[None, :]).astype(
        jnp.int32
    )
    position = jnp.sum((jnp.cumsum(onehot, axis=0) - onehot) * onehot, axis=1)
    slot_index = flat_ids * capacity + position
    slot_owner = (
        jnp.full((axis_size * capacity,), route_count, jnp.int32)
        .at[slot_index]
        .set(jnp.arange(route_count, dtype=jnp.int32))
    )
    filled = slot_owner < route_count
    owner_route = jnp.minimum(slot_owner, route_count - 1)
    owner_token = owner_route // route_top
    slot_gate = jnp.where(filled, gate_share.reshape(-1)[owner_route], 0.0)
    send_tokens = jnp.where(filled[:, None], tokens[owner_token], jnp.zeros((), tokens.dtype))
    send_tokens = send_tokens.reshape(axis_size, capacity, model_width)
    send_cot = (slot_gate[:, None] * cotangent[owner_token].astype(jnp.float32)).astype(
        jnp.bfloat16
    )
    send_cot = send_cot.reshape(axis_size, capacity, model_width)
    gate_mat = w_gate[0]
    up_mat = w_up[0]
    down_mat = w_down[0]
    arrived = lax.all_to_all(send_tokens, "wide", split_axis=0, concat_axis=0, tiled=True)
    arrived_cot = lax.all_to_all(send_cot, "wide", split_axis=0, concat_axis=0, tiled=True)
    senders, slot_count, _ = arrived.shape
    row_block = arrived.reshape(senders * slot_count, model_width)
    cot_rows = arrived_cot.reshape(senders * slot_count, model_width)
    pre_gate = jnp.dot(row_block, gate_mat, preferred_element_type=jnp.float32)
    pre_up = jnp.dot(row_block, up_mat, preferred_element_type=jnp.float32)
    logistic = jax.nn.sigmoid(pre_gate)
    activated = pre_gate * logistic
    hidden = (activated * pre_up).astype(jnp.bfloat16)
    outputs = jnp.dot(hidden, down_mat, preferred_element_type=jnp.float32).astype(jnp.bfloat16)
    outputs = outputs.reshape(senders, slot_count, model_width)
    hidden_grad = lax.dot_general(
        cot_rows, down_mat, contract_last, preferred_element_type=jnp.float32
    )
    gate_grad = (hidden_grad * pre_up * logistic * (1.0 + pre_gate * (1.0 - logistic))).astype(
        jnp.bfloat16
    )
    up_grad = (hidden_grad * activated).astype(jnp.bfloat16)
    input_grad = lax.dot_general(
        gate_grad, gate_mat, contract_last, preferred_element_type=jnp.float32
    ) + lax.dot_general(up_grad, up_mat, contract_last, preferred_element_type=jnp.float32)
    input_grad = input_grad.astype(jnp.bfloat16).reshape(senders, slot_count, model_width)
    outputs_home = lax.all_to_all(outputs, "wide", split_axis=0, concat_axis=0, tiled=True)
    grads_home = lax.all_to_all(input_grad, "wide", split_axis=0, concat_axis=0, tiled=True)
    outputs_home, grads_home = (outputs_home, grads_home)
    route_out = outputs_home.reshape(axis_size * capacity, model_width)[slot_index]
    route_out = route_out.reshape(tok_rows, route_top, model_width)
    moe_out = jnp.sum(gate_share[:, :, None] * route_out.astype(jnp.float32), axis=1).astype(
        jnp.bfloat16
    )
    route_grad = grads_home.reshape(axis_size * capacity, model_width)[slot_index]
    route_grad = route_grad.reshape(tok_rows, route_top, model_width)
    token_grad = jnp.sum(route_grad.astype(jnp.float32), axis=1).astype(jnp.bfloat16)
    return (moe_out, token_grad)


def solution(mesh):
    return jax.shard_map(
        per_device,
        mesh=mesh,
        in_specs=(
            P(("group", "wide"), None),
            P(("group", "wide"), None),
            P(("group", "wide"), None),
            P(("group", "wide"), None),
            P("wide", None, None),
            P("wide", None, None),
            P("wide", None, None),
        ),
        out_specs=(P(("group", "wide"), None), P(("group", "wide"), None)),
        check_vma=False,
    )
```

profile of v0, /device:TPU:13, one launch (start us, length us, event | category | flops | bytes accessed | tf_op | source)
XLA Modules:
  0.0 625.0 jit_solution(18173143428789356718)
XLA Ops:
  0.6 0.0 copy-start
  0.6 0.8 broadcast_multiply_fusion
  1.4 0.8 copy.12
  2.2 0.1 eq.29
  2.3 0.1 eq.25
  2.4 0.7 convert_reduce_fusion
  3.1 0.7 convert_divide_fusion
  3.8 0.1 copy.10
  3.9 0.1 reshape.101
  4.0 0.1 copy.11
  4.2 0.1 mul.62
  4.3 1.2 reduce-window.6
  5.4 0.2 slice_reduce_fusion
  5.7 0.1 fusion.17
  5.8 2.4 scatter_custom_fusion
  8.3 5.0 gather_fusion.2
  13.3 0.1 broadcast_in_dim.33
  13.4 0.0 copy-done
  13.4 5.7 gather_fusion
  19.1 5.9 broadcast_select_fusion
  25.0 0.0 copy-start.2
  25.0 6.7 %all-to-all-start = ((bf16[16,48,4096]{2,1,0:T(8,128)(2,1)}), bf16[16,48,4096]{2,1,0:T(8,128)(2,1)}, u32[]{:S(2)}, u32[]{:S(2)}) async-start(bf16[16,48,4096]{2,1,0:T(8,128)(2,1)} %broadcast_select_fusion), calls=%async_computation | async-start | bytes 12582912 | tf_op jit(solution)/shard_map/all_to_all | solution.py:41
  31.7 0.1 mul.67
  31.8 0.0 copy-done.2
  31.8 5.7 gather_fusion.3
  37.5 7.7 %fusion = bf16[16,48,4096]{2,1,0:T(8,128)(2,1)} fusion(bf16[16,48,4096]{2,1,0:T(8,128)(2,1)} %bitcast.49, f32[16,48]{1,0:T(8,128)S(1)} %mul.67), kind=kLoop, calls=%fused_computation.7 | loop fusion | flops 9437184 | bytes 12585984 | tf_op jit(solution)/shard_map/convert_element_type | solution.py:34
  45.2 124.0 %all-to-all-done = bf16[16,48,4096]{2,1,0:T(8,128)(2,1)} async-done(((bf16[16,48,4096]{2,1,0:T(8,128)(2,1)}), bf16[16,48,4096]{2,1,0:T(8,128)(2,1)}, u32[]{:S(2)}, u32[]{:S(2)}) %all-to-all-start) | async-done | bytes 6291488 | tf_op jit(solution)/shard_map/all_to_all | solution.py:41
  169.1 5.3 all-to-all-start.2
  174.4 9.0 %fusion.9 = f32[768,768]{1,0:T(8,128)S(1)} fusion(bf16[768,4096]{1,0:T(8,128)(2,1)} %bitcast.4, bf16[1,4096,768]{2,1,0:T(8,128)(2,1)} %param.11), kind=kOutput, calls=%fused_computation.19 | convolution fusion | flops 4831838208 | bytes 14942208 | tf_op jit(solution)/shard_map/dot_general | solution.py:46
  183.4 9.0 %fusion.5 = f32[768,768]{1,0:T(8,128)S(1)} fusion(bf16[768,4096]{1,0:T(8,128)(2,1)} %bitcast.4, bf16[1,4096,768]{2,1,0:T(8,128)(2,1)} %param.12), kind=kOutput, calls=%fused_computation.15 | convolution fusion | flops 4831838208 | bytes 14942208 | tf_op jit(solution)/shard_map/dot_general | solution.py:47
  192.3 0.0 copy-start.3
  192.4 1.4 copy-done.3
  193.8 9.9 %convolution_convert_fusion = bf16[768,4096]{1,0:T(8,128)(2,1)} fusion(bf16[1,768,4096]{2,1,0:T(8,128)(2,1)} %param.13, f32[768,768]{1,0:T(8,128)S(1)} %fusion.5, f32[768,768]{1,0:T(8,128)S(1)} %fusion.9), kind=kOutput, calls=%fused_computation.10 | convolution fusion | flops 4838522880 | bytes 17301504 | tf_op jit(solution)/shard_map/dot_general | solution.py:51
  203.7 108.0 %all-to-all-done.2 = bf16[16,48,4096]{2,1,0:T(8,128)(2,1)} async-done(((bf16[16,48,4096]{2,1,0:T(8,128)(2,1)}), bf16[16,48,4096]{2,1,0:T(8,128)(2,1)}, u32[]{:S(2)}, u32[]{:S(2)}) %all-to-all-start.2) | async-done | bytes 6291488 | tf_op jit(solution)/shard_map/all_to_all | solution.py:42
  311.7 5.4 all-to-all-start.1
  317.1 0.0 copy-start.4
  317.1 0.0 slice-start
  317.1 9.2 %fusion.1 = f32[768,768]{1,0:T(8,128)S(1)} fusion(bf16[768,4096]{1,0:T(8,128)(2,1)} %bitcast.11, bf16[1,768,4096]{2,1,0:T(8,128)(2,1)} %param.13), kind=kOutput, calls=%fused_computation.11 | convolution fusion | flops 4831838208 | bytes 14942208 | tf_op jit(solution)/shard_map/dot_general | solution.py:53
  326.3 0.0 copy-done.4
  326.3 0.0 slice-start.1
  326.3 11.5 %fusion.7 = f32[768,4096]{1,0:T(8,128)} fusion(bf16[1,4096,768]{2,1,0:T(8,128)(2,1)} %param.11, f32[768,768]{1,0:T(8,128)S(1)} %fusion.9, f32[768,768]{1,0:T(8,128)S(1)} %fusion.1, f32[768,768]{1,0:T(8,128)S(1)} %copy-done.4), kind=kOutput, calls=%fused_computation.17 | convolution fusion | flops 4837736448 | bytes 25952256 | tf_op jit(solution)/shard_map/dot_general | solution.py:60
  337.9 0.0 slice-done
  337.9 0.0 slice-done.1
  337.9 9.9 %add_convert_fusion = bf16[768,4096]{1,0:T(8,128)(2,1)} fusion(f32[768,4096]{1,0:T(8,128)} %fusion.7, bf16[1,4096,768]{2,1,0:T(8,128)(2,1)S(1)} %bitcast.57, f32[768,768]{1,0:T(8,128)S(1)} %fusion.1, f32[768,768]{1,0:T(8,128)S(1)} %fusion.9), kind=kOutput, calls=%fused_computation.8 | convolution fusion | flops 4841668608 | bytes 29884416 | tf_op jit(solution)/shard_map/dot_general | solution.py:62
  347.8 106.6 %all-to-all-done.1 = bf16[16,48,4096]{2,1,0:T(8,128)(2,1)} async-done(((bf16[16,48,4096]{2,1,0:T(8,128)(2,1)}), bf16[16,48,4096]{2,1,0:T(8,128)(2,1)}, u32[]{:S(2)}, u32[]{:S(2)}) %all-to-all-start.1) | async-done | bytes 6291488 | tf_op jit(solution)/shard_map/all_to_all | solution.py:64
  454.4 4.9 all-to-all-start.3
  459.3 12.2 %gather_fusion.1 = bf16[512,4096]{1,0:T(8,128)(2,1)} fusion(bf16[768,4096]{1,0:T(8,128)(2,1)} %bitcast.9, s32[1024]{0:T(1024)S(1)} %pad_clamp_fusion.1), kind=kCustom, calls=%fused_computation.1 | custom fusion | bytes 8390656 | tf_op jit(solution)/shard_map/gather | solution.py:67
  471.4 8.5 %reshape.106 = f32[128,4,4096]{2,1,0:T(4,128)} reshape(bf16[512,4096]{1,0:T(8,128)(2,1)} %gather_fusion.1) | data formatting | bytes 12582912 | tf_op jit(solution)/shard_map/convert_element_type | solution.py:69
  479.9 10.8 %multiply_reduce_fusion = bf16[128,4096]{1,0:T(8,128)(2,1)} fusion(f32[128,4,4096]{2,1,0:T(4,128)} %reshape.106, f32[128,4]{1,0:T(8,128)S(1)} %copy.10), kind=kLoop, calls=%fused_computation.9 | loop fusion | flops 3670016 | bytes 9439232 | tf_op jit(solution)/shard_map/reduce_sum | solution.py:69
  490.7 106.0 %all-to-all-done.3 = bf16[16,48,4096]{2,1,0:T(8,128)(2,1)} async-done(((bf16[16,48,4096]{2,1,0:T(8,128)(2,1)}), bf16[16,48,4096]{2,1,0:T(8,128)(2,1)}, u32[]{:S(2)}, u32[]{:S(2)}) %all-to-all-start.3) | async-done | bytes 6291488 | tf_op jit(solution)/shard_map/all_to_all | solution.py:65
  596.7 0.0 copy-start.1
  596.7 12.2 %gather_fusion.4 = bf16[512,4096]{1,0:T(8,128)(2,1)} fusion(bf16[768,4096]{1,0:T(8,128)(2,1)} %bitcast.13, s32[1024]{0:T(1024)S(1)} %pad_clamp_fusion.1), kind=kCustom, calls=%fused_computation.4 | custom fusion | bytes 8390656 | tf_op jit(solution)/shard_map/gather | solution.py:72
  608.9 7.4 %reshape.105 = bf16[128,4,4096]{2,1,0:T(4,128)(2,1)} reshape(bf16[512,4096]{1,0:T(8,128)(2,1)} %gather_fusion.4) | data formatting | bytes 8388608 | tf_op jit(solution)/shard_map/reshape | solution.py:73
  616.3 8.5 %reduce_sum.45 = bf16[128,4096]{1,0:T(8,128)(2,1)} reduce(bf16[128,4,4096]{2,1,0:T(4,128)(2,1)} %reshape.105, bf16[]{:T(256)} %constant.38.clone.1), dimensions={1}, to_apply=%region_6.7 | reduce | flops 1572864 | bytes 5242882 | tf_op jit(solution)/shard_map/reduce_sum | solution.py:74
  624.8 0.0 copy-done.1
  (10 shorter events, 0.1 us)
Async XLA Ops:
  0.6 12.8 %copy-start = (bf16[128,4096]{1,0:T(8,128)(2,1)S(1)}, bf16[128,4096]{1,0:T(8,128)(2,1)}, u32[]{:S(2)}) copy-start(bf16[128,4096]{1,0:T(8,128)(2,1)} %param.7) | copy-start | bytes 3145732
  25.0 6.8 %copy-start.2 = (bf16[128,4096]{1,0:T(8,128)(2,1)S(1)}, bf16[128,4096]{1,0:T(8,128)(2,1)}, u32[]{:S(2)}) copy-start(bf16[128,4096]{1,0:T(8,128)(2,1)} %param.8) | copy-start | bytes 3145732
  25.0 144.1 %all-to-all-start = ((bf16[16,48,4096]{2,1,0:T(8,128)(2,1)}), bf16[16,48,4096]{2,1,0:T(8,128)(2,1)}, u32[]{:S(2)}, u32[]{:S(2)}) async-start(bf16[16,48,4096]{2,1,0:T(8,128)(2,1)} %broadcast_select_fusion), calls=%async_computation | async-start | bytes 12582912 | tf_op jit(solution)/shard_map/all_to_all | solution.py:41
  169.1 142.5 %all-to-all-start.2 = ((bf16[16,48,4096]{2,1,0:T(8,128)(2,1)}), bf16[16,48,4096]{2,1,0:T(8,128)(2,1)}, u32[]{:S(2)}, u32[]{:S(2)}) async-start(bf16[16,48,4096]{2,1,0:T(8,128)(2,1)} %fusion), calls=%async_computation.2 | async-start | bytes 12582912 | tf_op jit(solution)/shard_map/all_to_all | solution.py:42
  192.3 1.4 copy-start.3
  311.7 142.7 %all-to-all-start.1 = ((bf16[16,48,4096]{2,1,0:T(8,128)(2,1)}), bf16[16,48,4096]{2,1,0:T(8,128)(2,1)}, u32[]{:S(2)}, u32[]{:S(2)}) async-start(bf16[16,48,4096]{2,1,0:T(8,128)(2,1)} %bitcast.52), calls=%async_computation.1 | async-start | bytes 12582912 | tf_op jit(solution)/shard_map/all_to_all | solution.py:64
  317.1 9.2 %copy-start.4 = (f32[768,768]{1,0:T(8,128)S(1)}, f32[768,768]{1,0:T(8,128)}, u32[]{:S(2)}) copy-start(f32[768,768]{1,0:T(8,128)} %copy-done.3) | copy-start | bytes 7077892
  317.1 20.8 %slice-start = ((s8[6291456]{0:T(1024)(128)(4,1)}), s8[4194304]{0:T(1024)(128)(4,1)S(1)}, s32[]{:S(2)}) async-start(s8[6291456]{0:T(1024)(128)(4,1)} %bitcast.56), calls=%async_computation.4 | async-start | bytes 8388608
  326.3 11.5 %slice-start.1 = ((s8[6291456]{0:T(1024)(128)(4,1)}), s8[2097152]{0:T(1024)(128)(4,1)S(1)}, s32[]{:S(2)}) async-start(s8[6291456]{0:T(1024)(128)(4,1)} %bitcast.56), calls=%async_computation.5 | async-start | bytes 4194304
  454.4 142.3 %all-to-all-start.3 = ((bf16[16,48,4096]{2,1,0:T(8,128)(2,1)}), bf16[16,48,4096]{2,1,0:T(8,128)(2,1)}, u32[]{:S(2)}, u32[]{:S(2)}) async-start(bf16[16,48,4096]{2,1,0:T(8,128)(2,1)} %bitcast.51), calls=%async_computation.3 | async-start | bytes 12582912 | tf_op jit(solution)/shard_map/all_to_all | solution.py:65
  596.7 28.1 %copy-start.1 = (bf16[128,4096]{1,0:T(8,128)(2,1)S(1)}, bf16[128,4096]{1,0:T(8,128)(2,1)}, u32[]{:S(2)}) copy-start(bf16[128,4096]{1,0:T(8,128)(2,1)} %param.7) | copy-start | bytes 3145732
where the time goes:
time: 632 us; the launch traced here: 625 us
  waiting for transfers between devices  445 us (70%)
  local copies, waits for them, and re-layouts  62.4 us (10%)
  matrix products  58.4 us (9%)
  other arithmetic  36.4 us (6%)
  starting transfers between devices  22.3 us (4%)
    all_to_all x1, waiting for transfers between devices, per_device(): lax.all_to_all(send_tokens, 'wide', split_axis=0, concat_axis=0, tiled=True)  124 us
    all_to_all x1, waiting for transfers between devices, per_device(): lax.all_to_all(send_cot, 'wide', split_axis=0, concat_axis=0, tiled=True)  108 us
    all_to_all x1, waiting for transfers between devices, per_device(): lax.all_to_all(outputs, 'wide', split_axis=0, concat_axis=0, tiled=True)  107 us
    all_to_all x1, waiting for transfers between devices, per_device(): lax.all_to_all(input_grad, 'wide', split_axis=0, concat_axis=0, tiled=True)  106 us
  transfers between devices with their start and end apart: 4, of which 4 were waited for; matrix products, arithmetic and copies ran while one was open for 17% of the time, Pallas kernels for 0%

commit v1 on v0

v1 whole, which is shorter than its diff:
```python
import jax
import jax.numpy as jnp
from jax import lax
from jax.sharding import PartitionSpec as P

contract_last = (((1,), (1,)), ((), ()))
contract_first = (((0,), (0,)), ((), ()))
STREAMS = 2


def layout(wide):
    if wide == 16:
        return 4, 2, (0, 1, 3, 2)
    return wide // 2, 1, tuple(range(wide // 2))


def per_device(tokens, cotangent, expert_ids, gate_codes, w_gate, w_up, w_down):
    wide = lax.axis_size("wide")
    rows, width = tokens.shape
    top = expert_ids.shape[1]
    cap = 3 * rows * top // (2 * wide)
    zs, ys, ring = layout(wide)
    me = lax.axis_index("wide")
    core, col, my_z = me % 2, (me // 2) % ys, me // (2 * ys)

    def pairs(move):
        out = []
        for z in range(zs):
            for y in range(ys):
                for c in range(2):
                    tz, ty, tc = move(z, y, c)
                    out.append(((z * ys + y) * 2 + c, (tz * ys + ty) * 2 + tc))
        return out

    place = {z: i for i, z in enumerate(ring)}
    ahead = pairs(lambda z, y, c: (ring[(place[z] + 1) % zs], y, c))
    back = pairs(lambda z, y, c: (ring[(place[z] - 1) % zs], y, c))
    across = pairs(lambda z, y, c: (z, (y + 1) % ys, c))
    twin = pairs(lambda z, y, c: (z, y, 1 - c))

    def permute(value, perm):
        return lax.ppermute(value, "wide", perm)

    codes = lax.all_gather(jnp.concatenate([expert_ids, gate_codes], axis=1), "wide")
    codes = codes.reshape(zs, ys, 2, rows, 2 * top)
    codes = lax.dynamic_index_in_dim(codes, core, 2, keepdims=False)
    order = jnp.array([[ring[(place[z] - r) % zs] for r in range(zs)] for z in range(zs)], jnp.int32)
    codes = codes[order[my_z]]
    mine = lax.dynamic_index_in_dim(codes, col, 1, keepdims=False)
    sides = [mine]
    if ys == 2:
        sides.append(lax.dynamic_index_in_dim(codes, 1 - col, 1, keepdims=False))
    chip = my_z * ys + col
    here = jnp.stack([2 * chip + core, 2 * chip + 1 - core])
    chips = [here]
    if ys == 2:
        there = my_z * ys + 1 - col
        chips.append(jnp.stack([2 * there + core, 2 * there + 1 - core]))

    def table(side, experts):
        ids, gates = side[..., :top], side[..., top:].astype(jnp.float32)
        share = gates / jnp.sum(gates, axis=-1, keepdims=True)
        same = ids[:, None] == experts[None, :, None, None]
        hit = jnp.any(same, axis=-1)
        gate = jnp.sum(jnp.where(same, share[:, None], 0.0), axis=-1)
        spot = jnp.cumsum(hit.astype(jnp.int32), axis=-1) - 1
        pick = hit[:, :, None] & (spot[:, :, None] == jnp.arange(cap)[None, None, :, None])
        slot_gate = jnp.sum(jnp.where(pick, gate[:, :, None], 0.0), axis=-1)
        return pick.astype(jnp.bfloat16), slot_gate

    pick_here, gate_here = table(mine, here)
    picks, gates = [pick_here], [gate_here]
    if ys == 2:
        pick_there, gate_there = table(mine, chips[1])
        picks.append(pick_there)
        gates.append(gate_there)
    pick = jnp.concatenate(picks, axis=1).reshape(zs, -1, rows)
    pick_gate = jnp.concatenate(gates, axis=1).reshape(zs, -1)
    slots = 2 * cap
    expert_gate = [gate_here]
    if ys == 2:
        expert_gate.append(table(sides[1], here)[1])
    expert_gate = jnp.concatenate(expert_gate, axis=0)

    def cut(value):
        step = width // STREAMS
        return [value[:, i * step : (i + 1) * step] for i in range(STREAMS)]

    def dispatch(value, weighted):
        parts = cut(value)
        own, other = [], []
        for r in range(zs):
            chosen = [
                lax.dot_general(pick[r], part, (((1,), (0,)), ((), ())), preferred_element_type=jnp.float32)
                for part in parts
            ]
            if weighted:
                chosen = [pick_gate[r][:, None] * part for part in chosen]
            chosen = jnp.concatenate([part.astype(jnp.bfloat16) for part in chosen], axis=1)
            own.append(chosen[:slots])
            if ys == 2:
                other.append(permute(chosen[slots:], across))
            if r < zs - 1:
                parts = [permute(part, ahead) for part in parts]
        sources = own + other
        return [jnp.concatenate([s[e * cap : (e + 1) * cap] for s in sources], axis=0) for e in range(2)]

    def combine(results):
        total = None
        for r in reversed(range(zs)):
            blocks = [res[r * cap : (r + 1) * cap] for res in results]
            if ys == 2:
                away = [res[(zs + r) * cap : (zs + r + 1) * cap] for res in results]
                blocks.append(permute(jnp.concatenate(away, axis=0), across))
            block = jnp.concatenate(blocks, axis=0)
            sums = [
                lax.dot_general(pick[r], part, contract_first, preferred_element_type=jnp.float32)
                for part in cut(block)
            ]
            if total is not None:
                sums = [s + t.astype(jnp.float32) for s, t in zip(sums, total)]
            total = [s.astype(jnp.bfloat16) for s in sums]
            if r > 0:
                total = [permute(t, back) for t in total]
        return jnp.concatenate(total, axis=1)

    def both(weight):
        return weight[0], permute(weight[0], twin)

    gate_mats, up_mats, down_mats = both(w_gate), both(w_up), both(w_down)
    token_rows = dispatch(tokens, False)
    cot_rows = dispatch(cotangent, True)
    outs, saved = [], []
    for e in range(2):
        pre_gate = jnp.dot(token_rows[e], gate_mats[e], preferred_element_type=jnp.float32)
        pre_up = jnp.dot(token_rows[e], up_mats[e], preferred_element_type=jnp.float32)
        logistic = jax.nn.sigmoid(pre_gate)
        activated = pre_gate * logistic
        hidden = (activated * pre_up).astype(jnp.bfloat16)
        out = jnp.dot(hidden, down_mats[e], preferred_element_type=jnp.float32)
        outs.append((expert_gate[:, e].reshape(-1)[:, None] * out).astype(jnp.bfloat16))
        saved.append((pre_gate, pre_up, logistic, activated))
    moe_out = combine(outs)
    grads = []
    for e in range(2):
        pre_gate, pre_up, logistic, activated = saved[e]
        hidden_grad = lax.dot_general(cot_rows[e], down_mats[e], contract_last, preferred_element_type=jnp.float32)
        gate_grad = (hidden_grad * pre_up * logistic * (1.0 + pre_gate * (1.0 - logistic))).astype(jnp.bfloat16)
        up_grad = (hidden_grad * activated).astype(jnp.bfloat16)
        grad = lax.dot_general(
            gate_grad, gate_mats[e], contract_last, preferred_element_type=jnp.float32
        ) + lax.dot_general(up_grad, up_mats[e], contract_last, preferred_element_type=jnp.float32)
        grads.append(grad.astype(jnp.bfloat16))
    token_grad = combine(grads)
    return (moe_out, token_grad)


def solution(mesh):
    return jax.shard_map(
        per_device,
        mesh=mesh,
        in_specs=(
            P(("group", "wide"), None),
            P(("group", "wide"), None),
            P(("group", "wide"), None),
            P(("group", "wide"), None),
            P("wide", None, None),
            P("wide", None, None),
            P("wide", None, None),
        ),
        out_specs=(P(("group", "wide"), None), P(("group", "wide"), None)),
        check_vma=False,
    )
```

time: 632 us -> 639 us (1.011)
  the two profiles are of different devices: /device:TPU:13 before, /device:TPU:0 now
where the time goes in v1:
time: 639 us; the launch traced here: 632 us
  waiting for transfers between devices  461 us (72%)
  matrix products  89 us (14%)
  starting transfers between devices  31.5 us (5%)
  blocking collectives  23.2 us (4%)
  other arithmetic  15.5 us (2%)
  local copies, waits for them, and re-layouts  9.29 us (1%)
    ppermute x43, waiting for transfers between devices, permute(): return lax.ppermute(value, 'wide', perm)  461 us
    ppermute x43, starting transfers between devices, permute(): return lax.ppermute(value, 'wide', perm)  31.5 us
    all_gather x1, blocking collectives, per_device(): lax.all_gather(jnp.concatenate([expert_ids, gate_codes], axis=1), 'wide')  23.2 us
    dot_general x2, matrix products, per_device(): lax.dot_general(up_grad, up_mats[e], contract_last, preferred_element_typ...  16.2 us
    dot_general x2, matrix products, per_device(): lax.dot_general(gate_grad, gate_mats[e], contract_last, preferred_element...  13.8 us
  transfers between devices with their start and end apart: 43, of which 28 were waited for; matrix products, arithmetic and copies ran while one was open for 12% of the time, Pallas kernels for 0%

profile of v1, /device:TPU:0, one launch (start us, length us, event | category | flops | bytes accessed | tf_op | source)
XLA Modules:
  0.0 632.0 jit_solution(15979039204108376597)
XLA Ops:
  2.2 23.2 %all-gather = s32[2048,8]{0,1:T(8,128)S(1)} all-gather(s32[128,8]{0,1:T(8,128)S(1)} %pad_add_fusion.1), channel_id=2, replica_groups=mesh['group'=2,'wide'=16] {'wide'}, dimensions={0}, use_global_device_ids=true | all-gather | bytes 69632 | tf_op jit(solution)/shard_map/all_gather | solution.py:44
  26.3 1.2 reduce_window_sum.24
  27.8 1.2 reduce_window_sum.20
  31.9 2.1 collective-permute-start.6
  34.0 1.0 fusion.111
  35.0 1.0 fusion.110
  37.9 1.2 reduce_window_sum.25
  39.7 22.6 %collective-permute-done.1 = bf16[128,2048]{1,0:T(8,128)(2,1)} collective-permute-done((bf16[128,2048]{1,0:T(8,128)(2,1)}, bf16[128,2048]{1,0:T(8,128)(2,1)}, u32[]{:S(2)}, u32[]{:S(2)}) %collective-permute-start.1) | collective-permute-done | bytes 524320 | tf_op jit(solution)/shard_map/ppermute | solution.py:42
  62.3 1.4 convolution_convert_fusion.4
  63.7 9.7 %collective-permute-done.24 = bf16[128,2048]{1,0:T(8,128)(2,1)S(1)} collective-permute-done((bf16[128,2048]{1,0:T(8,128)(2,1)}, bf16[128,2048]{1,0:T(8,128)(2,1)S(1)}, u32[]{:S(2)}, u32[]{:S(2)}) %collective-permute-start.24) | collective-permute-done | bytes 524320 | tf_op jit(solution)/shard_map/ppermute | solution.py:42
  73.8 1.5 convolution_convert_fusion.5
  75.4 8.0 %collective-permute-done.23 = bf16[128,2048]{1,0:T(8,128)(2,1)S(1)} collective-permute-done((bf16[128,2048]{1,0:T(8,128)(2,1)S(1)}, bf16[128,2048]{1,0:T(8,128)(2,1)S(1)}, u32[]{:S(2)}, u32[]{:S(2)}) %collective-permute-start.23) | collective-permute-done | bytes 524320 | tf_op jit(solution)/shard_map/ppermute | solution.py:42
  84.7 1.5 collective-permute-start.26
  86.4 13.5 %collective-permute-done.3 = bf16[128,2048]{1,0:T(8,128)(2,1)S(1)} collective-permute-done((bf16[128,2048]{1,0:T(8,128)(2,1)}, bf16[128,2048]{1,0:T(8,128)(2,1)S(1)}, u32[]{:S(2)}, u32[]{:S(2)}) %collective-permute-start.3) | collective-permute-done | bytes 524320 | tf_op jit(solution)/shard_map/ppermute | solution.py:42
  100.2 22.1 %collective-permute-done.26 = bf16[128,2048]{1,0:T(8,128)(2,1)S(1)} collective-permute-done((bf16[128,2048]{1,0:T(8,128)(2,1)S(1)}, bf16[128,2048]{1,0:T(8,128)(2,1)S(1)}, u32[]{:S(2)}, u32[]{:S(2)}) %collective-permute-start.26) | collective-permute-done | bytes 524320 | tf_op jit(solution)/shard_map/ppermute | solution.py:42
  123.1 8.3 %collective-permute-done.25 = bf16[128,2048]{1,0:T(8,128)(2,1)S(1)} collective-permute-done((bf16[128,2048]{1,0:T(8,128)(2,1)S(1)}, bf16[128,2048]{1,0:T(8,128)(2,1)S(1)}, u32[]{:S(2)}, u32[]{:S(2)}) %collective-permute-start.25) | collective-permute-done | bytes 524320 | tf_op jit(solution)/shard_map/ppermute | solution.py:42
  132.8 1.6 collective-permute-start.27
  134.4 13.3 %collective-permute-done.4 = bf16[128,2048]{1,0:T(8,128)(2,1)S(1)} collective-permute-done((bf16[128,2048]{1,0:T(8,128)(2,1)S(1)}, bf16[128,2048]{1,0:T(8,128)(2,1)S(1)}, u32[]{:S(2)}, u32[]{:S(2)}) %collective-permute-start.4) | collective-permute-done | bytes 524320 | tf_op jit(solution)/shard_map/ppermute | solution.py:42
  148.1 19.1 %collective-permute-done.27 = bf16[128,2048]{1,0:T(8,128)(2,1)S(1)} collective-permute-done((bf16[128,2048]{1,0:T(8,128)(2,1)S(1)}, bf16[128,2048]{1,0:T(8,128)(2,1)S(1)}, u32[]{:S(2)}, u32[]{:S(2)}) %collective-permute-start.27) | collective-permute-done | bytes 524320 | tf_op jit(solution)/shard_map/ppermute | solution.py:42
  168.2 14.8 %collective-permute-done.28 = bf16[128,2048]{1,0:T(8,128)(2,1)S(1)} collective-permute-done((bf16[128,2048]{1,0:T(8,128)(2,1)S(1)}, bf16[128,2048]{1,0:T(8,128)(2,1)S(1)}, u32[]{:S(2)}, u32[]{:S(2)}) %collective-permute-start.28) | collective-permute-done | bytes 524320 | tf_op jit(solution)/shard_map/ppermute | solution.py:42
  184.3 1.0 collective-permute-start.30
  186.1 18.2 %collective-permute-done.30 = bf16[96,4096]{1,0:T(8,128)(2,1)S(1)} collective-permute-done((bf16[96,4096]{1,0:T(8,128)(2,1)S(1)}, bf16[96,4096]{1,0:T(8,128)(2,1)S(1)}, u32[]{:S(2)}, u32[]{:S(2)}) %collective-permute-start.30) | collective-permute-done | bytes 786464 | tf_op jit(solution)/shard_map/ppermute | solution.py:42
  206.0 1.1 collective-permute-start.8
  207.2 17.6 %collective-permute-done.7 = bf16[96,4096]{1,0:T(8,128)(2,1)S(1)} collective-permute-done((bf16[96,4096]{1,0:T(8,128)(2,1)S(1)}, bf16[96,4096]{1,0:T(8,128)(2,1)S(1)}, u32[]{:S(2)}, u32[]{:S(2)}) %collective-permute-start.7) | collective-permute-done | bytes 786464 | tf_op jit(solution)/shard_map/ppermute | solution.py:42
  225.7 31.4 %collective-permute-done.31 = bf16[96,4096]{1,0:T(8,128)(2,1)S(1)} collective-permute-done((bf16[96,4096]{1,0:T(8,128)(2,1)S(1)}, bf16[96,4096]{1,0:T(8,128)(2,1)S(1)}, u32[]{:S(2)}, u32[]{:S(2)}) %collective-permute-start.31) | collective-permute-done | bytes 786464 | tf_op jit(solution)/shard_map/ppermute | solution.py:42
  258.9 1.1 collective-permute-start.32
  260.0 32.3 %collective-permute-done.32 = bf16[96,4096]{1,0:T(8,128)(2,1)S(1)} collective-permute-done((bf16[96,4096]{1,0:T(8,128)(2,1)S(1)}, bf16[96,4096]{1,0:T(8,128)(2,1)S(1)}, u32[]{:S(2)}, u32[]{:S(2)}) %collective-permute-start.32) | collective-permute-done | bytes 786464 | tf_op jit(solution)/shard_map/ppermute | solution.py:42
  293.2 6.5 %fusion.90 = f32[384,768]{1,0:T(8,128)S(1)} fusion(bf16[384,4096]{1,0:T(8,128)(2,1)S(1)} %get-tuple-element.70, bf16[1,4096,768]{2,1,0:T(8,128)(2,1)} %param.12), kind=kOutput, calls=%fused_computation.240 | convolution fusion | flops 2415919104 | bytes 10616832 | tf_op jit(solution)/shard_map/dot_general | solution.py:135
  299.7 5.4 fusion.87
  305.2 5.4 fusion.83
  310.6 5.9 multiply_convert_fusion.1
  316.6 5.4 fusion.46
  321.9 7.2 %add_convert_fusion.1 = bf16[384,4096]{1,0:T(8,128)(2,1)S(1)} fusion(f32[384,4096]{1,0:T(8,128)S(1)} %fusion.46, f32[384,768]{1,0:T(8,128)S(1)} %fusion.83, f32[384,768]{1,0:T(8,128)S(1)} %fusion.90, bf16[1,4096,768]{2,1,0:T(8,128)(2,1)} %param.13), kind=kOutput, calls=%fused_computation.2 | convolution fusion | flops 2420834304 | bytes 18087936 | tf_op jit(solution)/shard_map/dot_general | solution.py:152
  329.8 1.5 copy-done.6
  331.4 5.4 fusion.113
  336.8 5.6 fusion.112
  342.4 5.4 fusion.114
  347.8 9.0 %fusion.47 = f32[384,4096]{1,0:T(8,128)} fusion(bf16[4096,768]{1,0:T(8,128)(2,1)} %collective-permute-done.11, f32[384,768]{1,0:T(8,128)S(1)} %fusion.114, f32[384,768]{1,0:T(8,128)S(1)} %fusion.112), kind=kOutput, calls=%fused_computation.126 | convolution fusion | flops 2417688576 | bytes 14942208 | tf_op jit(solution)/shard_map/dot_general | solution.py:152
  356.8 8.5 %add_convert_fusion = bf16[384,4096]{1,0:T(8,128)(2,1)S(1)} fusion(f32[384,4096]{1,0:T(8,128)} %fusion.47, bf16[4096,768]{1,0:T(8,128)(2,1)} %collective-permute-done.10, f32[384,768]{1,0:T(8,128)S(1)} %fusion.112, f32[384,768]{1,0:T(8,128)S(1)} %fusion.114, f32[384,768]{1,0:T(8,128)S(1)} %fusion.113), kind=kOutput, calls=%fused_computation.1 | convolution fusion | flops 2422013952 | bytes 19267584 | tf_op jit(solution)/shard_map/dot_general | solution.py:150
  365.5 5.7 multiply_convert_fusion
  371.6 1.0 collective-permute-start.33
  372.7 1.2 collective-permute-start.34
  373.9 1.0 collective-permute-start.35
  374.9 1.2 collective-permute-start.36
  376.2 1.0 collective-permute-start.13
  377.3 14.8 %collective-permute-done.33 = bf16[96,4096]{1,0:T(8,128)(2,1)S(1)} collective-permute-done((bf16[96,4096]{1,0:T(8,128)(2,1)S(1)}, bf16[96,4096]{1,0:T(8,128)(2,1)S(1)}, u32[]{:S(2)}, u32[]{:S(2)}) %collective-permute-start.33) | collective-permute-done | bytes 786464 | tf_op jit(solution)/shard_map/ppermute | solution.py:42
  393.2 15.8 %collective-permute-done.34 = bf16[96,4096]{1,0:T(8,128)(2,1)S(1)} collective-permute-done((bf16[96,4096]{1,0:T(8,128)(2,1)S(1)}, bf16[96,4096]{1,0:T(8,128)(2,1)S(1)}, u32[]{:S(2)}, u32[]{:S(2)}) %collective-permute-start.34) | collective-permute-done | bytes 786464 | tf_op jit(solution)/shard_map/ppermute | solution.py:42
  410.1 32.6 %collective-permute-done.36 = bf16[96,4096]{1,0:T(8,128)(2,1)S(1)} collective-permute-done((bf16[96,4096]{1,0:T(8,128)(2,1)S(1)}, bf16[96,4096]{1,0:T(8,128)(2,1)S(1)}, u32[]{:S(2)}, u32[]{:S(2)}) %collective-permute-start.36) | collective-permute-done | bytes 786464 | tf_op jit(solution)/shard_map/ppermute | solution.py:42
  444.8 62.2 %collective-permute-done.16 = bf16[96,4096]{1,0:T(8,128)(2,1)S(1)} collective-permute-done((bf16[96,4096]{1,0:T(8,128)(2,1)S(1)}, bf16[96,4096]{1,0:T(8,128)(2,1)S(1)}, u32[]{:S(2)}, u32[]{:S(2)}) %collective-permute-start.16) | collective-permute-done | bytes 786464 | tf_op jit(solution)/shard_map/ppermute | solution.py:42
  508.7 1.8 collective-permute-start.20
  511.2 2.7 collective-permute-start.38
  513.9 8.0 %collective-permute-done.40 = bf16[128,2048]{1,0:T(8,128)(2,1)S(1)} collective-permute-done((bf16[128,2048]{1,0:T(8,128)(2,1)S(1)}, bf16[128,2048]{1,0:T(8,128)(2,1)S(1)}, u32[]{:S(2)}, u32[]{:S(2)}) %collective-permute-start.40) | collective-permute-done | bytes 524320 | tf_op jit(solution)/shard_map/ppermute | solution.py:42
  523.2 9.9 %collective-permute-done.17 = bf16[128,2048]{1,0:T(8,128)(2,1)S(1)} collective-permute-done((bf16[128,2048]{1,0:T(8,128)(2,1)S(1)}, bf16[128,2048]{1,0:T(8,128)(2,1)S(1)}, u32[]{:S(2)}, u32[]{:S(2)}) %collective-permute-start.17) | collective-permute-done | bytes 524320 | tf_op jit(solution)/shard_map/ppermute | solution.py:42
  534.4 9.9 %collective-permute-done.20 = bf16[128,2048]{1,0:T(8,128)(2,1)S(1)} collective-permute-done((bf16[128,2048]{1,0:T(8,128)(2,1)S(1)}, bf16[128,2048]{1,0:T(8,128)(2,1)S(1)}, u32[]{:S(2)}, u32[]{:S(2)}) %collective-permute-start.20) | collective-permute-done | bytes 524320 | tf_op jit(solution)/shard_map/ppermute | solution.py:42
  545.6 9.9 %collective-permute-done.38 = bf16[128,2048]{1,0:T(8,128)(2,1)S(1)} collective-permute-done((bf16[128,2048]{1,0:T(8,128)(2,1)S(1)}, bf16[128,2048]{1,0:T(8,128)(2,1)S(1)}, u32[]{:S(2)}, u32[]{:S(2)}) %collective-permute-start.38) | collective-permute-done | bytes 524320 | tf_op jit(solution)/shard_map/ppermute | solution.py:42
  556.9 9.9 %collective-permute-done.41 = bf16[128,2048]{1,0:T(8,128)(2,1)S(1)} collective-permute-done((bf16[128,2048]{1,0:T(8,128)(2,1)S(1)}, bf16[128,2048]{1,0:T(8,128)(2,1)S(1)}, u32[]{:S(2)}, u32[]{:S(2)}) %collective-permute-start.41) | collective-permute-done | bytes 524320 | tf_op jit(solution)/shard_map/ppermute | solution.py:42
  568.1 9.9 %collective-permute-done.18 = bf16[128,2048]{1,0:T(8,128)(2,1)S(1)} collective-permute-done((bf16[128,2048]{1,0:T(8,128)(2,1)S(1)}, bf16[128,2048]{1,0:T(8,128)(2,1)S(1)}, u32[]{:S(2)}, u32[]{:S(2)}) %collective-permute-start.18) | collective-permute-done | bytes 524320 | tf_op jit(solution)/shard_map/ppermute | solution.py:42
  579.3 9.9 %collective-permute-done.21 = bf16[128,2048]{1,0:T(8,128)(2,1)S(1)} collective-permute-done((bf16[128,2048]{1,0:T(8,128)(2,1)S(1)}, bf16[128,2048]{1,0:T(8,128)(2,1)S(1)}, u32[]{:S(2)}, u32[]{:S(2)}) %collective-permute-start.21) | collective-permute-done | bytes 524320 | tf_op jit(solution)/shard_map/ppermute | solution.py:42
  590.6 9.9 %collective-permute-done.39 = bf16[128,2048]{1,0:T(8,128)(2,1)S(1)} collective-permute-done((bf16[128,2048]{1,0:T(8,128)(2,1)S(1)}, bf16[128,2048]{1,0:T(8,128)(2,1)S(1)}, u32[]{:S(2)}, u32[]{:S(2)}) %collective-permute-start.39) | collective-permute-done | bytes 524320 | tf_op jit(solution)/shard_map/ppermute | solution.py:42
  600.9 10.9 %collective-permute-done.42 = bf16[128,2048]{1,0:T(8,128)(2,1)S(1)} collective-permute-done((bf16[128,2048]{1,0:T(8,128)(2,1)S(1)}, bf16[128,2048]{1,0:T(8,128)(2,1)S(1)}, u32[]{:S(2)}, u32[]{:S(2)}) %collective-permute-start.42) | collective-permute-done | bytes 524320 | tf_op jit(solution)/shard_map/ppermute | solution.py:42
  612.1 10.9 %collective-permute-done.19 = bf16[128,2048]{1,0:T(8,128)(2,1)S(1)} collective-permute-done((bf16[128,2048]{1,0:T(8,128)(2,1)S(1)}, bf16[128,2048]{1,0:T(8,128)(2,1)S(1)}, u32[]{:S(2)}, u32[]{:S(2)}) %collective-permute-start.19) | collective-permute-done | bytes 524320 | tf_op jit(solution)/shard_map/ppermute | solution.py:42
  623.3 1.1 pad_maximum_fusion.9
  624.4 5.8 collective-permute-done.22
  630.5 1.1 pad_maximum_fusion.8
  (169 shorter events, 39.4 us)
Async XLA Ops:
  0.6 28.7 %copy-start = (bf16[128,4096]{1,0:T(8,128)(2,1)S(1)}, bf16[128,4096]{1,0:T(8,128)(2,1)}, u32[]{:S(2)}) copy-start(bf16[128,4096]{1,0:T(8,128)(2,1)} %param.9) | copy-start | bytes 3145732
  29.8 1.3 copy-start.1
  31.1 153.2 %collective-permute-start.29 = (bf16[96,4096]{1,0:T(8,128)(2,1)}, bf16[96,4096]{1,0:T(8,128)(2,1)S(1)}, u32[]{:S(2)}, u32[]{:S(2)}) collective-permute-start(bf16[96,4096]{1,0:T(8,128)(2,1)} %fusion.25), channel_id=1, source_target_pairs={{0,2},{1,3},{2,0},{3,1},{4,6},{5,7},{6,4},{7,5},{8,10},{9,11},{10,... | collective-permute-start | bytes 2359304 | tf_op jit(solution)/shard_map/ppermute | solution.py:42
  31.9 174.2 %collective-permute-start.6 = (bf16[96,4096]{1,0:T(8,128)(2,1)S(1)}, bf16[96,4096]{1,0:T(8,128)(2,1)S(1)}, u32[]{:S(2)}, u32[]{:S(2)}) collective-permute-start(bf16[96,4096]{1,0:T(8,128)(2,1)S(1)} %fusion.29), channel_id=1, source_target_pairs={{0,2},{1,3},{2,0},{3,1},{4,6},{5,7},{6,4},{7,5},{8,10},{9,11},{10,... | collective-permute-start | bytes 2359304 | tf_op jit(solution)/shard_map/ppermute | solution.py:42
  35.0 38.8 %collective-permute-start = (bf16[128,2048]{1,0:T(8,128)(2,1)}, bf16[128,2048]{1,0:T(8,128)(2,1)}, u32[]{:S(2)}, u32[]{:S(2)}) collective-permute-start(bf16[128,2048]{1,0:T(8,128)(2,1)} %get-tuple-element.60), channel_id=1, source_target_pairs={{0,4},{1,5},{2,6},{3,7},{4,12},{5,13},{6,14},{7,15},{8,0},{9,1},{1... | collective-permute-start | bytes 1572872 | tf_op jit(solution)/shard_map/ppermute | solution.py:42
  35.0 27.3 %collective-permute-start.1 = (bf16[128,2048]{1,0:T(8,128)(2,1)}, bf16[128,2048]{1,0:T(8,128)(2,1)}, u32[]{:S(2)}, u32[]{:S(2)}) collective-permute-start(bf16[128,2048]{1,0:T(8,128)(2,1)} %get-tuple-element.61), channel_id=1, source_target_pairs={{0,4},{1,5},{2,6},{3,7},{4,12},{5,13},{6,14},{7,15},{8,0},{9,1},{1... | collective-permute-start | bytes 1572872 | tf_op jit(solution)/shard_map/ppermute | solution.py:42
  36.0 37.3 %collective-permute-start.24 = (bf16[128,2048]{1,0:T(8,128)(2,1)}, bf16[128,2048]{1,0:T(8,128)(2,1)S(1)}, u32[]{:S(2)}, u32[]{:S(2)}) collective-permute-start(bf16[128,2048]{1,0:T(8,128)(2,1)} %get-tuple-element.59), channel_id=1, source_target_pairs={{0,4},{1,5},{2,6},{3,7},{4,12},{5,13},{6,14},{7,15},{8,0},{9,1},{1... | collective-permute-start | bytes 1572872 | tf_op jit(solution)/shard_map/ppermute | solution.py:42
  37.0 25.3 %copy-start.2 = (bf16[128,2048]{1,0:T(8,128)(2,1)S(1)}, bf16[128,2048]{1,0:T(8,128)(2,1)}, u32[]{:S(2)}) copy-start(bf16[128,2048]{1,0:T(8,128)(2,1)} %get-tuple-element.58) | copy-start | bytes 1572868
  62.3 21.2 %collective-permute-start.23 = (bf16[128,2048]{1,0:T(8,128)(2,1)S(1)}, bf16[128,2048]{1,0:T(8,128)(2,1)S(1)}, u32[]{:S(2)}, u32[]{:S(2)}) collective-permute-start(bf16[128,2048]{1,0:T(8,128)(2,1)S(1)} %copy-done.2), channel_id=1, source_target_pairs={{0,4},{1,5},{2,6},{3,7},{4,12},{5,13},{6,14},{7,15},{8,0},{9,1},{1... | collective-permute-start | bytes 1572872 | tf_op jit(solution)/shard_map/ppermute | solution.py:42
  73.8 10.2 %copy-start.7 = (bf16[384,4096]{1,0:T(8,128)(2,1)S(1)}, bf16[384,4096]{1,0:T(8,128)(2,1)}, u32[]{:S(2)}) copy-start(bf16[384,4096]{1,0:T(8,128)(2,1)} %get-tuple-element.48) | copy-start | bytes 9437188
  75.3 11.0 %copy-start.4 = (bf16[384,4096]{1,0:T(8,128)(2,1)S(1)}, bf16[384,4096]{1,0:T(8,128)(2,1)}, u32[]{:S(2)}) copy-start(bf16[384,4096]{1,0:T(8,128)(2,1)} %get-tuple-element.57) | copy-start | bytes 9437188
  83.8 2.5 copy-start.3
  83.9 16.0 %collective-permute-start.3 = (bf16[128,2048]{1,0:T(8,128)(2,1)}, bf16[128,2048]{1,0:T(8,128)(2,1)S(1)}, u32[]{:S(2)}, u32[]{:S(2)}) collective-permute-start(bf16[128,2048]{1,0:T(8,128)(2,1)} %collective-permute-done.1), channel_id=1, source_target_pairs={{0,4},{1,5},{2,6},{3,7},{4,12},{5,13},{6,14},{7,15},{8,0},{9,1},{1... | collective-permute-start | bytes 1572872 | tf_op jit(solution)/shard_map/ppermute | solution.py:42
  84.7 38.0 %collective-permute-start.2 = (bf16[128,2048]{1,0:T(8,128)(2,1)}, bf16[128,2048]{1,0:T(8,128)(2,1)S(1)}, u32[]{:S(2)}, u32[]{:S(2)}) collective-permute-start(bf16[128,2048]{1,0:T(8,128)(2,1)} %collective-permute-done), channel_id=1, source_target_pairs={{0,4},{1,5},{2,6},{3,7},{4,12},{5,13},{6,14},{7,15},{8,0},{9,1},{1... | collective-permute-start | bytes 1572872 | tf_op jit(solution)/shard_map/ppermute | solution.py:42
  84.7 37.6 %collective-permute-start.26 = (bf16[128,2048]{1,0:T(8,128)(2,1)S(1)}, bf16[128,2048]{1,0:T(8,128)(2,1)S(1)}, u32[]{:S(2)}, u32[]{:S(2)}) collective-permute-start(bf16[128,2048]{1,0:T(8,128)(2,1)S(1)} %collective-permute-done.24), channel_id=1, source_target_pairs={{0,4},{1,5},{2,6},{3,7},{4,12},{5,13},{6,14},{7,15},{8,0},{9,1},{1... | collective-permute-start | bytes 1572872 | tf_op jit(solution)/shard_map/ppermute | solution.py:42
  99.9 31.6 %collective-permute-start.25 = (bf16[128,2048]{1,0:T(8,128)(2,1)S(1)}, bf16[128,2048]{1,0:T(8,128)(2,1)S(1)}, u32[]{:S(2)}, u32[]{:S(2)}) collective-permute-start(bf16[128,2048]{1,0:T(8,128)(2,1)S(1)} %collective-permute-done.23), channel_id=1, source_target_pairs={{0,4},{1,5},{2,6},{3,7},{4,12},{5,13},{6,14},{7,15},{8,0},{9,1},{1... | collective-permute-start | bytes 1572872 | tf_op jit(solution)/shard_map/ppermute | solution.py:42
  131.9 15.8 %collective-permute-start.4 = (bf16[128,2048]{1,0:T(8,128)(2,1)S(1)}, bf16[128,2048]{1,0:T(8,128)(2,1)S(1)}, u32[]{:S(2)}, u32[]{:S(2)}) collective-permute-start(bf16[128,2048]{1,0:T(8,128)(2,1)S(1)} %collective-permute-done.2), channel_id=1, source_target_pairs={{0,4},{1,5},{2,6},{3,7},{4,12},{5,13},{6,14},{7,15},{8,0},{9,1},{1... | collective-permute-start | bytes 1572872 | tf_op jit(solution)/shard_map/ppermute | solution.py:42
  132.8 34.7 %collective-permute-start.5 = (bf16[128,2048]{1,0:T(8,128)(2,1)S(1)}, bf16[128,2048]{1,0:T(8,128)(2,1)S(1)}, u32[]{:S(2)}, u32[]{:S(2)}) collective-permute-start(bf16[128,2048]{1,0:T(8,128)(2,1)S(1)} %collective-permute-done.3), channel_id=1, source_target_pairs={{0,4},{1,5},{2,6},{3,7},{4,12},{5,13},{6,14},{7,15},{8,0},{9,1},{1... | collective-permute-start | bytes 1572872 | tf_op jit(solution)/shard_map/ppermute | solution.py:42
  132.8 34.4 %collective-permute-start.27 = (bf16[128,2048]{1,0:T(8,128)(2,1)S(1)}, bf16[128,2048]{1,0:T(8,128)(2,1)S(1)}, u32[]{:S(2)}, u32[]{:S(2)}) collective-permute-start(bf16[128,2048]{1,0:T(8,128)(2,1)S(1)} %collective-permute-done.25), channel_id=1, source_target_pairs={{0,4},{1,5},{2,6},{3,7},{4,12},{5,13},{6,14},{7,15},{8,0},{9,1},{1... | collective-permute-start | bytes 1572872 | tf_op jit(solution)/shard_map/ppermute | solution.py:42
  147.7 194.7 %collective-permute-start.12 = (bf16[768,4096]{1,0:T(8,128)(2,1)}, bf16[768,4096]{1,0:T(8,128)(2,1)}, u32[]{:S(2)}, u32[]{:S(2)}) collective-permute-start(bf16[768,4096]{1,0:T(8,128)(2,1)} %bitcast.16), channel_id=1, source_target_pairs={{0,1},{1,0},{2,3},{3,2},{4,5},{5,4},{6,7},{7,6},{8,9},{9,8},{10,11... | collective-permute-start | bytes 18874376 | tf_op jit(solution)/shard_map/ppermute | solution.py:42
  167.1 162.7 %collective-permute-start.11 = (bf16[4096,768]{1,0:T(8,128)(2,1)}, bf16[4096,768]{1,0:T(8,128)(2,1)}, u32[]{:S(2)}, u32[]{:S(2)}) collective-permute-start(bf16[4096,768]{1,0:T(8,128)(2,1)} %bitcast.15), channel_id=1, source_target_pairs={{0,1},{1,0},{2,3},{3,2},{4,5},{5,4},{6,7},{7,6},{8,9},{9,8},{10,11... | collective-permute-start | bytes 18874376 | tf_op jit(solution)/shard_map/ppermute | solution.py:42
  167.5 15.5 %collective-permute-start.28 = (bf16[128,2048]{1,0:T(8,128)(2,1)S(1)}, bf16[128,2048]{1,0:T(8,128)(2,1)S(1)}, u32[]{:S(2)}, u32[]{:S(2)}) collective-permute-start(bf16[128,2048]{1,0:T(8,128)(2,1)S(1)} %collective-permute-done.26), channel_id=1, source_target_pairs={{0,4},{1,5},{2,6},{3,7},{4,12},{5,13},{6,14},{7,15},{8,0},{9,1},{1... | collective-permute-start | bytes 1572872 | tf_op jit(solution)/shard_map/ppermute | solution.py:42
  183.0 153.9 %collective-permute-start.10 = (bf16[4096,768]{1,0:T(8,128)(2,1)}, bf16[4096,768]{1,0:T(8,128)(2,1)}, u32[]{:S(2)}, u32[]{:S(2)}) collective-permute-start(bf16[4096,768]{1,0:T(8,128)(2,1)} %bitcast.14), channel_id=1, source_target_pairs={{0,1},{1,0},{2,3},{3,2},{4,5},{5,4},{6,7},{7,6},{8,9},{9,8},{10,11... | collective-permute-start | bytes 18874376 | tf_op jit(solution)/shard_map/ppermute | solution.py:42
  184.3 20.0 %collective-permute-start.30 = (bf16[96,4096]{1,0:T(8,128)(2,1)S(1)}, bf16[96,4096]{1,0:T(8,128)(2,1)S(1)}, u32[]{:S(2)}, u32[]{:S(2)}) collective-permute-start(bf16[96,4096]{1,0:T(8,128)(2,1)S(1)} %fusion.24), channel_id=1, source_target_pairs={{0,2},{1,3},{2,0},{3,1},{4,6},{5,7},{6,4},{7,5},{8,10},{9,11},{10,... | collective-permute-start | bytes 2359304 | tf_op jit(solution)/shard_map/ppermute | solution.py:42
  204.3 20.4 %collective-permute-start.7 = (bf16[96,4096]{1,0:T(8,128)(2,1)S(1)}, bf16[96,4096]{1,0:T(8,128)(2,1)S(1)}, u32[]{:S(2)}, u32[]{:S(2)}) collective-permute-start(bf16[96,4096]{1,0:T(8,128)(2,1)S(1)} %fusion.28), channel_id=1, source_target_pairs={{0,2},{1,3},{2,0},{3,1},{4,6},{5,7},{6,4},{7,5},{8,10},{9,11},{10,... | collective-permute-start | bytes 2359304 | tf_op jit(solution)/shard_map/ppermute | solution.py:42
  206.0 52.9 %collective-permute-start.8 = (bf16[96,4096]{1,0:T(8,128)(2,1)S(1)}, bf16[96,4096]{1,0:T(8,128)(2,1)S(1)}, u32[]{:S(2)}, u32[]{:S(2)}) collective-permute-start(bf16[96,4096]{1,0:T(8,128)(2,1)S(1)} %fusion.27), channel_id=1, source_target_pairs={{0,2},{1,3},{2,0},{3,1},{4,6},{5,7},{6,4},{7,5},{8,10},{9,11},{10,... | collective-permute-start | bytes 2359304 | tf_op jit(solution)/shard_map/ppermute | solution.py:42
  224.7 32.4 %collective-permute-start.31 = (bf16[96,4096]{1,0:T(8,128)(2,1)S(1)}, bf16[96,4096]{1,0:T(8,128)(2,1)S(1)}, u32[]{:S(2)}, u32[]{:S(2)}) collective-permute-start(bf16[96,4096]{1,0:T(8,128)(2,1)S(1)} %fusion.23), channel_id=1, source_target_pairs={{0,2},{1,3},{2,0},{3,1},{4,6},{5,7},{6,4},{7,5},{8,10},{9,11},{10,... | collective-permute-start | bytes 2359304 | tf_op jit(solution)/shard_map/ppermute | solution.py:42
  257.2 36.0 %collective-permute-start.9 = (bf16[96,4096]{1,0:T(8,128)(2,1)S(1)}, bf16[96,4096]{1,0:T(8,128)(2,1)S(1)}, u32[]{:S(2)}, u32[]{:S(2)}) collective-permute-start(bf16[96,4096]{1,0:T(8,128)(2,1)S(1)} %fusion.26), channel_id=1, source_target_pairs={{0,2},{1,3},{2,0},{3,1},{4,6},{5,7},{6,4},{7,5},{8,10},{9,11},{10,... | collective-permute-start | bytes 2359304 | tf_op jit(solution)/shard_map/ppermute | solution.py:42
  258.9 33.4 %collective-permute-start.32 = (bf16[96,4096]{1,0:T(8,128)(2,1)S(1)}, bf16[96,4096]{1,0:T(8,128)(2,1)S(1)}, u32[]{:S(2)}, u32[]{:S(2)}) collective-permute-start(bf16[96,4096]{1,0:T(8,128)(2,1)S(1)} %fusion.22), channel_id=1, source_target_pairs={{0,2},{1,3},{2,0},{3,1},{4,6},{5,7},{6,4},{7,5},{8,10},{9,11},{10,... | collective-permute-start | bytes 2359304 | tf_op jit(solution)/shard_map/ppermute | solution.py:42
  293.2 6.6 %copy-start.5 = (bf16[384,4096]{1,0:T(8,128)(2,1)}, bf16[384,4096]{1,0:T(8,128)(2,1)S(1)}, u32[]{:S(2)}) copy-start(bf16[384,4096]{1,0:T(8,128)(2,1)S(1)} %get-tuple-element.71) | copy-start | bytes 9437188
  329.5 1.9 copy-start.6
  336.8 5.6 copy-start.8
  371.6 20.5 %collective-permute-start.33 = (bf16[96,4096]{1,0:T(8,128)(2,1)S(1)}, bf16[96,4096]{1,0:T(8,128)(2,1)S(1)}, u32[]{:S(2)}, u32[]{:S(2)}) collective-permute-start(bf16[96,4096]{1,0:T(8,128)(2,1)S(1)} %pad_maximum_fusion.14), channel_id=1, source_target_pairs={{0,2},{1,3},{2,0},{3,1},{4,6},{5,7},{6,4},{7,5},{8,10},{9,11},{10,... | collective-permute-start | bytes 2359304 | tf_op jit(solution)/shard_map/ppermute | solution.py:42
  372.7 36.3 %collective-permute-start.34 = (bf16[96,4096]{1,0:T(8,128)(2,1)S(1)}, bf16[96,4096]{1,0:T(8,128)(2,1)S(1)}, u32[]{:S(2)}, u32[]{:S(2)}) collective-permute-start(bf16[96,4096]{1,0:T(8,128)(2,1)S(1)} %pad_maximum_fusion.15), channel_id=1, source_target_pairs={{0,2},{1,3},{2,0},{3,1},{4,6},{5,7},{6,4},{7,5},{8,10},{9,11},{10,... | collective-permute-start | bytes 2359304 | tf_op jit(solution)/shard_map/ppermute | solution.py:42
  373.9 70.3 %collective-permute-start.35 = (bf16[96,4096]{1,0:T(8,128)(2,1)S(1)}, bf16[96,4096]{1,0:T(8,128)(2,1)S(1)}, u32[]{:S(2)}, u32[]{:S(2)}) collective-permute-start(bf16[96,4096]{1,0:T(8,128)(2,1)S(1)} %pad_maximum_fusion.16), channel_id=1, source_target_pairs={{0,2},{1,3},{2,0},{3,1},{4,6},{5,7},{6,4},{7,5},{8,10},{9,11},{10,... | collective-permute-start | bytes 2359304 | tf_op jit(solution)/shard_map/ppermute | solution.py:42
  374.9 67.8 %collective-permute-start.36 = (bf16[96,4096]{1,0:T(8,128)(2,1)S(1)}, bf16[96,4096]{1,0:T(8,128)(2,1)S(1)}, u32[]{:S(2)}, u32[]{:S(2)}) collective-permute-start(bf16[96,4096]{1,0:T(8,128)(2,1)S(1)} %pad_maximum_fusion.17), channel_id=1, source_target_pairs={{0,2},{1,3},{2,0},{3,1},{4,6},{5,7},{6,4},{7,5},{8,10},{9,11},{10,... | collective-permute-start | bytes 2359304 | tf_op jit(solution)/shard_map/ppermute | solution.py:42
  376.2 131.4 %collective-permute-start.13 = (bf16[96,4096]{1,0:T(8,128)(2,1)S(1)}, bf16[96,4096]{1,0:T(8,128)(2,1)S(1)}, u32[]{:S(2)}, u32[]{:S(2)}) collective-permute-start(bf16[96,4096]{1,0:T(8,128)(2,1)S(1)} %pad_maximum_fusion.10), channel_id=1, source_target_pairs={{0,2},{1,3},{2,0},{3,1},{4,6},{5,7},{6,4},{7,5},{8,10},{9,11},{10,... | collective-permute-start | bytes 2359304 | tf_op jit(solution)/shard_map/ppermute | solution.py:42
  392.2 116.5 %collective-permute-start.14 = (bf16[96,4096]{1,0:T(8,128)(2,1)S(1)}, bf16[96,4096]{1,0:T(8,128)(2,1)S(1)}, u32[]{:S(2)}, u32[]{:S(2)}) collective-permute-start(bf16[96,4096]{1,0:T(8,128)(2,1)S(1)} %pad_maximum_fusion.11), channel_id=1, source_target_pairs={{0,2},{1,3},{2,0},{3,1},{4,6},{5,7},{6,4},{7,5},{8,10},{9,11},{10,... | collective-permute-start | bytes 2359304 | tf_op jit(solution)/shard_map/ppermute | solution.py:42
  409.0 101.6 %collective-permute-start.15 = (bf16[96,4096]{1,0:T(8,128)(2,1)S(1)}, bf16[96,4096]{1,0:T(8,128)(2,1)S(1)}, u32[]{:S(2)}, u32[]{:S(2)}) collective-permute-start(bf16[96,4096]{1,0:T(8,128)(2,1)S(1)} %pad_maximum_fusion.12), channel_id=1, source_target_pairs={{0,2},{1,3},{2,0},{3,1},{4,6},{5,7},{6,4},{7,5},{8,10},{9,11},{10,... | collective-permute-start | bytes 2359304 | tf_op jit(solution)/shard_map/ppermute | solution.py:42
  442.7 64.3 %collective-permute-start.16 = (bf16[96,4096]{1,0:T(8,128)(2,1)S(1)}, bf16[96,4096]{1,0:T(8,128)(2,1)S(1)}, u32[]{:S(2)}, u32[]{:S(2)}) collective-permute-start(bf16[96,4096]{1,0:T(8,128)(2,1)S(1)} %pad_maximum_fusion.13), channel_id=1, source_target_pairs={{0,2},{1,3},{2,0},{3,1},{4,6},{5,7},{6,4},{7,5},{8,10},{9,11},{10,... | collective-permute-start | bytes 2359304 | tf_op jit(solution)/shard_map/ppermute | solution.py:42
  444.7 66.1 %collective-permute-start.37 = (bf16[128,2048]{1,0:T(8,128)(2,1)S(1)}, bf16[128,2048]{1,0:T(8,128)(2,1)S(1)}, u32[]{:S(2)}, u32[]{:S(2)}) collective-permute-start(bf16[128,2048]{1,0:T(8,128)(2,1)S(1)} %convolution_convert_fusion.9), channel_id=1, source_target_pairs={{0,8},{1,9},{2,10},{3,11},{4,0},{5,1},{6,2},{7,3},{8,12},{9,13},{1... | collective-permute-start | bytes 1572872 | tf_op jit(solution)/shard_map/ppermute | solution.py:42
  507.0 14.9 %collective-permute-start.40 = (bf16[128,2048]{1,0:T(8,128)(2,1)S(1)}, bf16[128,2048]{1,0:T(8,128)(2,1)S(1)}, u32[]{:S(2)}, u32[]{:S(2)}) collective-permute-start(bf16[128,2048]{1,0:T(8,128)(2,1)S(1)} %convolution_convert_fusion.8), channel_id=1, source_target_pairs={{0,8},{1,9},{2,10},{3,11},{4,0},{5,1},{6,2},{7,3},{8,12},{9,13},{1... | collective-permute-start | bytes 1572872 | tf_op jit(solution)/shard_map/ppermute | solution.py:42
  507.5 25.6 %collective-permute-start.17 = (bf16[128,2048]{1,0:T(8,128)(2,1)S(1)}, bf16[128,2048]{1,0:T(8,128)(2,1)S(1)}, u32[]{:S(2)}, u32[]{:S(2)}) collective-permute-start(bf16[128,2048]{1,0:T(8,128)(2,1)S(1)} %convolution_convert_fusion.11), channel_id=1, source_target_pairs={{0,8},{1,9},{2,10},{3,11},{4,0},{5,1},{6,2},{7,3},{8,12},{9,13},{1... | collective-permute-start | bytes 1572872 | tf_op jit(solution)/shard_map/ppermute | solution.py:42
  508.7 35.7 %collective-permute-start.20 = (bf16[128,2048]{1,0:T(8,128)(2,1)S(1)}, bf16[128,2048]{1,0:T(8,128)(2,1)S(1)}, u32[]{:S(2)}, u32[]{:S(2)}) collective-permute-start(bf16[128,2048]{1,0:T(8,128)(2,1)S(1)} %convolution_convert_fusion.10), channel_id=1, source_target_pairs={{0,8},{1,9},{2,10},{3,11},{4,0},{5,1},{6,2},{7,3},{8,12},{9,13},{1... | collective-permute-start | bytes 1572872 | tf_op jit(solution)/shard_map/ppermute | solution.py:42
  511.2 44.4 %collective-permute-start.38 = (bf16[128,2048]{1,0:T(8,128)(2,1)S(1)}, bf16[128,2048]{1,0:T(8,128)(2,1)S(1)}, u32[]{:S(2)}, u32[]{:S(2)}) collective-permute-start(bf16[128,2048]{1,0:T(8,128)(2,1)S(1)} %fusion.16), channel_id=1, source_target_pairs={{0,8},{1,9},{2,10},{3,11},{4,0},{5,1},{6,2},{7,3},{8,12},{9,13},{1... | collective-permute-start | bytes 1572872 | tf_op jit(solution)/shard_map/ppermute | solution.py:42
  522.2 44.6 %collective-permute-start.41 = (bf16[128,2048]{1,0:T(8,128)(2,1)S(1)}, bf16[128,2048]{1,0:T(8,128)(2,1)S(1)}, u32[]{:S(2)}, u32[]{:S(2)}) collective-permute-start(bf16[128,2048]{1,0:T(8,128)(2,1)S(1)} %fusion.19), channel_id=1, source_target_pairs={{0,8},{1,9},{2,10},{3,11},{4,0},{5,1},{6,2},{7,3},{8,12},{9,13},{1... | collective-permute-start | bytes 1572872 | tf_op jit(solution)/shard_map/ppermute | solution.py:42
  533.5 44.6 %collective-permute-start.18 = (bf16[128,2048]{1,0:T(8,128)(2,1)S(1)}, bf16[128,2048]{1,0:T(8,128)(2,1)S(1)}, u32[]{:S(2)}, u32[]{:S(2)}) collective-permute-start(bf16[128,2048]{1,0:T(8,128)(2,1)S(1)} %fusion.10), channel_id=1, source_target_pairs={{0,8},{1,9},{2,10},{3,11},{4,0},{5,1},{6,2},{7,3},{8,12},{9,13},{1... | collective-permute-start | bytes 1572872 | tf_op jit(solution)/shard_map/ppermute | solution.py:42
  544.7 44.6 %collective-permute-start.21 = (bf16[128,2048]{1,0:T(8,128)(2,1)S(1)}, bf16[128,2048]{1,0:T(8,128)(2,1)S(1)}, u32[]{:S(2)}, u32[]{:S(2)}) collective-permute-start(bf16[128,2048]{1,0:T(8,128)(2,1)S(1)} %fusion.13), channel_id=1, source_target_pairs={{0,8},{1,9},{2,10},{3,11},{4,0},{5,1},{6,2},{7,3},{8,12},{9,13},{1... | collective-permute-start | bytes 1572872 | tf_op jit(solution)/shard_map/ppermute | solution.py:42
  555.9 44.6 %collective-permute-start.39 = (bf16[128,2048]{1,0:T(8,128)(2,1)S(1)}, bf16[128,2048]{1,0:T(8,128)(2,1)S(1)}, u32[]{:S(2)}, u32[]{:S(2)}) collective-permute-start(bf16[128,2048]{1,0:T(8,128)(2,1)S(1)} %fusion.15), channel_id=1, source_target_pairs={{0,8},{1,9},{2,10},{3,11},{4,0},{5,1},{6,2},{7,3},{8,12},{9,13},{1... | collective-permute-start | bytes 1572872 | tf_op jit(solution)/shard_map/ppermute | solution.py:42
  567.2 44.6 %collective-permute-start.42 = (bf16[128,2048]{1,0:T(8,128)(2,1)S(1)}, bf16[128,2048]{1,0:T(8,128)(2,1)S(1)}, u32[]{:S(2)}, u32[]{:S(2)}) collective-permute-start(bf16[128,2048]{1,0:T(8,128)(2,1)S(1)} %fusion.18), channel_id=1, source_target_pairs={{0,8},{1,9},{2,10},{3,11},{4,0},{5,1},{6,2},{7,3},{8,12},{9,13},{1... | collective-permute-start | bytes 1572872 | tf_op jit(solution)/shard_map/ppermute | solution.py:42
  578.4 44.6 %collective-permute-start.19 = (bf16[128,2048]{1,0:T(8,128)(2,1)S(1)}, bf16[128,2048]{1,0:T(8,128)(2,1)S(1)}, u32[]{:S(2)}, u32[]{:S(2)}) collective-permute-start(bf16[128,2048]{1,0:T(8,128)(2,1)S(1)} %fusion.9), channel_id=1, source_target_pairs={{0,8},{1,9},{2,10},{3,11},{4,0},{5,1},{6,2},{7,3},{8,12},{9,13},{1... | collective-permute-start | bytes 1572872 | tf_op jit(solution)/shard_map/ppermute | solution.py:42
  589.6 40.5 %collective-permute-start.22 = (bf16[128,2048]{1,0:T(8,128)(2,1)S(1)}, bf16[128,2048]{1,0:T(8,128)(2,1)S(1)}, u32[]{:S(2)}, u32[]{:S(2)}) collective-permute-start(bf16[128,2048]{1,0:T(8,128)(2,1)S(1)} %fusion.12), channel_id=1, source_target_pairs={{0,8},{1,9},{2,10},{3,11},{4,0},{5,1},{6,2},{7,3},{8,12},{9,13},{1... | collective-permute-start | bytes 1572872 | tf_op jit(solution)/shard_map/ppermute | solution.py:42

commit v2 on v1

v2 whole, which is shorter than its diff:
```python
import jax
import jax.numpy as jnp
from jax import lax
from jax.experimental import pallas as pl
from jax.experimental.pallas import tpu as pltpu
from jax.sharding import PartitionSpec as P

contract_last = (((1,), (1,)), ((), ()))
contract_first = (((0,), (0,)), ((), ()))
STREAMS = 2


def layout(wide):
    if wide == 16:
        return 4, 2, (0, 1, 3, 2)
    return wide // 2, 1, tuple(range(wide // 2))


def tie(value, *others):
    others = [other for other in others if other is not None]
    if not others:
        return value
    return pl.pallas_call(
        lambda *refs: None,
        out_shape=jax.ShapeDtypeStruct(value.shape, value.dtype),
        in_specs=[pl.BlockSpec(memory_space=pl.ANY)] * (1 + len(others)),
        out_specs=pl.BlockSpec(memory_space=pl.ANY),
        input_output_aliases={0: 0},
        name="tie",
    )(value, *others)


def whole_spec(shape):
    return pl.BlockSpec(shape, lambda *_: (0,) * len(shape))


ANYWHERE = pl.BlockSpec(memory_space=pl.ANY)


def params(mib):
    return pltpu.CompilerParams(vmem_limit_bytes=mib * 2**20)


def pick_rows(parts, pick, weight, refs):
    start = 0
    for part in parts:
        stop = start + part.shape[1]
        rows = jnp.dot(pick, part, preferred_element_type=jnp.float32)
        if weight is not None:
            rows = weight * rows
        rows = rows.astype(jnp.bfloat16)
        at = 0
        for ref in refs:
            ref[:, start:stop] = rows[at : at + ref.shape[0]]
            at += ref.shape[0]
        start = stop


def first_choice(experts, parts, width, cap, top, deps):
    rows = parts[0].shape[0]
    half = width // len(parts)
    count = experts.shape[0]
    chips = count // 2

    def body(experts, *refs):
        parts = refs[: len(refs) - chips - 2 - len(deps)]
        outs = refs[len(refs) - chips - 2 : len(refs) - 2]
        pick_ref, gated_ref = refs[-2:]
        routes = parts[0][0:16, half : half + rows].astype(jnp.float32)
        line = [routes[j : j + 1] for j in range(3 * top)]
        codes = [line[top + j] * 32.0 + line[2 * top + j] for j in range(top)]
        total = sum(codes[1:], codes[0])
        share = [code / total for code in codes]
        ids = [value.astype(jnp.int32) for value in line[:top]]
        hits, gates = [], []
        for k in range(count):
            hit, gate = jnp.zeros((1, rows), jnp.float32), jnp.zeros((1, rows), jnp.float32)
            for j in range(top):
                same = ids[j] == experts[k]
                hit = jnp.where(same, 1.0, hit)
                gate = jnp.where(same, gate + share[j], gate)
            hits.append(hit)
            gates.append(gate)
        stacked = jnp.concatenate(hits + [jnp.zeros((8 - count, rows), jnp.float32)], axis=0)
        upto = lax.broadcasted_iota(jnp.int32, (rows, rows), 0) <= lax.broadcasted_iota(jnp.int32, (rows, rows), 1)
        upto = jnp.where(upto, 1.0, 0.0).astype(jnp.bfloat16)
        spot = jnp.dot(stacked.astype(jnp.bfloat16), upto, preferred_element_type=jnp.float32).astype(jnp.int32) - 1
        slot = lax.broadcasted_iota(jnp.int32, (cap, rows), 0)
        picks, gated = [], []
        for k in range(count):
            chosen = jnp.where(slot == spot[k : k + 1], jnp.broadcast_to(hits[k], (cap, rows)), 0.0)
            picks.append(chosen)
            gated.append(chosen * gates[k])
        pick = jnp.concatenate(picks, axis=0).astype(jnp.bfloat16)
        pick_ref[...] = pick
        gated_ref[...] = jnp.concatenate(gated, axis=0)
        pick_rows([parts[0][:, :half]] + [part[...] for part in parts[1:]], pick, None, outs)

    rows_of = jax.ShapeDtypeStruct((2 * cap, width), jnp.bfloat16)
    results = pl.pallas_call(
        body,
        grid=(1,),
        in_specs=[pl.BlockSpec(memory_space=pltpu.SMEM)]
        + [whole_spec(part.shape) for part in parts]
        + [ANYWHERE] * len(deps),
        out_specs=[whole_spec((2 * cap, width))] * chips + [whole_spec((count * cap, rows))] * 2,
        out_shape=[rows_of] * chips
        + [
            jax.ShapeDtypeStruct((count * cap, rows), jnp.bfloat16),
            jax.ShapeDtypeStruct((count * cap, rows), jnp.float32),
        ],
        compiler_params=params(24),
        name="first_choice",
    )(experts, *parts, *deps)
    return results[:chips], results[chips:]


def next_choice(tables, parts, width, cap, deps):
    pick, gated = tables
    chips = pick.shape[0] // (2 * cap)

    def body(pick, gated, *refs):
        parts = refs[: len(refs) - chips - len(deps)]
        weight = jnp.sum(gated[...], axis=1, keepdims=True)
        pick_rows([part[...] for part in parts], pick[...], weight, refs[len(refs) - chips :])

    return pl.pallas_call(
        body,
        grid=(1,),
        in_specs=[whole_spec(pick.shape), whole_spec(gated.shape)]
        + [whole_spec(part.shape) for part in parts]
        + [ANYWHERE] * len(deps),
        out_specs=[whole_spec((2 * cap, width))] * chips,
        out_shape=[jax.ShapeDtypeStruct((2 * cap, width), jnp.bfloat16)] * chips,
        compiler_params=params(24),
        name="next_choice",
    )(pick, gated, *parts, *deps)


def back_sum(tables, weighted, pieces, came, part, parts, full=None):
    pick, gated = tables
    rows = pick.shape[1]
    width = pieces[0].shape[1]
    step = width // parts
    final = full is not None

    def body(mix, *refs):
        out = refs[-1]
        at, total = 0, None
        if came is not None:
            total = refs[len(pieces)][...].astype(jnp.float32)
        for ref in refs[: len(pieces)]:
            share = mix[at : at + ref.shape[0]]
            at += ref.shape[0]
            if weighted:
                upper = share.astype(jnp.bfloat16)
                shares = [upper, (share - upper.astype(jnp.float32)).astype(jnp.bfloat16)]
            else:
                shares = [share]
            for value in shares:
                more = lax.dot_general(value, ref[...], contract_first, preferred_element_type=jnp.float32)
                total = more if total is None else total + more
        out[...] = total.astype(jnp.bfloat16)

    mix = gated if weighted else pick
    operands = [mix, *pieces]
    specs = [whole_spec(mix.shape)] + [pl.BlockSpec((piece.shape[0], step), lambda g: (0, part)) for piece in pieces]
    if came is not None:
        operands.append(came)
        specs.append(whole_spec((rows, step)))
    aliases = {}
    if final and part > 0:
        aliases = {len(operands): 0}
        operands.append(full)
        specs.append(ANYWHERE)
    return pl.pallas_call(
        body,
        grid=(1,),
        in_specs=specs,
        out_specs=pl.BlockSpec((rows, step), lambda g: (0, part if final else 0)),
        out_shape=jax.ShapeDtypeStruct((rows, width if final else step), jnp.bfloat16),
        input_output_aliases=aliases,
        compiler_params=params(24),
        name="back_sum",
    )(*operands)


TILE = 256
WIDE_TILE = 1024


def expert_call(body, pieces, extras, weights, scratch, more_outs, cap, width, hidden, name, deps):
    firsts, seconds = hidden // TILE, width // WIDE_TILE
    total = len(pieces) * cap

    def first(j):
        return jnp.minimum(j, firsts - 1)

    def second(j):
        return jnp.maximum(j - firsts, 0)

    def at(e, mine, index, last):
        return jnp.where(e == mine, index, 0 if mine else last)

    specs = [pl.BlockSpec(piece.shape, lambda e, j: (0, 0), pipeline_mode=pl.Buffered(1)) for piece in pieces]
    specs += [pl.BlockSpec((1, total, TILE), lambda e, j: (e, 0, first(j)))] * len(extras)
    operands = list(pieces) + list(extras)
    for pair, block, axis, stage in weights:
        for mine, weight in enumerate(pair):
            last = (firsts if stage == 0 else seconds) - 1

            def where(e, j, mine=mine, axis=axis, stage=stage, last=last):
                index = at(e, mine, first(j) if stage == 0 else second(j), last)
                return (index, 0) if axis == 0 else (0, index)

            specs.append(pl.BlockSpec(block, where))
            operands.append(weight)
    specs += [ANYWHERE] * len(deps)
    operands += deps
    out_specs = [pl.BlockSpec((cap, WIDE_TILE), lambda e, j: (e, second(j)))] * len(pieces)
    out_shape = [jax.ShapeDtypeStruct((2 * cap, width), jnp.bfloat16)] * len(pieces)
    out_specs += [pl.BlockSpec((1, total, TILE), lambda e, j: (e, 0, first(j)))] * len(more_outs)
    out_shape += more_outs
    size = 6 * total * width * hidden * 2
    return pl.pallas_call(
        body,
        grid=(2, firsts + seconds),
        in_specs=specs,
        out_specs=out_specs,
        out_shape=out_shape,
        scratch_shapes=scratch,
        compiler_params=params(56),
        cost_estimate=pl.CostEstimate(flops=size, bytes_accessed=12 * width * hidden + 8 * total * width, transcendentals=0),
        name=name,
    )(*operands)


def put_rows(pieces, rows, e, cap):
    for i, piece in enumerate(pieces):
        rows[i * cap : (i + 1) * cap] = piece[pl.ds(pl.multiple_of(e * cap, 16), cap)]


def take_rows(outs, value, cap):
    for i, out in enumerate(outs):
        out[...] = value[i * cap : (i + 1) * cap]


def expert_forward(pieces, gates, ups, downs, cap, deps=()):
    width, hidden = gates[0].shape
    total = len(pieces) * cap
    firsts = hidden // TILE

    def body(*refs):
        n = len(pieces)
        pieces_in, refs = refs[:n], refs[n:]
        (gate0, gate1, up0, up1, down0, down1), refs = refs[:6], refs[6 + len(deps) :]
        outs, (slope, active, rows, inner) = refs[:n], refs[n:]
        e, j = pl.program_id(0), pl.program_id(1)

        @pl.when(j == 0)
        def _():
            put_rows(pieces_in, rows, e, cap)

        def enter(gate, up):
            pre_gate = jnp.dot(rows[...], gate[...], preferred_element_type=jnp.float32)
            pre_up = jnp.dot(rows[...], up[...], preferred_element_type=jnp.float32)
            logistic = jax.nn.sigmoid(pre_gate)
            activated = pre_gate * logistic
            active[0] = activated
            slope[0] = pre_up * logistic * (1.0 + pre_gate * (1.0 - logistic))
            for k in range(firsts):

                @pl.when(j == k)
                def _():
                    inner[:, k * TILE : (k + 1) * TILE] = (activated * pre_up).astype(jnp.bfloat16)

        def leave(down):
            value = jnp.dot(inner[...], down[...], preferred_element_type=jnp.float32)
            take_rows(outs, value.astype(jnp.bfloat16), cap)

        for mine, (gate, up, down) in enumerate(((gate0, up0, down0), (gate1, up1, down1))):
            pl.when((e == mine) & (j < firsts))(lambda gate=gate, up=up: enter(gate, up))
            pl.when((e == mine) & (j >= firsts))(lambda down=down: leave(down))

    saved = jax.ShapeDtypeStruct((2, total, hidden), jnp.float32)
    weights = [
        (gates, (width, TILE), 1, 0),
        (ups, (width, TILE), 1, 0),
        (downs, (hidden, WIDE_TILE), 1, 1),
    ]
    scratch = [pltpu.VMEM((total, width), jnp.bfloat16), pltpu.VMEM((total, hidden), jnp.bfloat16)]
    results = expert_call(
        body, pieces, [], weights, scratch, [saved, saved], cap, width, hidden, "expert_forward", list(deps)
    )
    return list(results[:-2]), list(results[-2:])


def expert_backward(pieces, saved, gates, ups, downs, cap, deps=()):
    width, hidden = gates[0].shape
    total = len(pieces) * cap
    firsts = hidden // TILE

    def body(*refs):
        n = len(pieces)
        pieces_in, refs = refs[:n], refs[n:]
        (slope, active), refs = refs[:2], refs[2:]
        (down0, down1, gate0, gate1, up0, up1), refs = refs[:6], refs[6 + len(deps) :]
        outs, (rows, gate_grad, up_grad) = refs[:n], refs[n:]
        e, j = pl.program_id(0), pl.program_id(1)

        @pl.when(j == 0)
        def _():
            put_rows(pieces_in, rows, e, cap)

        def enter(down):
            hidden_grad = lax.dot_general(rows[...], down[...], contract_last, preferred_element_type=jnp.float32)
            for k in range(firsts):

                @pl.when(j == k)
                def _():
                    gate_grad[:, k * TILE : (k + 1) * TILE] = (hidden_grad * slope[0]).astype(jnp.bfloat16)
                    up_grad[:, k * TILE : (k + 1) * TILE] = (hidden_grad * active[0]).astype(jnp.bfloat16)

        def leave(gate, up):
            value = lax.dot_general(gate_grad[...], gate[...], contract_last, preferred_element_type=jnp.float32)
            value += lax.dot_general(up_grad[...], up[...], contract_last, preferred_element_type=jnp.float32)
            take_rows(outs, value.astype(jnp.bfloat16), cap)

        for mine, (gate, up, down) in enumerate(((gate0, up0, down0), (gate1, up1, down1))):
            pl.when((e == mine) & (j < firsts))(lambda down=down: enter(down))
            pl.when((e == mine) & (j >= firsts))(lambda gate=gate, up=up: leave(gate, up))

    weights = [
        (downs, (TILE, width), 0, 0),
        (gates, (WIDE_TILE, hidden), 0, 1),
        (ups, (WIDE_TILE, hidden), 0, 1),
    ]
    scratch = [pltpu.VMEM((total, width), jnp.bfloat16)] + [pltpu.VMEM((total, hidden), jnp.bfloat16)] * 2
    return expert_call(
        body, pieces, list(saved), weights, scratch, [], cap, width, hidden, "expert_backward", list(deps)
    )


def per_device(tokens, cotangent, expert_ids, gate_codes, w_gate, w_up, w_down):
    wide = lax.axis_size("wide")
    rows, width = tokens.shape
    top = expert_ids.shape[1]
    cap = -(-3 * rows * top // (2 * wide) // 16) * 16
    zs, ys, ring = layout(wide)
    me = lax.axis_index("wide")
    core, col, my_z = me % 2, (me // 2) % ys, me // (2 * ys)

    def pairs(move):
        out = []
        for z in range(zs):
            for y in range(ys):
                for c in range(2):
                    tz, ty, tc = move(z, y, c)
                    out.append(((z * ys + y) * 2 + c, (tz * ys + ty) * 2 + tc))
        return out

    place = {z: i for i, z in enumerate(ring)}
    ahead = pairs(lambda z, y, c: (ring[(place[z] + 1) % zs], y, c))
    back = pairs(lambda z, y, c: (ring[(place[z] - 1) % zs], y, c))
    across = pairs(lambda z, y, c: (z, (y + 1) % ys, c))
    twin = pairs(lambda z, y, c: (z, y, 1 - c))

    def permute(value, perm):
        return lax.ppermute(value, "wide", perm)

    lanes = {}

    def send(lane, value, perm, depth=0):
        got = lanes.setdefault(lane, [])
        if depth and len(got) >= depth:
            value = tie(value, got[-depth])
        got.append(permute(value, perm))
        return got[-1]

    chip = my_z * ys + col
    experts = jnp.stack([2 * chip + core, 2 * chip + 1 - core])
    if ys == 2:
        there = my_z * ys + 1 - col
        experts = jnp.concatenate([experts, jnp.stack([2 * there + core, 2 * there + 1 - core])])
    slots = 2 * cap

    def cut(value):
        step = width // STREAMS
        return [value[:, i * step : (i + 1) * step] for i in range(STREAMS)]

    half = width // STREAMS
    routes = jnp.concatenate([expert_ids, gate_codes // 32, gate_codes % 32], axis=1).astype(jnp.bfloat16)
    routes = jnp.pad(routes.T, ((0, rows - 3 * top), (0, 0)))
    blocks = {
        "tokens": [[jnp.concatenate([tokens[:, :half], routes], axis=1)] + cut(tokens)[1:]],
        "cot": [cut(cotangent)],
    }
    own, other = {"tokens": [], "cot": []}, {"tokens": [], "cot": []}
    tables = []

    def came(lane, index):
        got = lanes.get(lane, [])
        return got[index] if index < len(got) else None

    def onward(name, early=(), late=()):
        parts = blocks[name][-1]
        parts[0] = tie(parts[0], *early)
        parts[-1] = tie(parts[-1], *late)
        first = 1 if len(blocks[name]) == 1 else 0
        blocks[name].append([send(i, part, ahead, first) for i, part in enumerate(parts)])

    def choose(name, r, deps=()):
        deps = [dep for dep in deps if dep is not None]
        if name == "tokens":
            chosen, found = first_choice(experts, blocks[name][r], width, cap, top, deps)
            tables.append(found)
        else:
            chosen = next_choice(tables[r], blocks[name][r], width, cap, deps)
        own[name].append(chosen[0])
        if ys == 2:
            other[name].append(send("y", chosen[1], across))

    def homeward(results, r, depth=2):
        return send("y", results[zs + r], across, depth) if ys == 2 else None

    def combine(results, weighted, far=None):
        total, steps = [None] * STREAMS, []
        for r in reversed(range(zs)):
            pieces = [results[r]]
            if ys == 2:
                pieces.append(far if r == zs - 1 and far is not None else homeward(results, r))
            if r == 0:
                full = tokens
                for i in range(STREAMS):
                    full = back_sum(tables[0], weighted, pieces, total[i], i, STREAMS, full)
                return full, steps
            for i in range(STREAMS):
                value = back_sum(tables[r], weighted, pieces, total[i], i, STREAMS)
                total[i] = send(i, value, back, 1 if r == zs - 1 else 0)
            steps.append(list(total))

    def both(weight):
        return weight[0], permute(weight[0], twin)

    gate_mats, up_mats, down_mats = both(w_gate), both(w_up), both(w_down)
    last = zs - 1
    choose("tokens", 0)
    choose("cot", 0)
    for r in range(1, zs):
        onward("tokens", [own["cot"][0] if r == 2 else own["tokens"][r - 2]] if r > 1 else [], [came("y", r - 2) if r > 1 else None])
        choose("tokens", r)
    for r in range(1, zs):
        if r == last:
            outs, saved = expert_forward(own["tokens"] + other["tokens"], gate_mats, up_mats, down_mats, cap)
        onward("cot", [own["tokens"][-1]] if r > 1 else [], [came("y", r + 1)] + ([outs[0]] if r == last else []))
        if r < last:
            choose("cot", r)
    far = homeward(outs, last)
    choose("cot", last, [outs[0]])
    moe_out, steps = combine(outs, True, far)
    deps = [came("y", 2 * zs + 1)] if ys == 2 else []
    grads = expert_backward(own["cot"] + other["cot"], saved, gate_mats, up_mats, down_mats, cap, deps + steps[0][:1])
    token_grad, _ = combine(grads, False)
    return (moe_out, token_grad)


def solution(mesh):
    return jax.shard_map(
        per_device,
        mesh=mesh,
        in_specs=(
            P(("group", "wide"), None),
            P(("group", "wide"), None),
            P(("group", "wide"), None),
            P(("group", "wide"), None),
            P("wide", None, None),
            P("wide", None, None),
            P("wide", None, None),
        ),
        out_specs=(P(("group", "wide"), None), P(("group", "wide"), None)),
        check_vma=False,
    )
```

time: 639 us -> 371 us (0.58)
  waiting for transfers between devices: 461 us -> 204 us
  Pallas kernels: 0 us -> 100 us
  matrix products: 89 us -> 0 us
  blocking collectives: 23.2 us -> 0 us
  local copies, waits for them, and re-layouts: 9.29 us -> 24.1 us
  other arithmetic: 15.5 us -> 1.59 us
  starting transfers between devices: 31.5 us -> 39.4 us
    ppermute x43, waiting for transfers between devices: 461 us -> 204 us  [permute(): return lax.ppermute(value, 'wide', perm)]
    pallas_call x0 -> x49, Pallas kernels: none -> 100 us  [the longest x2 60.8 us: expert_call(): pl.pallas_call(body, grid=(2, firsts + seconds), in_specs=specs, out_spec...]
    dot_general x44 -> x0, matrix products: 89 us -> none  [the longest x2 16.2 us: per_device(): lax.dot_general(up_grad, up_mats[e], contract_last, preferred_element_typ...]
    all_gather x1 -> x0, blocking collectives: 23.2 us -> none  [per_device(): lax.all_gather(jnp.concatenate([expert_ids, gate_codes], axis=1), 'wide')]
    unnamed x24 -> x128, local copies, waits for them, and re-layouts: 4.13 us -> 22.8 us
    ppermute x43, starting transfers between devices: 31.5 us -> 39.4 us  [permute(): return lax.ppermute(value, 'wide', perm)]
  transfers between devices with their start and end apart: 43 -> 43, of which waited for: 28 -> 22; matrix products, arithmetic and copies ran while one was open for 12% -> 1% of each run, Pallas kernels for 0% -> 27%
where the time goes in v2:
time: 371 us; the launch traced here: 370 us
  waiting for transfers between devices  204 us (55%)
  Pallas kernels  100 us (27%)
  starting transfers between devices  39.4 us (11%)
  local copies, waits for them, and re-layouts  24.1 us (6%)
    ppermute x43, waiting for transfers between devices, permute(): return lax.ppermute(value, 'wide', perm)  204 us
    pallas_call x2, Pallas kernels, expert_call(): pl.pallas_call(body, grid=(2, firsts + seconds), in_specs=specs, out_spec...  60.8 us
    ppermute x43, starting transfers between devices, permute(): return lax.ppermute(value, 'wide', perm)  39.4 us
    pallas_call x16, Pallas kernels, back_sum(): pl.pallas_call(body, grid=(1,), in_specs=specs, out_specs=pl.BlockSpec((r...  28.7 us
    unnamed x128, local copies, waits for them, and re-layouts  22.8 us
  transfers between devices with their start and end apart: 43, of which 22 were waited for; matrix products, arithmetic and copies ran while one was open for 1% of the time, Pallas kernels for 27%

profile of v2, /device:TPU:0, one launch (start us, length us, event | category | flops | bytes accessed | tf_op | source)
XLA Modules:
  0.0 370.2 jit_solution(17138482456472910446)
XLA Ops:
  1.7 1.3 fusion.6
  2.9 2.7 collective-permute-start.1
  7.2 1.2 first_choice.4
  8.5 1.6 collective-permute-start.3
  10.1 9.1 %collective-permute-done.1.refs_1_.refs_0_ = bf16[128,2048]{1,0:T(8,128)(2,1)S(1)} collective-permute-done((bf16[128,2048]{1,0:T(8,128)(2,1)S(1)}, bf16[128,2048]{1,0:T(8,128)(2,1)S(1)}, u32[]{:S(2)}, u32[]{:S(2)}) %collective-permute-start.1) | collective-permute-done | bytes 524320 | tf_op jit(solution)/shard_map/ppermute | solution.py:369
  20.1 1.5 next_choice.4
  22.6 11.9 %collective-permute-done.refs_0_ = bf16[128,2176]{1,0:T(8,128)(2,1)S(1)} collective-permute-done((bf16[128,2176]{1,0:T(8,128)(2,1)S(1)}, bf16[128,2176]{1,0:T(8,128)(2,1)S(1)}, u32[]{:S(2)}, u32[]{:S(2)}) %collective-permute-start) | collective-permute-done | bytes 557088 | tf_op jit(solution)/shard_map/ppermute | solution.py:369
  34.5 2.1 first_choice.5
  38.2 3.4 collective-permute-start.4
  41.6 12.6 %collective-permute-done.2.refs_0_ = bf16[128,2176]{1,0:T(8,128)(2,1)S(1)} collective-permute-done((bf16[128,2176]{1,0:T(8,128)(2,1)}, bf16[128,2176]{1,0:T(8,128)(2,1)S(1)}, u32[]{:S(2)}, u32[]{:S(2)}) %collective-permute-start.2) | collective-permute-done | bytes 557088 | tf_op jit(solution)/shard_map/ppermute | solution.py:369
  54.2 1.4 collective-permute-start.6
  55.6 7.8 %collective-permute-done.4.refs_1_.refs_0_ = bf16[128,2048]{1,0:T(8,128)(2,1)S(1)} collective-permute-done((bf16[128,2048]{1,0:T(8,128)(2,1)}, bf16[128,2048]{1,0:T(8,128)(2,1)S(1)}, u32[]{:S(2)}, u32[]{:S(2)}) %collective-permute-start.4) | collective-permute-done | bytes 524320 | tf_op jit(solution)/shard_map/ppermute | solution.py:369
  63.4 1.2 collective-permute-start.8
  64.5 1.2 first_choice.6
  67.3 7.7 %collective-permute-done.6.refs_1_.refs_4_ = bf16[96,4096]{1,0:T(8,128)(2,1)} collective-permute-done((bf16[96,4096]{1,0:T(8,128)(2,1)}, bf16[96,4096]{1,0:T(8,128)(2,1)}, u32[]{:S(2)}, u32[]{:S(2)}) %collective-permute-start.6) | collective-permute-done | bytes 786464 | tf_op jit(solution)/shard_map/ppermute | solution.py:369
  75.7 11.1 %collective-permute-done.8.refs_5_.refs_1_ = bf16[96,4096]{1,0:T(8,128)(2,1)} collective-permute-done((bf16[96,4096]{1,0:T(8,128)(2,1)}, bf16[96,4096]{1,0:T(8,128)(2,1)}, u32[]{:S(2)}, u32[]{:S(2)}) %collective-permute-start.8) | collective-permute-done | bytes 786464 | tf_op jit(solution)/shard_map/ppermute | solution.py:369
  87.1 11.5 %collective-permute-done.7.refs_1_ = bf16[128,2048]{1,0:T(8,128)(2,1)S(1)} collective-permute-done((bf16[128,2048]{1,0:T(8,128)(2,1)}, bf16[128,2048]{1,0:T(8,128)(2,1)S(1)}, u32[]{:S(2)}, u32[]{:S(2)}) %collective-permute-start.7) | collective-permute-done | bytes 524320 | tf_op jit(solution)/shard_map/ppermute | solution.py:369
  100.1 3.1 collective-permute-start.14
  103.3 10.7 %collective-permute-done.15.refs_1_.refs_0_ = bf16[128,2048]{1,0:T(8,128)(2,1)S(1)} collective-permute-done((bf16[128,2048]{1,0:T(8,128)(2,1)}, bf16[128,2048]{1,0:T(8,128)(2,1)S(1)}, u32[]{:S(2)}, u32[]{:S(2)}) %collective-permute-start.15) | collective-permute-done | bytes 524320 | tf_op jit(solution)/shard_map/ppermute | solution.py:369
  113.9 1.2 collective-permute-start.9
  115.1 1.1 copy-done.24
  117.2 2.1 first_choice.7
  122.6 12.0 %collective-permute-done.9.refs_6_.refs_1_ = bf16[96,4096]{1,0:T(8,128)(2,1)} collective-permute-done((bf16[96,4096]{1,0:T(8,128)(2,1)S(1)}, bf16[96,4096]{1,0:T(8,128)(2,1)}, u32[]{:S(2)}, u32[]{:S(2)}) %collective-permute-start.9) | collective-permute-done | bytes 786464 | tf_op jit(solution)/shard_map/ppermute | solution.py:369
  134.5 1.1 collective-permute-start.16
  135.7 13.7 %collective-permute-done.10.refs_7_.refs_1_ = bf16[96,4096]{1,0:T(8,128)(2,1)} collective-permute-done((bf16[96,4096]{1,0:T(8,128)(2,1)}, bf16[96,4096]{1,0:T(8,128)(2,1)}, u32[]{:S(2)}, u32[]{:S(2)}) %collective-permute-start.10) | collective-permute-done | bytes 786464 | tf_op jit(solution)/shard_map/ppermute | solution.py:369
  149.4 1.1 collective-permute-start.20
  150.5 3.3 collective-permute-start.22
  153.8 30.5 %expert_forward.1 = (bf16[96,4096]{1,0:T(8,128)(2,1)}, bf16[96,4096]{1,0:T(8,128)(2,1)}, bf16[96,4096]{1,0:T(8,128)(2,1)}, bf16[96,4096]{1,0:T(8,128)(2,1)}, bf1...) custom-call(bf16[96,4096]{1,0:T(8,128)(2,1)} %copy-done.58, ...), custom_call_target="tpu_custom_call" | custom-call | flops 14495514624 | bytes 50331648 | tf_op jit(solution)/shard_map/expert_forward/pallas_call | solution.py:225
  184.3 1.6 collective-permute-start.17
  189.3 12.7 %collective-permute-done.21.refs_0_.refs_1_ = bf16[128,2048]{1,0:T(8,128)(2,1)S(1)} collective-permute-done((bf16[128,2048]{1,0:T(8,128)(2,1)}, bf16[128,2048]{1,0:T(8,128)(2,1)S(1)}, u32[]{:S(2)}, u32[]{:S(2)}) %collective-permute-start.21) | collective-permute-done | bytes 524320 | tf_op jit(solution)/shard_map/ppermute | solution.py:369
  202.0 13.7 %collective-permute-done.23.refs_1_ = bf16[128,2048]{1,0:T(8,128)(2,1)S(1)} collective-permute-done((bf16[128,2048]{1,0:T(8,128)(2,1)}, bf16[128,2048]{1,0:T(8,128)(2,1)S(1)}, u32[]{:S(2)}, u32[]{:S(2)}) %collective-permute-start.23) | collective-permute-done | bytes 524320 | tf_op jit(solution)/shard_map/ppermute | solution.py:369
  216.6 1.4 next_choice.6
  220.3 1.5 collective-permute-start.18
  222.3 1.1 copy-done.5
  226.6 13.1 %collective-permute-done.24.refs_1_.refs_7_ = bf16[96,4096]{1,0:T(8,128)(2,1)} collective-permute-done((bf16[96,4096]{1,0:T(8,128)(2,1)}, bf16[96,4096]{1,0:T(8,128)(2,1)}, u32[]{:S(2)}, u32[]{:S(2)}) %collective-permute-start.24) | collective-permute-done | bytes 786464 | tf_op jit(solution)/shard_map/ppermute | solution.py:369
  240.2 15.3 %collective-permute-done.18.refs_1_.refs_16_ = bf16[96,4096]{1,0:T(8,128)(2,1)S(1)} collective-permute-done((bf16[96,4096]{1,0:T(8,128)(2,1)}, bf16[96,4096]{1,0:T(8,128)(2,1)S(1)}, u32[]{:S(2)}, u32[]{:S(2)}) %collective-permute-start.18) | collective-permute-done | bytes 786464 | tf_op jit(solution)/shard_map/ppermute | solution.py:369
  256.4 1.4 collective-permute-start.19
  257.9 1.1 copy-done.9
  259.0 2.6 back_sum.17
  261.6 2.6 back_sum.20
  264.3 7.6 %collective-permute-done.32.refs_6_ = bf16[96,4096]{1,0:T(8,128)(2,1)} collective-permute-done((bf16[96,4096]{1,0:T(8,128)(2,1)}, bf16[96,4096]{1,0:T(8,128)(2,1)}, u32[]{:S(2)}, u32[]{:S(2)}) %collective-permute-start.32) | collective-permute-done | bytes 786464 | tf_op jit(solution)/shard_map/ppermute | solution.py:369
  271.8 30.3 %expert_backward.1 = (bf16[96,4096]{1,0:T(8,128)(2,1)}, bf16[96,4096]{1,0:T(8,128)(2,1)}, bf16[96,4096]{1,0:T(8,128)(2,1)}, bf16[96,4096]{1,0:T(8,128)(2,1)}, bf...) custom-call(bf16[96,4096]{1,0:T(8,128)(2,1)} %copy-done.47, ...), custom_call_target="tpu_custom_call" | custom-call | flops 14495514624 | bytes 50331648 | tf_op jit(solution)/shard_map/expert_backward/pallas_call | solution.py:225
  303.1 1.5 collective-permute-start.35
  304.5 1.1 copy-done.11
  305.7 2.7 back_sum.21
  308.4 2.7 back_sum.18
  312.5 10.4 %collective-permute-done.35.refs_1_ = bf16[96,4096]{1,0:T(8,128)(2,1)S(1)} collective-permute-done((bf16[96,4096]{1,0:T(8,128)(2,1)}, bf16[96,4096]{1,0:T(8,128)(2,1)S(1)}, u32[]{:S(2)}, u32[]{:S(2)}) %collective-permute-start.35) | collective-permute-done | bytes 786464 | tf_op jit(solution)/shard_map/ppermute | solution.py:369
  325.6 7.9 %collective-permute-done.28.refs_2_.refs_1_ = bf16[128,2048]{1,0:T(8,128)(2,1)} collective-permute-done((bf16[128,2048]{1,0:T(8,128)(2,1)}, bf16[128,2048]{1,0:T(8,128)(2,1)}, u32[]{:S(2)}, u32[]{:S(2)}) %collective-permute-start.28) | collective-permute-done | bytes 524320 | tf_op jit(solution)/shard_map/ppermute | solution.py:369
  333.5 1.3 collective-permute-start.37
  335.9 4.5 %collective-permute-done.40.refs_2_ = bf16[128,2048]{1,0:T(8,128)(2,1)} collective-permute-done((bf16[128,2048]{1,0:T(8,128)(2,1)}, bf16[128,2048]{1,0:T(8,128)(2,1)}, u32[]{:S(2)}, u32[]{:S(2)}) %collective-permute-start.40) | collective-permute-done | bytes 524320 | tf_op jit(solution)/shard_map/ppermute | solution.py:369
  340.3 2.3 back_sum.28
  342.8 3.1 collective-permute-done.37.refs_2_
  345.9 2.4 back_sum.25
  349.4 2.7 collective-permute-done.41.refs_2_
  352.2 1.7 back_sum.29
  353.9 1.1 collective-permute-start.42
  355.0 2.7 collective-permute-done.38.refs_2_
  357.7 1.5 back_sum.26
  359.2 1.1 collective-permute-start.39
  360.2 2.6 back_sum.22.refs_3_
  362.9 2.7 back_sum.23
  365.6 1.3 back_sum.30.refs_3_
  366.8 2.1 collective-permute-done.39.refs_2_
  368.9 1.3 back_sum.31
  (206 shorter events, 33.4 us)
Async XLA Ops:
  0.6 149.9 %collective-permute-start.11 = (bf16[4096,768]{1,0:T(8,128)(2,1)}, bf16[4096,768]{1,0:T(8,128)(2,1)}, u32[]{:S(2)}, u32[]{:S(2)}) collective-permute-start(bf16[4096,768]{1,0:T(8,128)(2,1)} %bitcast.9), channel_id=1, source_target_pairs={{0,1},{1,0},{2,3},{3,2},{4,5},{5,4},{6,7},{7,6},{8,9},{9,8},{10,11... | collective-permute-start | bytes 18874376 | tf_op jit(solution)/shard_map/ppermute | solution.py:369
  1.1 152.6 %collective-permute-start.12 = (bf16[4096,768]{1,0:T(8,128)(2,1)}, bf16[4096,768]{1,0:T(8,128)(2,1)}, u32[]{:S(2)}, u32[]{:S(2)}) collective-permute-start(bf16[4096,768]{1,0:T(8,128)(2,1)} %bitcast.12), channel_id=1, source_target_pairs={{0,1},{1,0},{2,3},{3,2},{4,5},{5,4},{6,7},{7,6},{8,9},{9,8},{10,11... | collective-permute-start | bytes 18874376 | tf_op jit(solution)/shard_map/ppermute | solution.py:369
  1.2 152.5 %collective-permute-start.13 = (bf16[768,4096]{1,0:T(8,128)(2,1)}, bf16[768,4096]{1,0:T(8,128)(2,1)}, u32[]{:S(2)}, u32[]{:S(2)}) collective-permute-start(bf16[768,4096]{1,0:T(8,128)(2,1)} %bitcast.15), channel_id=1, source_target_pairs={{0,1},{1,0},{2,3},{3,2},{4,5},{5,4},{6,7},{7,6},{8,9},{9,8},{10,11... | collective-permute-start | bytes 18874376 | tf_op jit(solution)/shard_map/ppermute | solution.py:369
  2.9 16.2 %collective-permute-start.1 = (bf16[128,2048]{1,0:T(8,128)(2,1)S(1)}, bf16[128,2048]{1,0:T(8,128)(2,1)S(1)}, u32[]{:S(2)}, u32[]{:S(2)}) collective-permute-start(bf16[128,2048]{1,0:T(8,128)(2,1)S(1)} %get-tuple-element.88.refs_1_), channel_id=1, source_target_pairs={{0,4},{1,5},{2,6},{3,7},{4,12},{5,13},{6,14},{7,15},{8,0},{9,1},{1... | collective-permute-start | bytes 1572872 | tf_op jit(solution)/shard_map/ppermute | solution.py:369
  5.6 14.4 %copy-start.63 = (bf16[128,4096]{1,0:T(8,128)(2,1)S(1)}, bf16[128,4096]{1,0:T(8,128)(2,1)}, u32[]{:S(2)}) copy-start(bf16[128,4096]{1,0:T(8,128)(2,1)} %param.8) | copy-start | bytes 3145732
  8.5 11.6 %copy-start.58 = (bf16[96,4096]{1,0:T(8,128)(2,1)}, bf16[96,4096]{1,0:T(8,128)(2,1)S(1)}, u32[]{:S(2)}) copy-start(bf16[96,4096]{1,0:T(8,128)(2,1)S(1)} %get-tuple-element.45.refs_0_) | copy-start | bytes 2359300
  8.5 29.7 %collective-permute-start.3 = (bf16[96,4096]{1,0:T(8,128)(2,1)S(1)}, bf16[96,4096]{1,0:T(8,128)(2,1)}, u32[]{:S(2)}, u32[]{:S(2)}) collective-permute-start(bf16[96,4096]{1,0:T(8,128)(2,1)S(1)} %get-tuple-element.49), channel_id=1, source_target_pairs={{0,2},{1,3},{2,0},{3,1},{4,6},{5,7},{6,4},{7,5},{8,10},{9,11},{10,... | collective-permute-start | bytes 2359304 | tf_op jit(solution)/shard_map/ppermute | solution.py:369
  19.2 18.3 %copy-start.31 = (bf16[128,2048]{1,0:T(8,128)(2,1)}, bf16[128,2048]{1,0:T(8,128)(2,1)S(1)}, u32[]{:S(2)}) copy-start(bf16[128,2048]{1,0:T(8,128)(2,1)S(1)} %collective-permute-done.1.refs_1_.refs_0_) | copy-start | bytes 1572868
  19.2 15.3 %collective-permute-start = (bf16[128,2176]{1,0:T(8,128)(2,1)S(1)}, bf16[128,2176]{1,0:T(8,128)(2,1)S(1)}, u32[]{:S(2)}, u32[]{:S(2)}) collective-permute-start(bf16[128,2176]{1,0:T(8,128)(2,1)S(1)} %fusion.1.refs_0_), channel_id=1, source_target_pairs={{0,4},{1,5},{2,6},{3,7},{4,12},{5,13},{6,14},{7,15},{8,0},{9,1},{1... | collective-permute-start | bytes 1671176 | tf_op jit(solution)/shard_map/ppermute | solution.py:369
  20.1 18.1 %copy-start.1 = (bf16[128,2048]{1,0:T(8,128)(2,1)}, bf16[128,2048]{1,0:T(8,128)(2,1)S(1)}, u32[]{:S(2)}) copy-start(bf16[128,2048]{1,0:T(8,128)(2,1)S(1)} %get-tuple-element.86.refs_1_.refs_0_) | copy-start | bytes 1572868
  20.1 18.1 %copy-start.13 = (bf16[128,2048]{1,0:T(8,128)(2,1)}, bf16[128,2048]{1,0:T(8,128)(2,1)S(1)}, u32[]{:S(2)}) copy-start(bf16[128,2048]{1,0:T(8,128)(2,1)S(1)} %get-tuple-element.87.refs_0_) | copy-start | bytes 1572868
  37.4 83.7 %copy-start.43 = (f32[192,128]{1,0:T(8,128)}, f32[192,128]{1,0:T(8,128)S(1)}, u32[]{:S(2)}) copy-start(f32[192,128]{1,0:T(8,128)S(1)} %get-tuple-element.61.gated.mix) | copy-start | bytes 294916
  37.4 83.7 %copy-start.52 = (bf16[192,128]{1,0:T(8,128)(2,1)}, bf16[192,128]{1,0:T(8,128)(2,1)S(1)}, u32[]{:S(2)}) copy-start(bf16[192,128]{1,0:T(8,128)(2,1)S(1)} %get-tuple-element.60.pick.mix) | copy-start | bytes 147460
  37.4 16.7 %collective-permute-start.2 = (bf16[128,2176]{1,0:T(8,128)(2,1)}, bf16[128,2176]{1,0:T(8,128)(2,1)S(1)}, u32[]{:S(2)}, u32[]{:S(2)}) collective-permute-start(bf16[128,2176]{1,0:T(8,128)(2,1)} %tie.23), channel_id=1, source_target_pairs={{0,4},{1,5},{2,6},{3,7},{4,12},{5,13},{6,14},{7,15},{8,0},{9,1},{1... | collective-permute-start | bytes 1671176 | tf_op jit(solution)/shard_map/ppermute | solution.py:369
  38.2 25.2 %collective-permute-start.4 = (bf16[128,2048]{1,0:T(8,128)(2,1)}, bf16[128,2048]{1,0:T(8,128)(2,1)S(1)}, u32[]{:S(2)}, u32[]{:S(2)}) collective-permute-start(bf16[128,2048]{1,0:T(8,128)(2,1)} %tie.24), channel_id=1, source_target_pairs={{0,4},{1,5},{2,6},{3,7},{4,12},{5,13},{6,14},{7,15},{8,0},{9,1},{1... | collective-permute-start | bytes 1572872 | tf_op jit(solution)/shard_map/ppermute | solution.py:369
  54.2 13.1 %copy-start.25 = (bf16[128,2176]{1,0:T(8,128)(2,1)}, bf16[128,2176]{1,0:T(8,128)(2,1)S(1)}, u32[]{:S(2)}) copy-start(bf16[128,2176]{1,0:T(8,128)(2,1)S(1)} %collective-permute-done.2.refs_0_) | copy-start | bytes 1671172
  54.2 20.8 %collective-permute-start.6 = (bf16[96,4096]{1,0:T(8,128)(2,1)}, bf16[96,4096]{1,0:T(8,128)(2,1)}, u32[]{:S(2)}, u32[]{:S(2)}) collective-permute-start(bf16[96,4096]{1,0:T(8,128)(2,1)} %get-tuple-element.51), channel_id=1, source_target_pairs={{0,2},{1,3},{2,0},{3,1},{4,6},{5,7},{6,4},{7,5},{8,10},{9,11},{10,... | collective-permute-start | bytes 2359304 | tf_op jit(solution)/shard_map/ppermute | solution.py:369
  63.4 12.4 %copy-start.34 = (bf16[128,2048]{1,0:T(8,128)(2,1)}, bf16[128,2048]{1,0:T(8,128)(2,1)S(1)}, u32[]{:S(2)}) copy-start(bf16[128,2048]{1,0:T(8,128)(2,1)S(1)} %collective-permute-done.4.refs_1_.refs_0_) | copy-start | bytes 1572868
  63.4 23.4 %collective-permute-start.8 = (bf16[96,4096]{1,0:T(8,128)(2,1)}, bf16[96,4096]{1,0:T(8,128)(2,1)}, u32[]{:S(2)}, u32[]{:S(2)}) collective-permute-start(bf16[96,4096]{1,0:T(8,128)(2,1)} %get-tuple-element.53), channel_id=1, source_target_pairs={{0,2},{1,3},{2,0},{3,1},{4,6},{5,7},{6,4},{7,5},{8,10},{9,11},{10,... | collective-permute-start | bytes 2359304 | tf_op jit(solution)/shard_map/ppermute | solution.py:369
  67.3 118.6 %copy-start.45 = (f32[192,128]{1,0:T(8,128)}, f32[192,128]{1,0:T(8,128)S(1)}, u32[]{:S(2)}) copy-start(f32[192,128]{1,0:T(8,128)S(1)} %get-tuple-element.68.mix.gated) | copy-start | bytes 294916
  75.0 24.4 %collective-permute-start.5 = (bf16[128,2176]{1,0:T(8,128)(2,1)}, bf16[128,2176]{1,0:T(8,128)(2,1)S(1)}, u32[]{:S(2)}, u32[]{:S(2)}) collective-permute-start(bf16[128,2176]{1,0:T(8,128)(2,1)} %tie.25), channel_id=1, source_target_pairs={{0,4},{1,5},{2,6},{3,7},{4,12},{5,13},{6,14},{7,15},{8,0},{9,1},{1... | collective-permute-start | bytes 1671176 | tf_op jit(solution)/shard_map/ppermute | solution.py:369
  86.8 11.8 %collective-permute-start.7 = (bf16[128,2048]{1,0:T(8,128)(2,1)}, bf16[128,2048]{1,0:T(8,128)(2,1)S(1)}, u32[]{:S(2)}, u32[]{:S(2)}) collective-permute-start(bf16[128,2048]{1,0:T(8,128)(2,1)} %tie.26), channel_id=1, source_target_pairs={{0,4},{1,5},{2,6},{3,7},{4,12},{5,13},{6,14},{7,15},{8,0},{9,1},{1... | collective-permute-start | bytes 1572872 | tf_op jit(solution)/shard_map/ppermute | solution.py:369
  99.3 14.6 %collective-permute-start.15 = (bf16[128,2048]{1,0:T(8,128)(2,1)}, bf16[128,2048]{1,0:T(8,128)(2,1)S(1)}, u32[]{:S(2)}, u32[]{:S(2)}) collective-permute-start(bf16[128,2048]{1,0:T(8,128)(2,1)} %tie.29), channel_id=1, source_target_pairs={{0,4},{1,5},{2,6},{3,7},{4,12},{5,13},{6,14},{7,15},{8,0},{9,1},{1... | collective-permute-start | bytes 1572872 | tf_op jit(solution)/shard_map/ppermute | solution.py:369
  100.1 20.1 %collective-permute-start.14 = (bf16[128,2048]{1,0:T(8,128)(2,1)}, bf16[128,2048]{1,0:T(8,128)(2,1)S(1)}, u32[]{:S(2)}, u32[]{:S(2)}) collective-permute-start(bf16[128,2048]{1,0:T(8,128)(2,1)} %tie.27), channel_id=1, source_target_pairs={{0,4},{1,5},{2,6},{3,7},{4,12},{5,13},{6,14},{7,15},{8,0},{9,1},{1... | collective-permute-start | bytes 1572872 | tf_op jit(solution)/shard_map/ppermute | solution.py:369
  113.9 21.7 %copy-start.29 = (bf16[128,2048]{1,0:T(8,128)(2,1)}, bf16[128,2048]{1,0:T(8,128)(2,1)S(1)}, u32[]{:S(2)}) copy-start(bf16[128,2048]{1,0:T(8,128)(2,1)S(1)} %collective-permute-done.15.refs_1_.refs_0_) | copy-start | bytes 1572868
  113.9 20.6 %collective-permute-start.9 = (bf16[96,4096]{1,0:T(8,128)(2,1)S(1)}, bf16[96,4096]{1,0:T(8,128)(2,1)}, u32[]{:S(2)}, u32[]{:S(2)}) collective-permute-start(bf16[96,4096]{1,0:T(8,128)(2,1)S(1)} %get-tuple-element.54), channel_id=1, source_target_pairs={{0,2},{1,3},{2,0},{3,1},{4,6},{5,7},{6,4},{7,5},{8,10},{9,11},{10,... | collective-permute-start | bytes 2359304 | tf_op jit(solution)/shard_map/ppermute | solution.py:369
  120.2 29.2 %collective-permute-start.10 = (bf16[96,4096]{1,0:T(8,128)(2,1)}, bf16[96,4096]{1,0:T(8,128)(2,1)}, u32[]{:S(2)}, u32[]{:S(2)}) collective-permute-start(bf16[96,4096]{1,0:T(8,128)(2,1)} %get-tuple-element.55), channel_id=1, source_target_pairs={{0,2},{1,3},{2,0},{3,1},{4,6},{5,7},{6,4},{7,5},{8,10},{9,11},{10,... | collective-permute-start | bytes 2359304 | tf_op jit(solution)/shard_map/ppermute | solution.py:369
  134.5 49.7 %collective-permute-start.16 = (bf16[96,4096]{1,0:T(8,128)(2,1)S(1)}, bf16[96,4096]{1,0:T(8,128)(2,1)}, u32[]{:S(2)}, u32[]{:S(2)}) collective-permute-start(bf16[96,4096]{1,0:T(8,128)(2,1)S(1)} %get-tuple-element.62), channel_id=1, source_target_pairs={{0,2},{1,3},{2,0},{3,1},{4,6},{5,7},{6,4},{7,5},{8,10},{9,11},{10,... | collective-permute-start | bytes 2359304 | tf_op jit(solution)/shard_map/ppermute | solution.py:369
  149.4 36.5 %collective-permute-start.20 = (bf16[128,2048]{1,0:T(8,128)(2,1)}, bf16[128,2048]{1,0:T(8,128)(2,1)S(1)}, u32[]{:S(2)}, u32[]{:S(2)}) collective-permute-start(bf16[128,2048]{1,0:T(8,128)(2,1)} %tie.33), channel_id=1, source_target_pairs={{0,4},{1,5},{2,6},{3,7},{4,12},{5,13},{6,14},{7,15},{8,0},{9,1},{1... | collective-permute-start | bytes 1572872 | tf_op jit(solution)/shard_map/ppermute | solution.py:369
  150.5 35.4 %collective-permute-start.22 = (bf16[128,2048]{1,0:T(8,128)(2,1)}, bf16[128,2048]{1,0:T(8,128)(2,1)S(1)}, u32[]{:S(2)}, u32[]{:S(2)}) collective-permute-start(bf16[128,2048]{1,0:T(8,128)(2,1)} %tie.35), channel_id=1, source_target_pairs={{0,4},{1,5},{2,6},{3,7},{4,12},{5,13},{6,14},{7,15},{8,0},{9,1},{1... | collective-permute-start | bytes 1572872 | tf_op jit(solution)/shard_map/ppermute | solution.py:369
  184.3 35.1 %collective-permute-start.17 = (bf16[96,4096]{1,0:T(8,128)(2,1)}, bf16[96,4096]{1,0:T(8,128)(2,1)S(1)}, u32[]{:S(2)}, u32[]{:S(2)}) collective-permute-start(bf16[96,4096]{1,0:T(8,128)(2,1)} %tie.30), channel_id=1, source_target_pairs={{0,2},{1,3},{2,0},{3,1},{4,6},{5,7},{6,4},{7,5},{8,10},{9,11},{10,... | collective-permute-start | bytes 2359304 | tf_op jit(solution)/shard_map/ppermute | solution.py:369
  188.5 27.2 %copy-start = (bf16[96,4096]{1,0:T(8,128)(2,1)S(1)}, bf16[96,4096]{1,0:T(8,128)(2,1)}, u32[]{:S(2)}) copy-start(bf16[96,4096]{1,0:T(8,128)(2,1)} %get-tuple-element.56.refs_2_.refs_0_) | copy-start | bytes 2359300
  188.5 13.5 %collective-permute-start.21 = (bf16[128,2048]{1,0:T(8,128)(2,1)}, bf16[128,2048]{1,0:T(8,128)(2,1)S(1)}, u32[]{:S(2)}, u32[]{:S(2)}) collective-permute-start(bf16[128,2048]{1,0:T(8,128)(2,1)} %tie.34), channel_id=1, source_target_pairs={{0,4},{1,5},{2,6},{3,7},{4,12},{5,13},{6,14},{7,15},{8,0},{9,1},{1... | collective-permute-start | bytes 1572872 | tf_op jit(solution)/shard_map/ppermute | solution.py:369
  188.5 33.8 %copy-start.16 = (bf16[96,4096]{1,0:T(8,128)(2,1)S(1)}, bf16[96,4096]{1,0:T(8,128)(2,1)}, u32[]{:S(2)}) copy-start(bf16[96,4096]{1,0:T(8,128)(2,1)} %get-tuple-element.70.refs_0_) | copy-start | bytes 2359300
  188.5 27.2 %collective-permute-start.23 = (bf16[128,2048]{1,0:T(8,128)(2,1)}, bf16[128,2048]{1,0:T(8,128)(2,1)S(1)}, u32[]{:S(2)}, u32[]{:S(2)}) collective-permute-start(bf16[128,2048]{1,0:T(8,128)(2,1)} %tie.36), channel_id=1, source_target_pairs={{0,4},{1,5},{2,6},{3,7},{4,12},{5,13},{6,14},{7,15},{8,0},{9,1},{1... | collective-permute-start | bytes 1572872 | tf_op jit(solution)/shard_map/ppermute | solution.py:369
  202.0 20.3 %copy-start.35 = (bf16[128,2048]{1,0:T(8,128)(2,1)}, bf16[128,2048]{1,0:T(8,128)(2,1)S(1)}, u32[]{:S(2)}) copy-start(bf16[128,2048]{1,0:T(8,128)(2,1)S(1)} %collective-permute-done.21.refs_0_.refs_1_) | copy-start | bytes 1572868
  218.9 20.8 %collective-permute-start.24 = (bf16[96,4096]{1,0:T(8,128)(2,1)}, bf16[96,4096]{1,0:T(8,128)(2,1)}, u32[]{:S(2)}, u32[]{:S(2)}) collective-permute-start(bf16[96,4096]{1,0:T(8,128)(2,1)} %get-tuple-element.67), channel_id=1, source_target_pairs={{0,2},{1,3},{2,0},{3,1},{4,6},{5,7},{6,4},{7,5},{8,10},{9,11},{10,... | collective-permute-start | bytes 2359304 | tf_op jit(solution)/shard_map/ppermute | solution.py:369
  220.3 35.2 %collective-permute-start.18 = (bf16[96,4096]{1,0:T(8,128)(2,1)}, bf16[96,4096]{1,0:T(8,128)(2,1)S(1)}, u32[]{:S(2)}, u32[]{:S(2)}) collective-permute-start(bf16[96,4096]{1,0:T(8,128)(2,1)} %tie.31), channel_id=1, source_target_pairs={{0,2},{1,3},{2,0},{3,1},{4,6},{5,7},{6,4},{7,5},{8,10},{9,11},{10,... | collective-permute-start | bytes 2359304 | tf_op jit(solution)/shard_map/ppermute | solution.py:369
  221.8 50.0 %collective-permute-start.32 = (bf16[96,4096]{1,0:T(8,128)(2,1)}, bf16[96,4096]{1,0:T(8,128)(2,1)}, u32[]{:S(2)}, u32[]{:S(2)}) collective-permute-start(bf16[96,4096]{1,0:T(8,128)(2,1)} %copy-done.61), channel_id=1, source_target_pairs={{0,2},{1,3},{2,0},{3,1},{4,6},{5,7},{6,4},{7,5},{8,10},{9,11},{10,... | collective-permute-start | bytes 2359304 | tf_op jit(solution)/shard_map/ppermute | solution.py:369
  225.0 32.8 %collective-permute-start.26 = (bf16[128,2048]{1,0:T(8,128)(2,1)}, bf16[128,2048]{1,0:T(8,128)(2,1)}, u32[]{:S(2)}, u32[]{:S(2)}) collective-permute-start(bf16[128,2048]{1,0:T(8,128)(2,1)} %tie.38), channel_id=1, source_target_pairs={{0,8},{1,9},{2,10},{3,11},{4,0},{5,1},{6,2},{7,3},{8,12},{9,13},{1... | collective-permute-start | bytes 1572872 | tf_op jit(solution)/shard_map/ppermute | solution.py:369
  226.6 35.1 %collective-permute-start.29 = (bf16[128,2048]{1,0:T(8,128)(2,1)}, bf16[128,2048]{1,0:T(8,128)(2,1)}, u32[]{:S(2)}, u32[]{:S(2)}) collective-permute-start(bf16[128,2048]{1,0:T(8,128)(2,1)} %tie.39), channel_id=1, source_target_pairs={{0,8},{1,9},{2,10},{3,11},{4,0},{5,1},{6,2},{7,3},{8,12},{9,13},{1... | collective-permute-start | bytes 1572872 | tf_op jit(solution)/shard_map/ppermute | solution.py:369
  239.7 18.1 %copy-start.20 = (bf16[96,4096]{1,0:T(8,128)(2,1)S(1)}, bf16[96,4096]{1,0:T(8,128)(2,1)}, u32[]{:S(2)}) copy-start(bf16[96,4096]{1,0:T(8,128)(2,1)} %get-tuple-element.69.refs_0_) | copy-start | bytes 2359300
  239.7 18.1 %copy-start.46 = (f32[192,128]{1,0:T(8,128)S(1)}, f32[192,128]{1,0:T(8,128)}, u32[]{:S(2)}) copy-start(f32[192,128]{1,0:T(8,128)} %copy-done.45) | copy-start | bytes 294916
  239.7 62.5 %collective-permute-start.25 = (bf16[96,4096]{1,0:T(8,128)(2,1)}, bf16[96,4096]{1,0:T(8,128)(2,1)S(1)}, u32[]{:S(2)}, u32[]{:S(2)}) collective-permute-start(bf16[96,4096]{1,0:T(8,128)(2,1)} %tie.37), channel_id=1, source_target_pairs={{0,2},{1,3},{2,0},{3,1},{4,6},{5,7},{6,4},{7,5},{8,10},{9,11},{10,... | collective-permute-start | bytes 2359304 | tf_op jit(solution)/shard_map/ppermute | solution.py:369
  256.4 54.7 %collective-permute-start.19 = (bf16[96,4096]{1,0:T(8,128)(2,1)}, bf16[96,4096]{1,0:T(8,128)(2,1)S(1)}, u32[]{:S(2)}, u32[]{:S(2)}) collective-permute-start(bf16[96,4096]{1,0:T(8,128)(2,1)} %tie.32), channel_id=1, source_target_pairs={{0,2},{1,3},{2,0},{3,1},{4,6},{5,7},{6,4},{7,5},{8,10},{9,11},{10,... | collective-permute-start | bytes 2359304 | tf_op jit(solution)/shard_map/ppermute | solution.py:369
  261.6 46.7 %collective-permute-start.27 = (bf16[128,2048]{1,0:T(8,128)(2,1)}, bf16[128,2048]{1,0:T(8,128)(2,1)}, u32[]{:S(2)}, u32[]{:S(2)}) collective-permute-start(bf16[128,2048]{1,0:T(8,128)(2,1)} %back_sum.17), channel_id=1, source_target_pairs={{0,8},{1,9},{2,10},{3,11},{4,0},{5,1},{6,2},{7,3},{8,12},{9,13},{1... | collective-permute-start | bytes 1572872 | tf_op jit(solution)/shard_map/ppermute | solution.py:369
  264.3 40.3 %collective-permute-start.30 = (bf16[128,2048]{1,0:T(8,128)(2,1)}, bf16[128,2048]{1,0:T(8,128)(2,1)}, u32[]{:S(2)}, u32[]{:S(2)}) collective-permute-start(bf16[128,2048]{1,0:T(8,128)(2,1)} %back_sum.20), channel_id=1, source_target_pairs={{0,8},{1,9},{2,10},{3,11},{4,0},{5,1},{6,2},{7,3},{8,12},{9,13},{1... | collective-permute-start | bytes 1572872 | tf_op jit(solution)/shard_map/ppermute | solution.py:369
  303.1 19.9 %collective-permute-start.35 = (bf16[96,4096]{1,0:T(8,128)(2,1)}, bf16[96,4096]{1,0:T(8,128)(2,1)S(1)}, u32[]{:S(2)}, u32[]{:S(2)}) collective-permute-start(bf16[96,4096]{1,0:T(8,128)(2,1)} %tie.42), channel_id=1, source_target_pairs={{0,2},{1,3},{2,0},{3,1},{4,6},{5,7},{6,4},{7,5},{8,10},{9,11},{10,... | collective-permute-start | bytes 2359304 | tf_op jit(solution)/shard_map/ppermute | solution.py:369
  308.3 14.6 %copy-start.17 = (bf16[96,4096]{1,0:T(8,128)(2,1)S(1)}, bf16[96,4096]{1,0:T(8,128)(2,1)}, u32[]{:S(2)}) copy-start(bf16[96,4096]{1,0:T(8,128)(2,1)} %get-tuple-element.85.refs_0_) | copy-start | bytes 2359300
  308.3 14.6 %copy-start.51 = (bf16[192,128]{1,0:T(8,128)(2,1)S(1)}, bf16[192,128]{1,0:T(8,128)(2,1)}, u32[]{:S(2)}) copy-start(bf16[192,128]{1,0:T(8,128)(2,1)} %copy-done.49) | copy-start | bytes 147460
  308.3 15.9 %collective-permute-start.31 = (bf16[128,2048]{1,0:T(8,128)(2,1)}, bf16[128,2048]{1,0:T(8,128)(2,1)}, u32[]{:S(2)}, u32[]{:S(2)}) collective-permute-start(bf16[128,2048]{1,0:T(8,128)(2,1)} %back_sum.21), channel_id=1, source_target_pairs={{0,8},{1,9},{2,10},{3,11},{4,0},{5,1},{6,2},{7,3},{8,12},{9,13},{1... | collective-permute-start | bytes 1572872 | tf_op jit(solution)/shard_map/ppermute | solution.py:369
  311.0 22.5 %collective-permute-start.28 = (bf16[128,2048]{1,0:T(8,128)(2,1)}, bf16[128,2048]{1,0:T(8,128)(2,1)}, u32[]{:S(2)}, u32[]{:S(2)}) collective-permute-start(bf16[128,2048]{1,0:T(8,128)(2,1)} %back_sum.18), channel_id=1, source_target_pairs={{0,8},{1,9},{2,10},{3,11},{4,0},{5,1},{6,2},{7,3},{8,12},{9,13},{1... | collective-permute-start | bytes 1572872 | tf_op jit(solution)/shard_map/ppermute | solution.py:369
  311.9 23.9 %collective-permute-start.33 = (bf16[96,4096]{1,0:T(8,128)(2,1)}, bf16[96,4096]{1,0:T(8,128)(2,1)S(1)}, u32[]{:S(2)}, u32[]{:S(2)}) collective-permute-start(bf16[96,4096]{1,0:T(8,128)(2,1)} %tie.40), channel_id=1, source_target_pairs={{0,2},{1,3},{2,0},{3,1},{4,6},{5,7},{6,4},{7,5},{8,10},{9,11},{10,... | collective-permute-start | bytes 2359304 | tf_op jit(solution)/shard_map/ppermute | solution.py:369
  324.2 16.1 %collective-permute-start.40 = (bf16[128,2048]{1,0:T(8,128)(2,1)}, bf16[128,2048]{1,0:T(8,128)(2,1)}, u32[]{:S(2)}, u32[]{:S(2)}) collective-permute-start(bf16[128,2048]{1,0:T(8,128)(2,1)} %tie.45), channel_id=1, source_target_pairs={{0,8},{1,9},{2,10},{3,11},{4,0},{5,1},{6,2},{7,3},{8,12},{9,13},{1... | collective-permute-start | bytes 1572872 | tf_op jit(solution)/shard_map/ppermute | solution.py:369
  325.6 14.7 %copy-start.22 = (bf16[96,4096]{1,0:T(8,128)(2,1)S(1)}, bf16[96,4096]{1,0:T(8,128)(2,1)}, u32[]{:S(2)}) copy-start(bf16[96,4096]{1,0:T(8,128)(2,1)} %get-tuple-element.84.refs_0_) | copy-start | bytes 2359300
  325.6 14.7 %copy-start.56 = (bf16[192,128]{1,0:T(8,128)(2,1)S(1)}, bf16[192,128]{1,0:T(8,128)(2,1)}, u32[]{:S(2)}) copy-start(bf16[192,128]{1,0:T(8,128)(2,1)} %copy-done.54) | copy-start | bytes 147460
  333.5 12.4 %collective-permute-start.37 = (bf16[128,2048]{1,0:T(8,128)(2,1)}, bf16[128,2048]{1,0:T(8,128)(2,1)}, u32[]{:S(2)}, u32[]{:S(2)}) collective-permute-start(bf16[128,2048]{1,0:T(8,128)(2,1)} %tie.44), channel_id=1, source_target_pairs={{0,8},{1,9},{2,10},{3,11},{4,0},{5,1},{6,2},{7,3},{8,12},{9,13},{1... | collective-permute-start | bytes 1572872 | tf_op jit(solution)/shard_map/ppermute | solution.py:369
  334.8 14.6 %collective-permute-start.36 = (bf16[96,4096]{1,0:T(8,128)(2,1)}, bf16[96,4096]{1,0:T(8,128)(2,1)}, u32[]{:S(2)}, u32[]{:S(2)}) collective-permute-start(bf16[96,4096]{1,0:T(8,128)(2,1)} %tie.43), channel_id=1, source_target_pairs={{0,2},{1,3},{2,0},{3,1},{4,6},{5,7},{6,4},{7,5},{8,10},{9,11},{10,... | collective-permute-start | bytes 2359304 | tf_op jit(solution)/shard_map/ppermute | solution.py:369
  335.9 12.4 %copy-start.12 = (bf16[96,4096]{1,0:T(8,128)(2,1)}, bf16[96,4096]{1,0:T(8,128)(2,1)S(1)}, u32[]{:S(2)}) copy-start(bf16[96,4096]{1,0:T(8,128)(2,1)S(1)} %collective-permute-done.33.refs_1_) | copy-start | bytes 2359300
  342.7 9.5 %collective-permute-start.41 = (bf16[128,2048]{1,0:T(8,128)(2,1)}, bf16[128,2048]{1,0:T(8,128)(2,1)}, u32[]{:S(2)}, u32[]{:S(2)}) collective-permute-start(bf16[128,2048]{1,0:T(8,128)(2,1)} %back_sum.28), channel_id=1, source_target_pairs={{0,8},{1,9},{2,10},{3,11},{4,0},{5,1},{6,2},{7,3},{8,12},{9,13},{1... | collective-permute-start | bytes 1572872 | tf_op jit(solution)/shard_map/ppermute | solution.py:369
  348.3 9.4 %collective-permute-start.38 = (bf16[128,2048]{1,0:T(8,128)(2,1)}, bf16[128,2048]{1,0:T(8,128)(2,1)S(1)}, u32[]{:S(2)}, u32[]{:S(2)}) collective-permute-start(bf16[128,2048]{1,0:T(8,128)(2,1)} %back_sum.25), channel_id=1, source_target_pairs={{0,8},{1,9},{2,10},{3,11},{4,0},{5,1},{6,2},{7,3},{8,12},{9,13},{1... | collective-permute-start | bytes 1572872 | tf_op jit(solution)/shard_map/ppermute | solution.py:369
  348.4 17.1 %collective-permute-start.34 = (bf16[96,4096]{1,0:T(8,128)(2,1)}, bf16[96,4096]{1,0:T(8,128)(2,1)S(1)}, u32[]{:S(2)}, u32[]{:S(2)}) collective-permute-start(bf16[96,4096]{1,0:T(8,128)(2,1)} %tie.41), channel_id=1, source_target_pairs={{0,2},{1,3},{2,0},{3,1},{4,6},{5,7},{6,4},{7,5},{8,10},{9,11},{10,... | collective-permute-start | bytes 2359304 | tf_op jit(solution)/shard_map/ppermute | solution.py:369
  353.9 11.6 %collective-permute-start.42 = (bf16[128,2048]{1,0:T(8,128)(2,1)S(1)}, bf16[128,2048]{1,0:T(8,128)(2,1)S(1)}, u32[]{:S(2)}, u32[]{:S(2)}) collective-permute-start(bf16[128,2048]{1,0:T(8,128)(2,1)S(1)} %back_sum.29), channel_id=1, source_target_pairs={{0,8},{1,9},{2,10},{3,11},{4,0},{5,1},{6,2},{7,3},{8,12},{9,13},{1... | collective-permute-start | bytes 1572872 | tf_op jit(solution)/shard_map/ppermute | solution.py:369
  359.2 9.8 %collective-permute-start.39 = (bf16[128,2048]{1,0:T(8,128)(2,1)S(1)}, bf16[128,2048]{1,0:T(8,128)(2,1)S(1)}, u32[]{:S(2)}, u32[]{:S(2)}) collective-permute-start(bf16[128,2048]{1,0:T(8,128)(2,1)S(1)} %back_sum.26), channel_id=1, source_target_pairs={{0,8},{1,9},{2,10},{3,11},{4,0},{5,1},{6,2},{7,3},{8,12},{9,13},{1... | collective-permute-start | bytes 1572872 | tf_op jit(solution)/shard_map/ppermute | solution.py:369
  (43 other events, 98.5 us)

commit v3 on v2

--- a/solution.py
+++ b/solution.py
@@ -443,11 +443,12 @@
         return weight[0], permute(weight[0], twin)
 
     gate_mats, up_mats, down_mats = both(w_gate), both(w_up), both(w_down)
+    twins = [gate_mats[1], up_mats[1], down_mats[1]]
     last = zs - 1
     choose("tokens", 0)
     choose("cot", 0)
     for r in range(1, zs):
-        onward("tokens", [own["cot"][0] if r == 2 else own["tokens"][r - 2]] if r > 1 else [], [came("y", r - 2) if r > 1 else None])
+        onward("tokens", [own["cot"][0] if r == 2 else own["tokens"][r - 2]] if r > 1 else [], [came("y", r - 2), *(twins if r == 2 else [])] if r > 1 else [])
         choose("tokens", r)
     for r in range(1, zs):
         if r == last:

time: 371 us -> 357 us (0.962)
  waiting for transfers between devices: 204 us -> 184 us
  starting transfers between devices: 39.4 us -> 47.4 us
    ppermute x43, waiting for transfers between devices: 204 us -> 184 us  [permute(): return lax.ppermute(value, 'wide', perm)]
    ppermute x43, starting transfers between devices: 39.4 us -> 47.4 us  [permute(): return lax.ppermute(value, 'wide', perm)]
    unnamed x128 -> x124, local copies, waits for them, and re-layouts: 22.8 us -> 19.8 us
  transfers between devices with their start and end apart: 43 -> 43, of which waited for: 22 -> 20; matrix products, arithmetic and copies ran while one was open for 1% -> 1% of each run, Pallas kernels for 27% -> 28%
where the time goes in v3:
time: 357 us; the launch traced here: 356 us
  waiting for transfers between devices  184 us (52%)
  Pallas kernels  101 us (28%)
  starting transfers between devices  47.4 us (13%)
  local copies, waits for them, and re-layouts  21.1 us (6%)
    ppermute x43, waiting for transfers between devices, permute(): return lax.ppermute(value, 'wide', perm)  184 us
    pallas_call x2, Pallas kernels, expert_call(): pl.pallas_call(body, grid=(2, firsts + seconds), in_specs=specs, out_spec...  61.1 us
    ppermute x43, starting transfers between devices, permute(): return lax.ppermute(value, 'wide', perm)  47.4 us
    pallas_call x16, Pallas kernels, back_sum(): pl.pallas_call(body, grid=(1,), in_specs=specs, out_specs=pl.BlockSpec((r...  28.7 us
    unnamed x124, local copies, waits for them, and re-layouts  19.8 us
    pallas_call x4, Pallas kernels, first_choice(): pl.pallas_call(body, grid=(1,), in_specs=[pl.BlockSpec(memory_space=pltpu...  7.58 us
  transfers between devices with their start and end apart: 43, of which 20 were waited for; matrix products, arithmetic and copies ran while one was open for 1% of the time, Pallas kernels for 28%

profile of v3, /device:TPU:0, one launch (start us, length us, event | category | flops | bytes accessed | tf_op | source)
XLA Modules:
  0.0 356.2 jit_solution(13705102996172593571)
XLA Ops:
  1.7 1.3 fusion.6
  2.9 2.7 collective-permute-start.1
  7.2 2.1 first_choice.4
  9.3 1.5 collective-permute-start.3
  10.8 8.4 %collective-permute-done.1.refs_1_.refs_0_ = bf16[128,2048]{1,0:T(8,128)(2,1)S(1)} collective-permute-done((bf16[128,2048]{1,0:T(8,128)(2,1)S(1)}, bf16[128,2048]{1,0:T(8,128)(2,1)S(1)}, u32[]{:S(2)}, u32[]{:S(2)}) %collective-permute-start.1) | collective-permute-done | bytes 524320 | tf_op jit(solution)/shard_map/ppermute | solution.py:369
  20.1 1.5 next_choice.4
  21.6 1.0 copy-done.45
  22.6 11.9 %collective-permute-done.refs_0_ = bf16[128,2176]{1,0:T(8,128)(2,1)S(1)} collective-permute-done((bf16[128,2176]{1,0:T(8,128)(2,1)S(1)}, bf16[128,2176]{1,0:T(8,128)(2,1)S(1)}, u32[]{:S(2)}, u32[]{:S(2)}) %collective-permute-start) | collective-permute-done | bytes 557088 | tf_op jit(solution)/shard_map/ppermute | solution.py:369
  34.5 1.4 collective-permute-start.9
  35.8 1.2 first_choice.5
  38.8 3.4 collective-permute-start.7
  42.3 12.4 %collective-permute-done.2.refs_0_ = bf16[128,2176]{1,0:T(8,128)(2,1)S(1)} collective-permute-done((bf16[128,2176]{1,0:T(8,128)(2,1)}, bf16[128,2176]{1,0:T(8,128)(2,1)S(1)}, u32[]{:S(2)}, u32[]{:S(2)}) %collective-permute-start.2) | collective-permute-done | bytes 557088 | tf_op jit(solution)/shard_map/ppermute | solution.py:369
  54.7 8.7 %collective-permute-done.7.refs_1_.refs_0_ = bf16[128,2048]{1,0:T(8,128)(2,1)S(1)} collective-permute-done((bf16[128,2048]{1,0:T(8,128)(2,1)}, bf16[128,2048]{1,0:T(8,128)(2,1)S(1)}, u32[]{:S(2)}, u32[]{:S(2)}) %collective-permute-start.7) | collective-permute-done | bytes 524320 | tf_op jit(solution)/shard_map/ppermute | solution.py:369
  63.4 2.1 first_choice.6
  68.4 3.3 collective-permute-start.10
  71.7 1.5 collective-permute-start.12
  73.2 18.2 %collective-permute-done.10.refs_1_ = bf16[128,2048]{1,0:T(8,128)(2,1)S(1)} collective-permute-done((bf16[128,2048]{1,0:T(8,128)(2,1)}, bf16[128,2048]{1,0:T(8,128)(2,1)S(1)}, u32[]{:S(2)}, u32[]{:S(2)}) %collective-permute-start.10) | collective-permute-done | bytes 524320 | tf_op jit(solution)/shard_map/ppermute | solution.py:369
  91.4 2.1 first_choice.7
  95.1 1.1 collective-permute-start.13
  96.6 3.3 collective-permute-start.14
  99.9 12.4 %collective-permute-done.15.refs_1_.refs_0_ = bf16[128,2048]{1,0:T(8,128)(2,1)S(1)} collective-permute-done((bf16[128,2048]{1,0:T(8,128)(2,1)}, bf16[128,2048]{1,0:T(8,128)(2,1)S(1)}, u32[]{:S(2)}, u32[]{:S(2)}) %collective-permute-start.15) | collective-permute-done | bytes 524320 | tf_op jit(solution)/shard_map/ppermute | solution.py:369
  112.3 6.8 %collective-permute-done.14.refs_0_ = bf16[128,2048]{1,0:T(8,128)(2,1)S(1)} collective-permute-done((bf16[128,2048]{1,0:T(8,128)(2,1)}, bf16[128,2048]{1,0:T(8,128)(2,1)S(1)}, u32[]{:S(2)}, u32[]{:S(2)}) %collective-permute-start.14) | collective-permute-done | bytes 524320 | tf_op jit(solution)/shard_map/ppermute | solution.py:369
  122.1 3.3 collective-permute-start.22
  125.4 30.7 %expert_forward.1 = (bf16[96,4096]{1,0:T(8,128)(2,1)}, bf16[96,4096]{1,0:T(8,128)(2,1)}, bf16[96,4096]{1,0:T(8,128)(2,1)}, bf16[96,4096]{1,0:T(8,128)(2,1)}, bf1...) custom-call(bf16[96,4096]{1,0:T(8,128)(2,1)} %copy-done.56, ...), custom_call_target="tpu_custom_call" | custom-call | flops 14495514624 | bytes 50331648 | tf_op jit(solution)/shard_map/expert_forward/pallas_call | solution.py:225
  159.4 1.5 collective-permute-start.23
  160.9 13.5 %collective-permute-done.21.refs_0_.refs_1_ = bf16[128,2048]{1,0:T(8,128)(2,1)S(1)} collective-permute-done((bf16[128,2048]{1,0:T(8,128)(2,1)}, bf16[128,2048]{1,0:T(8,128)(2,1)S(1)}, u32[]{:S(2)}, u32[]{:S(2)}) %collective-permute-start.21) | collective-permute-done | bytes 524320 | tf_op jit(solution)/shard_map/ppermute | solution.py:369
  174.5 5.6 %collective-permute-done.23.refs_1_ = bf16[128,2048]{1,0:T(8,128)(2,1)S(1)} collective-permute-done((bf16[128,2048]{1,0:T(8,128)(2,1)}, bf16[128,2048]{1,0:T(8,128)(2,1)S(1)}, u32[]{:S(2)}, u32[]{:S(2)}) %collective-permute-start.23) | collective-permute-done | bytes 524320 | tf_op jit(solution)/shard_map/ppermute | solution.py:369
  180.9 1.4 next_choice.6
  183.3 1.3 collective-permute-start.24
  186.2 1.3 collective-permute-start.32
  187.5 1.1 copy-done.5
  191.7 1.0 collective-permute-start.29
  192.7 11.4 %collective-permute-done.24.refs_1_.refs_7_ = bf16[96,4096]{1,0:T(8,128)(2,1)} collective-permute-done((bf16[96,4096]{1,0:T(8,128)(2,1)}, bf16[96,4096]{1,0:T(8,128)(2,1)}, u32[]{:S(2)}, u32[]{:S(2)}) %collective-permute-start.24) | collective-permute-done | bytes 786464 | tf_op jit(solution)/shard_map/ppermute | solution.py:369
  204.1 1.3 collective-permute-start.25
  205.3 15.5 %collective-permute-done.18.refs_1_.refs_16_ = bf16[96,4096]{1,0:T(8,128)(2,1)S(1)} collective-permute-done((bf16[96,4096]{1,0:T(8,128)(2,1)}, bf16[96,4096]{1,0:T(8,128)(2,1)S(1)}, u32[]{:S(2)}, u32[]{:S(2)}) %collective-permute-start.18) | collective-permute-done | bytes 786464 | tf_op jit(solution)/shard_map/ppermute | solution.py:369
  221.7 1.3 collective-permute-start.19
  223.0 1.1 copy-done.9
  224.1 2.6 back_sum.17
  226.7 2.7 back_sum.20
  229.4 1.0 collective-permute-start.30
  230.4 7.3 %collective-permute-done.32.refs_6_ = bf16[96,4096]{1,0:T(8,128)(2,1)} collective-permute-done((bf16[96,4096]{1,0:T(8,128)(2,1)}, bf16[96,4096]{1,0:T(8,128)(2,1)}, u32[]{:S(2)}, u32[]{:S(2)}) %collective-permute-start.32) | collective-permute-done | bytes 786464 | tf_op jit(solution)/shard_map/ppermute | solution.py:369
  237.8 30.4 %expert_backward.1 = (bf16[96,4096]{1,0:T(8,128)(2,1)}, bf16[96,4096]{1,0:T(8,128)(2,1)}, bf16[96,4096]{1,0:T(8,128)(2,1)}, bf16[96,4096]{1,0:T(8,128)(2,1)}, bf...) custom-call(bf16[96,4096]{1,0:T(8,128)(2,1)} %copy-done.45, ...), custom_call_target="tpu_custom_call" | custom-call | flops 14495514624 | bytes 50331648 | tf_op jit(solution)/shard_map/expert_backward/pallas_call | solution.py:225
  269.1 1.3 collective-permute-start.35
  270.4 1.1 copy-done.11
  271.5 2.7 back_sum.21
  274.2 2.7 back_sum.18
  278.7 1.3 collective-permute-start.33
  280.0 9.8 %collective-permute-done.35.refs_1_ = bf16[96,4096]{1,0:T(8,128)(2,1)S(1)} collective-permute-done((bf16[96,4096]{1,0:T(8,128)(2,1)}, bf16[96,4096]{1,0:T(8,128)(2,1)S(1)}, u32[]{:S(2)}, u32[]{:S(2)}) %collective-permute-start.35) | collective-permute-done | bytes 786464 | tf_op jit(solution)/shard_map/ppermute | solution.py:369
  292.4 8.2 %collective-permute-done.28.refs_2_.refs_1_ = bf16[128,2048]{1,0:T(8,128)(2,1)} collective-permute-done((bf16[128,2048]{1,0:T(8,128)(2,1)}, bf16[128,2048]{1,0:T(8,128)(2,1)}, u32[]{:S(2)}, u32[]{:S(2)}) %collective-permute-start.28) | collective-permute-done | bytes 524320 | tf_op jit(solution)/shard_map/ppermute | solution.py:369
  302.2 4.4 %collective-permute-done.33.refs_1_ = bf16[96,4096]{1,0:T(8,128)(2,1)S(1)} collective-permute-done((bf16[96,4096]{1,0:T(8,128)(2,1)}, bf16[96,4096]{1,0:T(8,128)(2,1)S(1)}, u32[]{:S(2)}, u32[]{:S(2)}) %collective-permute-start.33) | collective-permute-done | bytes 786464 | tf_op jit(solution)/shard_map/ppermute | solution.py:369
  306.7 5.2 %collective-permute-done.40.refs_2_ = bf16[128,2048]{1,0:T(8,128)(2,1)} collective-permute-done((bf16[128,2048]{1,0:T(8,128)(2,1)}, bf16[128,2048]{1,0:T(8,128)(2,1)}, u32[]{:S(2)}, u32[]{:S(2)}) %collective-permute-start.40) | collective-permute-done | bytes 524320 | tf_op jit(solution)/shard_map/ppermute | solution.py:369
  311.9 2.4 back_sum.28
  315.1 8.0 %collective-permute-done.37.refs_2_ = bf16[128,2048]{1,0:T(8,128)(2,1)} collective-permute-done((bf16[128,2048]{1,0:T(8,128)(2,1)}, bf16[128,2048]{1,0:T(8,128)(2,1)}, u32[]{:S(2)}, u32[]{:S(2)}) %collective-permute-start.37) | collective-permute-done | bytes 524320 | tf_op jit(solution)/shard_map/ppermute | solution.py:369
  323.1 2.4 back_sum.25
  327.1 7.3 %collective-permute-done.41.refs_2_ = bf16[128,2048]{1,0:T(8,128)(2,1)} collective-permute-done((bf16[128,2048]{1,0:T(8,128)(2,1)}, bf16[128,2048]{1,0:T(8,128)(2,1)}, u32[]{:S(2)}, u32[]{:S(2)}) %collective-permute-start.41) | collective-permute-done | bytes 524320 | tf_op jit(solution)/shard_map/ppermute | solution.py:369
  334.3 1.7 back_sum.29
  337.0 6.7 %collective-permute-done.38.refs_2_ = bf16[128,2048]{1,0:T(8,128)(2,1)S(1)} collective-permute-done((bf16[128,2048]{1,0:T(8,128)(2,1)}, bf16[128,2048]{1,0:T(8,128)(2,1)S(1)}, u32[]{:S(2)}, u32[]{:S(2)}) %collective-permute-start.38) | collective-permute-done | bytes 524320 | tf_op jit(solution)/shard_map/ppermute | solution.py:369
  343.7 1.5 back_sum.26
  345.2 1.2 collective-permute-start.39
  346.5 2.6 back_sum.22.refs_3_
  349.1 2.7 back_sum.23
  351.8 1.3 back_sum.30.refs_3_
  353.0 2.0 collective-permute-done.39.refs_2_
  355.0 1.3 back_sum.31
  (202 shorter events, 34.0 us)
Async XLA Ops:
  0.6 19.4 %copy-start.61 = (bf16[128,4096]{1,0:T(8,128)(2,1)S(1)}, bf16[128,4096]{1,0:T(8,128)(2,1)}, u32[]{:S(2)}) copy-start(bf16[128,4096]{1,0:T(8,128)(2,1)} %param.8) | copy-start | bytes 3145732
  0.6 38.2 %collective-permute-start.4 = (bf16[4096,768]{1,0:T(8,128)(2,1)}, bf16[4096,768]{1,0:T(8,128)(2,1)}, u32[]{:S(2)}, u32[]{:S(2)}) collective-permute-start(bf16[4096,768]{1,0:T(8,128)(2,1)} %bitcast.9), channel_id=1, source_target_pairs={{0,1},{1,0},{2,3},{3,2},{4,5},{5,4},{6,7},{7,6},{8,9},{9,8},{10,11... | collective-permute-start | bytes 18874376 | tf_op jit(solution)/shard_map/ppermute | solution.py:369
  1.2 37.6 %collective-permute-start.5 = (bf16[4096,768]{1,0:T(8,128)(2,1)}, bf16[4096,768]{1,0:T(8,128)(2,1)}, u32[]{:S(2)}, u32[]{:S(2)}) collective-permute-start(bf16[4096,768]{1,0:T(8,128)(2,1)} %bitcast.12), channel_id=1, source_target_pairs={{0,1},{1,0},{2,3},{3,2},{4,5},{5,4},{6,7},{7,6},{8,9},{9,8},{10,11... | collective-permute-start | bytes 18874376 | tf_op jit(solution)/shard_map/ppermute | solution.py:369
  1.2 37.6 %collective-permute-start.6 = (bf16[768,4096]{1,0:T(8,128)(2,1)}, bf16[768,4096]{1,0:T(8,128)(2,1)}, u32[]{:S(2)}, u32[]{:S(2)}) collective-permute-start(bf16[768,4096]{1,0:T(8,128)(2,1)} %bitcast.15), channel_id=1, source_target_pairs={{0,1},{1,0},{2,3},{3,2},{4,5},{5,4},{6,7},{7,6},{8,9},{9,8},{10,11... | collective-permute-start | bytes 18874376 | tf_op jit(solution)/shard_map/ppermute | solution.py:369
  2.9 16.2 %collective-permute-start.1 = (bf16[128,2048]{1,0:T(8,128)(2,1)S(1)}, bf16[128,2048]{1,0:T(8,128)(2,1)S(1)}, u32[]{:S(2)}, u32[]{:S(2)}) collective-permute-start(bf16[128,2048]{1,0:T(8,128)(2,1)S(1)} %get-tuple-element.88.refs_1_), channel_id=1, source_target_pairs={{0,4},{1,5},{2,6},{3,7},{4,12},{5,13},{6,14},{7,15},{8,0},{9,1},{1... | collective-permute-start | bytes 1572872 | tf_op jit(solution)/shard_map/ppermute | solution.py:369
  9.3 25.2 %copy-start.39 = (f32[192,128]{1,0:T(8,128)}, f32[192,128]{1,0:T(8,128)S(1)}, u32[]{:S(2)}) copy-start(f32[192,128]{1,0:T(8,128)S(1)} %get-tuple-element.44.gated.mix) | copy-start | bytes 294916
  9.3 28.7 %collective-permute-start.3 = (bf16[96,4096]{1,0:T(8,128)(2,1)}, bf16[96,4096]{1,0:T(8,128)(2,1)}, u32[]{:S(2)}, u32[]{:S(2)}) collective-permute-start(bf16[96,4096]{1,0:T(8,128)(2,1)} %get-tuple-element.49), channel_id=1, source_target_pairs={{0,2},{1,3},{2,0},{3,1},{4,6},{5,7},{6,4},{7,5},{8,10},{9,11},{10,... | collective-permute-start | bytes 2359304 | tf_op jit(solution)/shard_map/ppermute | solution.py:369
  19.2 18.8 %copy-start.30 = (bf16[128,2048]{1,0:T(8,128)(2,1)}, bf16[128,2048]{1,0:T(8,128)(2,1)S(1)}, u32[]{:S(2)}) copy-start(bf16[128,2048]{1,0:T(8,128)(2,1)S(1)} %collective-permute-done.1.refs_1_.refs_0_) | copy-start | bytes 1572868
  19.2 15.3 %collective-permute-start = (bf16[128,2176]{1,0:T(8,128)(2,1)S(1)}, bf16[128,2176]{1,0:T(8,128)(2,1)S(1)}, u32[]{:S(2)}, u32[]{:S(2)}) collective-permute-start(bf16[128,2176]{1,0:T(8,128)(2,1)S(1)} %fusion.1.refs_0_), channel_id=1, source_target_pairs={{0,4},{1,5},{2,6},{3,7},{4,12},{5,13},{6,14},{7,15},{8,0},{9,1},{1... | collective-permute-start | bytes 1671176 | tf_op jit(solution)/shard_map/ppermute | solution.py:369
  20.1 18.7 %copy-start.1 = (bf16[128,2048]{1,0:T(8,128)(2,1)}, bf16[128,2048]{1,0:T(8,128)(2,1)S(1)}, u32[]{:S(2)}) copy-start(bf16[128,2048]{1,0:T(8,128)(2,1)S(1)} %get-tuple-element.86.refs_1_.refs_0_) | copy-start | bytes 1572868
  20.1 18.7 %copy-start.13 = (bf16[128,2048]{1,0:T(8,128)(2,1)}, bf16[128,2048]{1,0:T(8,128)(2,1)S(1)}, u32[]{:S(2)}) copy-start(bf16[128,2048]{1,0:T(8,128)(2,1)S(1)} %get-tuple-element.87.refs_0_) | copy-start | bytes 1572868
  34.5 33.9 %collective-permute-start.9 = (bf16[96,4096]{1,0:T(8,128)(2,1)}, bf16[96,4096]{1,0:T(8,128)(2,1)}, u32[]{:S(2)}, u32[]{:S(2)}) collective-permute-start(bf16[96,4096]{1,0:T(8,128)(2,1)} %get-tuple-element.51), channel_id=1, source_target_pairs={{0,2},{1,3},{2,0},{3,1},{4,6},{5,7},{6,4},{7,5},{8,10},{9,11},{10,... | collective-permute-start | bytes 2359304 | tf_op jit(solution)/shard_map/ppermute | solution.py:369
  37.9 81.1 %copy-start.41 = (f32[192,128]{1,0:T(8,128)}, f32[192,128]{1,0:T(8,128)S(1)}, u32[]{:S(2)}) copy-start(f32[192,128]{1,0:T(8,128)S(1)} %get-tuple-element.61.gated.mix) | copy-start | bytes 294916
  37.9 81.1 %copy-start.50 = (bf16[192,128]{1,0:T(8,128)(2,1)}, bf16[192,128]{1,0:T(8,128)(2,1)S(1)}, u32[]{:S(2)}) copy-start(bf16[192,128]{1,0:T(8,128)(2,1)S(1)} %get-tuple-element.60.pick.mix) | copy-start | bytes 147460
  38.0 16.7 %collective-permute-start.2 = (bf16[128,2176]{1,0:T(8,128)(2,1)}, bf16[128,2176]{1,0:T(8,128)(2,1)S(1)}, u32[]{:S(2)}, u32[]{:S(2)}) collective-permute-start(bf16[128,2176]{1,0:T(8,128)(2,1)} %tie.23), channel_id=1, source_target_pairs={{0,4},{1,5},{2,6},{3,7},{4,12},{5,13},{6,14},{7,15},{8,0},{9,1},{1... | collective-permute-start | bytes 1671176 | tf_op jit(solution)/shard_map/ppermute | solution.py:369
  38.8 24.5 %collective-permute-start.7 = (bf16[128,2048]{1,0:T(8,128)(2,1)}, bf16[128,2048]{1,0:T(8,128)(2,1)S(1)}, u32[]{:S(2)}, u32[]{:S(2)}) collective-permute-start(bf16[128,2048]{1,0:T(8,128)(2,1)} %tie.24), channel_id=1, source_target_pairs={{0,4},{1,5},{2,6},{3,7},{4,12},{5,13},{6,14},{7,15},{8,0},{9,1},{1... | collective-permute-start | bytes 1572872 | tf_op jit(solution)/shard_map/ppermute | solution.py:369
  54.7 12.3 %copy-start.24 = (bf16[128,2176]{1,0:T(8,128)(2,1)}, bf16[128,2176]{1,0:T(8,128)(2,1)S(1)}, u32[]{:S(2)}) copy-start(bf16[128,2176]{1,0:T(8,128)(2,1)S(1)} %collective-permute-done.2.refs_0_) | copy-start | bytes 1671172
  67.0 89.7 %copy-start.43 = (f32[192,128]{1,0:T(8,128)}, f32[192,128]{1,0:T(8,128)S(1)}, u32[]{:S(2)}) copy-start(f32[192,128]{1,0:T(8,128)S(1)} %get-tuple-element.68.mix.gated) | copy-start | bytes 294916
  67.0 24.4 %collective-permute-start.8 = (bf16[128,2176]{1,0:T(8,128)(2,1)}, bf16[128,2176]{1,0:T(8,128)(2,1)S(1)}, u32[]{:S(2)}, u32[]{:S(2)}) collective-permute-start(bf16[128,2176]{1,0:T(8,128)(2,1)} %tie.25), channel_id=1, source_target_pairs={{0,4},{1,5},{2,6},{3,7},{4,12},{5,13},{6,14},{7,15},{8,0},{9,1},{1... | collective-permute-start | bytes 1671176 | tf_op jit(solution)/shard_map/ppermute | solution.py:369
  67.9 28.3 %collective-permute-start.11 = (bf16[96,4096]{1,0:T(8,128)(2,1)S(1)}, bf16[96,4096]{1,0:T(8,128)(2,1)}, u32[]{:S(2)}, u32[]{:S(2)}) collective-permute-start(bf16[96,4096]{1,0:T(8,128)(2,1)S(1)} %get-tuple-element.53), channel_id=1, source_target_pairs={{0,2},{1,3},{2,0},{3,1},{4,6},{5,7},{6,4},{7,5},{8,10},{9,11},{10,... | collective-permute-start | bytes 2359304 | tf_op jit(solution)/shard_map/ppermute | solution.py:369
  68.4 23.0 %collective-permute-start.10 = (bf16[128,2048]{1,0:T(8,128)(2,1)}, bf16[128,2048]{1,0:T(8,128)(2,1)S(1)}, u32[]{:S(2)}, u32[]{:S(2)}) collective-permute-start(bf16[128,2048]{1,0:T(8,128)(2,1)} %tie.26), channel_id=1, source_target_pairs={{0,4},{1,5},{2,6},{3,7},{4,12},{5,13},{6,14},{7,15},{8,0},{9,1},{1... | collective-permute-start | bytes 1572872 | tf_op jit(solution)/shard_map/ppermute | solution.py:369
  71.7 50.4 %collective-permute-start.12 = (bf16[96,4096]{1,0:T(8,128)(2,1)}, bf16[96,4096]{1,0:T(8,128)(2,1)}, u32[]{:S(2)}, u32[]{:S(2)}) collective-permute-start(bf16[96,4096]{1,0:T(8,128)(2,1)} %get-tuple-element.54), channel_id=1, source_target_pairs={{0,2},{1,3},{2,0},{3,1},{4,6},{5,7},{6,4},{7,5},{8,10},{9,11},{10,... | collective-permute-start | bytes 2359304 | tf_op jit(solution)/shard_map/ppermute | solution.py:369
  95.1 30.3 %collective-permute-start.13 = (bf16[96,4096]{1,0:T(8,128)(2,1)}, bf16[96,4096]{1,0:T(8,128)(2,1)}, u32[]{:S(2)}, u32[]{:S(2)}) collective-permute-start(bf16[96,4096]{1,0:T(8,128)(2,1)} %get-tuple-element.55), channel_id=1, source_target_pairs={{0,2},{1,3},{2,0},{3,1},{4,6},{5,7},{6,4},{7,5},{8,10},{9,11},{10,... | collective-permute-start | bytes 2359304 | tf_op jit(solution)/shard_map/ppermute | solution.py:369
  96.2 16.0 %collective-permute-start.15 = (bf16[128,2048]{1,0:T(8,128)(2,1)}, bf16[128,2048]{1,0:T(8,128)(2,1)S(1)}, u32[]{:S(2)}, u32[]{:S(2)}) collective-permute-start(bf16[128,2048]{1,0:T(8,128)(2,1)} %tie.29), channel_id=1, source_target_pairs={{0,4},{1,5},{2,6},{3,7},{4,12},{5,13},{6,14},{7,15},{8,0},{9,1},{1... | collective-permute-start | bytes 1572872 | tf_op jit(solution)/shard_map/ppermute | solution.py:369
  96.6 22.4 %collective-permute-start.14 = (bf16[128,2048]{1,0:T(8,128)(2,1)}, bf16[128,2048]{1,0:T(8,128)(2,1)S(1)}, u32[]{:S(2)}, u32[]{:S(2)}) collective-permute-start(bf16[128,2048]{1,0:T(8,128)(2,1)} %tie.27), channel_id=1, source_target_pairs={{0,4},{1,5},{2,6},{3,7},{4,12},{5,13},{6,14},{7,15},{8,0},{9,1},{1... | collective-permute-start | bytes 1572872 | tf_op jit(solution)/shard_map/ppermute | solution.py:369
  120.5 35.6 %collective-permute-start.16 = (bf16[96,4096]{1,0:T(8,128)(2,1)S(1)}, bf16[96,4096]{1,0:T(8,128)(2,1)}, u32[]{:S(2)}, u32[]{:S(2)}) collective-permute-start(bf16[96,4096]{1,0:T(8,128)(2,1)S(1)} %get-tuple-element.62), channel_id=1, source_target_pairs={{0,2},{1,3},{2,0},{3,1},{4,6},{5,7},{6,4},{7,5},{8,10},{9,11},{10,... | collective-permute-start | bytes 2359304 | tf_op jit(solution)/shard_map/ppermute | solution.py:369
  121.2 35.5 %collective-permute-start.20 = (bf16[128,2048]{1,0:T(8,128)(2,1)}, bf16[128,2048]{1,0:T(8,128)(2,1)S(1)}, u32[]{:S(2)}, u32[]{:S(2)}) collective-permute-start(bf16[128,2048]{1,0:T(8,128)(2,1)} %tie.33), channel_id=1, source_target_pairs={{0,4},{1,5},{2,6},{3,7},{4,12},{5,13},{6,14},{7,15},{8,0},{9,1},{1... | collective-permute-start | bytes 1572872 | tf_op jit(solution)/shard_map/ppermute | solution.py:369
  122.1 34.6 %collective-permute-start.22 = (bf16[128,2048]{1,0:T(8,128)(2,1)}, bf16[128,2048]{1,0:T(8,128)(2,1)S(1)}, u32[]{:S(2)}, u32[]{:S(2)}) collective-permute-start(bf16[128,2048]{1,0:T(8,128)(2,1)} %tie.35), channel_id=1, source_target_pairs={{0,4},{1,5},{2,6},{3,7},{4,12},{5,13},{6,14},{7,15},{8,0},{9,1},{1... | collective-permute-start | bytes 1572872 | tf_op jit(solution)/shard_map/ppermute | solution.py:369
  156.1 28.4 %collective-permute-start.17 = (bf16[96,4096]{1,0:T(8,128)(2,1)}, bf16[96,4096]{1,0:T(8,128)(2,1)S(1)}, u32[]{:S(2)}, u32[]{:S(2)}) collective-permute-start(bf16[96,4096]{1,0:T(8,128)(2,1)} %tie.30), channel_id=1, source_target_pairs={{0,2},{1,3},{2,0},{3,1},{4,6},{5,7},{6,4},{7,5},{8,10},{9,11},{10,... | collective-permute-start | bytes 2359304 | tf_op jit(solution)/shard_map/ppermute | solution.py:369
  159.3 20.8 %copy-start = (bf16[96,4096]{1,0:T(8,128)(2,1)S(1)}, bf16[96,4096]{1,0:T(8,128)(2,1)}, u32[]{:S(2)}) copy-start(bf16[96,4096]{1,0:T(8,128)(2,1)} %get-tuple-element.56.refs_2_.refs_0_) | copy-start | bytes 2359300
  159.3 15.1 %collective-permute-start.21 = (bf16[128,2048]{1,0:T(8,128)(2,1)}, bf16[128,2048]{1,0:T(8,128)(2,1)S(1)}, u32[]{:S(2)}, u32[]{:S(2)}) collective-permute-start(bf16[128,2048]{1,0:T(8,128)(2,1)} %tie.34), channel_id=1, source_target_pairs={{0,4},{1,5},{2,6},{3,7},{4,12},{5,13},{6,14},{7,15},{8,0},{9,1},{1... | collective-permute-start | bytes 1572872 | tf_op jit(solution)/shard_map/ppermute | solution.py:369
  159.4 28.0 %copy-start.16 = (bf16[96,4096]{1,0:T(8,128)(2,1)S(1)}, bf16[96,4096]{1,0:T(8,128)(2,1)}, u32[]{:S(2)}) copy-start(bf16[96,4096]{1,0:T(8,128)(2,1)} %get-tuple-element.70.refs_0_) | copy-start | bytes 2359300
  159.4 20.7 %collective-permute-start.23 = (bf16[128,2048]{1,0:T(8,128)(2,1)}, bf16[128,2048]{1,0:T(8,128)(2,1)S(1)}, u32[]{:S(2)}, u32[]{:S(2)}) collective-permute-start(bf16[128,2048]{1,0:T(8,128)(2,1)} %tie.36), channel_id=1, source_target_pairs={{0,4},{1,5},{2,6},{3,7},{4,12},{5,13},{6,14},{7,15},{8,0},{9,1},{1... | collective-permute-start | bytes 1572872 | tf_op jit(solution)/shard_map/ppermute | solution.py:369
  174.5 13.0 %copy-start.33 = (bf16[128,2048]{1,0:T(8,128)(2,1)}, bf16[128,2048]{1,0:T(8,128)(2,1)S(1)}, u32[]{:S(2)}) copy-start(bf16[128,2048]{1,0:T(8,128)(2,1)S(1)} %collective-permute-done.21.refs_0_.refs_1_) | copy-start | bytes 1572868
  183.3 20.8 %collective-permute-start.24 = (bf16[96,4096]{1,0:T(8,128)(2,1)}, bf16[96,4096]{1,0:T(8,128)(2,1)}, u32[]{:S(2)}, u32[]{:S(2)}) collective-permute-start(bf16[96,4096]{1,0:T(8,128)(2,1)} %get-tuple-element.67), channel_id=1, source_target_pairs={{0,2},{1,3},{2,0},{3,1},{4,6},{5,7},{6,4},{7,5},{8,10},{9,11},{10,... | collective-permute-start | bytes 2359304 | tf_op jit(solution)/shard_map/ppermute | solution.py:369
  185.4 35.4 %collective-permute-start.18 = (bf16[96,4096]{1,0:T(8,128)(2,1)}, bf16[96,4096]{1,0:T(8,128)(2,1)S(1)}, u32[]{:S(2)}, u32[]{:S(2)}) collective-permute-start(bf16[96,4096]{1,0:T(8,128)(2,1)} %tie.31), channel_id=1, source_target_pairs={{0,2},{1,3},{2,0},{3,1},{4,6},{5,7},{6,4},{7,5},{8,10},{9,11},{10,... | collective-permute-start | bytes 2359304 | tf_op jit(solution)/shard_map/ppermute | solution.py:369
  186.2 51.6 %collective-permute-start.32 = (bf16[96,4096]{1,0:T(8,128)(2,1)}, bf16[96,4096]{1,0:T(8,128)(2,1)}, u32[]{:S(2)}, u32[]{:S(2)}) collective-permute-start(bf16[96,4096]{1,0:T(8,128)(2,1)} %copy-done.59), channel_id=1, source_target_pairs={{0,2},{1,3},{2,0},{3,1},{4,6},{5,7},{6,4},{7,5},{8,10},{9,11},{10,... | collective-permute-start | bytes 2359304 | tf_op jit(solution)/shard_map/ppermute | solution.py:369
  190.1 32.8 %collective-permute-start.26 = (bf16[128,2048]{1,0:T(8,128)(2,1)}, bf16[128,2048]{1,0:T(8,128)(2,1)}, u32[]{:S(2)}, u32[]{:S(2)}) collective-permute-start(bf16[128,2048]{1,0:T(8,128)(2,1)} %tie.38), channel_id=1, source_target_pairs={{0,8},{1,9},{2,10},{3,11},{4,0},{5,1},{6,2},{7,3},{8,12},{9,13},{1... | collective-permute-start | bytes 1572872 | tf_op jit(solution)/shard_map/ppermute | solution.py:369
  191.7 35.1 %collective-permute-start.29 = (bf16[128,2048]{1,0:T(8,128)(2,1)}, bf16[128,2048]{1,0:T(8,128)(2,1)}, u32[]{:S(2)}, u32[]{:S(2)}) collective-permute-start(bf16[128,2048]{1,0:T(8,128)(2,1)} %tie.39), channel_id=1, source_target_pairs={{0,8},{1,9},{2,10},{3,11},{4,0},{5,1},{6,2},{7,3},{8,12},{9,13},{1... | collective-permute-start | bytes 1572872 | tf_op jit(solution)/shard_map/ppermute | solution.py:369
  204.1 18.9 %copy-start.20 = (bf16[96,4096]{1,0:T(8,128)(2,1)S(1)}, bf16[96,4096]{1,0:T(8,128)(2,1)}, u32[]{:S(2)}) copy-start(bf16[96,4096]{1,0:T(8,128)(2,1)} %get-tuple-element.69.refs_0_) | copy-start | bytes 2359300
  204.1 18.9 %copy-start.44 = (f32[192,128]{1,0:T(8,128)S(1)}, f32[192,128]{1,0:T(8,128)}, u32[]{:S(2)}) copy-start(f32[192,128]{1,0:T(8,128)} %copy-done.43) | copy-start | bytes 294916
  204.1 64.2 %collective-permute-start.25 = (bf16[96,4096]{1,0:T(8,128)(2,1)}, bf16[96,4096]{1,0:T(8,128)(2,1)S(1)}, u32[]{:S(2)}, u32[]{:S(2)}) collective-permute-start(bf16[96,4096]{1,0:T(8,128)(2,1)} %tie.37), channel_id=1, source_target_pairs={{0,2},{1,3},{2,0},{3,1},{4,6},{5,7},{6,4},{7,5},{8,10},{9,11},{10,... | collective-permute-start | bytes 2359304 | tf_op jit(solution)/shard_map/ppermute | solution.py:369
  221.7 56.2 %collective-permute-start.19 = (bf16[96,4096]{1,0:T(8,128)(2,1)}, bf16[96,4096]{1,0:T(8,128)(2,1)S(1)}, u32[]{:S(2)}, u32[]{:S(2)}) collective-permute-start(bf16[96,4096]{1,0:T(8,128)(2,1)} %tie.32), channel_id=1, source_target_pairs={{0,2},{1,3},{2,0},{3,1},{4,6},{5,7},{6,4},{7,5},{8,10},{9,11},{10,... | collective-permute-start | bytes 2359304 | tf_op jit(solution)/shard_map/ppermute | solution.py:369
  226.7 47.5 %collective-permute-start.27 = (bf16[128,2048]{1,0:T(8,128)(2,1)}, bf16[128,2048]{1,0:T(8,128)(2,1)}, u32[]{:S(2)}, u32[]{:S(2)}) collective-permute-start(bf16[128,2048]{1,0:T(8,128)(2,1)} %back_sum.17), channel_id=1, source_target_pairs={{0,8},{1,9},{2,10},{3,11},{4,0},{5,1},{6,2},{7,3},{8,12},{9,13},{1... | collective-permute-start | bytes 1572872 | tf_op jit(solution)/shard_map/ppermute | solution.py:369
  229.4 41.0 %collective-permute-start.30 = (bf16[128,2048]{1,0:T(8,128)(2,1)}, bf16[128,2048]{1,0:T(8,128)(2,1)}, u32[]{:S(2)}, u32[]{:S(2)}) collective-permute-start(bf16[128,2048]{1,0:T(8,128)(2,1)} %back_sum.20), channel_id=1, source_target_pairs={{0,8},{1,9},{2,10},{3,11},{4,0},{5,1},{6,2},{7,3},{8,12},{9,13},{1... | collective-permute-start | bytes 1572872 | tf_op jit(solution)/shard_map/ppermute | solution.py:369
  269.1 20.7 %collective-permute-start.35 = (bf16[96,4096]{1,0:T(8,128)(2,1)}, bf16[96,4096]{1,0:T(8,128)(2,1)S(1)}, u32[]{:S(2)}, u32[]{:S(2)}) collective-permute-start(bf16[96,4096]{1,0:T(8,128)(2,1)} %tie.42), channel_id=1, source_target_pairs={{0,2},{1,3},{2,0},{3,1},{4,6},{5,7},{6,4},{7,5},{8,10},{9,11},{10,... | collective-permute-start | bytes 2359304 | tf_op jit(solution)/shard_map/ppermute | solution.py:369
  274.2 15.6 %copy-start.17 = (bf16[96,4096]{1,0:T(8,128)(2,1)S(1)}, bf16[96,4096]{1,0:T(8,128)(2,1)}, u32[]{:S(2)}) copy-start(bf16[96,4096]{1,0:T(8,128)(2,1)} %get-tuple-element.85.refs_0_) | copy-start | bytes 2359300
  274.2 15.6 %copy-start.49 = (bf16[192,128]{1,0:T(8,128)(2,1)S(1)}, bf16[192,128]{1,0:T(8,128)(2,1)}, u32[]{:S(2)}) copy-start(bf16[192,128]{1,0:T(8,128)(2,1)} %copy-done.47) | copy-start | bytes 147460
  274.2 16.9 %collective-permute-start.31 = (bf16[128,2048]{1,0:T(8,128)(2,1)}, bf16[128,2048]{1,0:T(8,128)(2,1)}, u32[]{:S(2)}, u32[]{:S(2)}) collective-permute-start(bf16[128,2048]{1,0:T(8,128)(2,1)} %back_sum.21), channel_id=1, source_target_pairs={{0,8},{1,9},{2,10},{3,11},{4,0},{5,1},{6,2},{7,3},{8,12},{9,13},{1... | collective-permute-start | bytes 1572872 | tf_op jit(solution)/shard_map/ppermute | solution.py:369
  276.9 23.7 %collective-permute-start.28 = (bf16[128,2048]{1,0:T(8,128)(2,1)}, bf16[128,2048]{1,0:T(8,128)(2,1)}, u32[]{:S(2)}, u32[]{:S(2)}) collective-permute-start(bf16[128,2048]{1,0:T(8,128)(2,1)} %back_sum.18), channel_id=1, source_target_pairs={{0,8},{1,9},{2,10},{3,11},{4,0},{5,1},{6,2},{7,3},{8,12},{9,13},{1... | collective-permute-start | bytes 1572872 | tf_op jit(solution)/shard_map/ppermute | solution.py:369
  278.7 27.9 %collective-permute-start.33 = (bf16[96,4096]{1,0:T(8,128)(2,1)}, bf16[96,4096]{1,0:T(8,128)(2,1)S(1)}, u32[]{:S(2)}, u32[]{:S(2)}) collective-permute-start(bf16[96,4096]{1,0:T(8,128)(2,1)} %tie.40), channel_id=1, source_target_pairs={{0,2},{1,3},{2,0},{3,1},{4,6},{5,7},{6,4},{7,5},{8,10},{9,11},{10,... | collective-permute-start | bytes 2359304 | tf_op jit(solution)/shard_map/ppermute | solution.py:369
  291.1 20.7 %collective-permute-start.40 = (bf16[128,2048]{1,0:T(8,128)(2,1)}, bf16[128,2048]{1,0:T(8,128)(2,1)}, u32[]{:S(2)}, u32[]{:S(2)}) collective-permute-start(bf16[128,2048]{1,0:T(8,128)(2,1)} %tie.45), channel_id=1, source_target_pairs={{0,8},{1,9},{2,10},{3,11},{4,0},{5,1},{6,2},{7,3},{8,12},{9,13},{1... | collective-permute-start | bytes 1572872 | tf_op jit(solution)/shard_map/ppermute | solution.py:369
  292.4 19.5 %copy-start.22 = (bf16[96,4096]{1,0:T(8,128)(2,1)S(1)}, bf16[96,4096]{1,0:T(8,128)(2,1)}, u32[]{:S(2)}) copy-start(bf16[96,4096]{1,0:T(8,128)(2,1)} %get-tuple-element.84.refs_0_) | copy-start | bytes 2359300
  292.4 19.5 %copy-start.54 = (bf16[192,128]{1,0:T(8,128)(2,1)S(1)}, bf16[192,128]{1,0:T(8,128)(2,1)}, u32[]{:S(2)}) copy-start(bf16[192,128]{1,0:T(8,128)(2,1)} %copy-done.52) | copy-start | bytes 147460
  300.6 22.5 %collective-permute-start.37 = (bf16[128,2048]{1,0:T(8,128)(2,1)}, bf16[128,2048]{1,0:T(8,128)(2,1)}, u32[]{:S(2)}, u32[]{:S(2)}) collective-permute-start(bf16[128,2048]{1,0:T(8,128)(2,1)} %tie.44), channel_id=1, source_target_pairs={{0,8},{1,9},{2,10},{3,11},{4,0},{5,1},{6,2},{7,3},{8,12},{9,13},{1... | collective-permute-start | bytes 1572872 | tf_op jit(solution)/shard_map/ppermute | solution.py:369
  301.5 25.6 %collective-permute-start.36 = (bf16[96,4096]{1,0:T(8,128)(2,1)}, bf16[96,4096]{1,0:T(8,128)(2,1)}, u32[]{:S(2)}, u32[]{:S(2)}) collective-permute-start(bf16[96,4096]{1,0:T(8,128)(2,1)} %tie.43), channel_id=1, source_target_pairs={{0,2},{1,3},{2,0},{3,1},{4,6},{5,7},{6,4},{7,5},{8,10},{9,11},{10,... | collective-permute-start | bytes 2359304 | tf_op jit(solution)/shard_map/ppermute | solution.py:369
  306.7 18.8 %copy-start.12 = (bf16[96,4096]{1,0:T(8,128)(2,1)}, bf16[96,4096]{1,0:T(8,128)(2,1)S(1)}, u32[]{:S(2)}) copy-start(bf16[96,4096]{1,0:T(8,128)(2,1)S(1)} %collective-permute-done.33.refs_1_) | copy-start | bytes 2359300
  314.2 20.1 %copy-start.21 = (bf16[96,4096]{1,0:T(8,128)(2,1)S(1)}, bf16[96,4096]{1,0:T(8,128)(2,1)}, u32[]{:S(2)}) copy-start(bf16[96,4096]{1,0:T(8,128)(2,1)} %get-tuple-element.81.refs_0_) | copy-start | bytes 2359300
  314.2 20.1 %copy-start.51 = (bf16[192,128]{1,0:T(8,128)(2,1)S(1)}, bf16[192,128]{1,0:T(8,128)(2,1)}, u32[]{:S(2)}) copy-start(bf16[192,128]{1,0:T(8,128)(2,1)} %copy-done.50) | copy-start | bytes 147460
  314.2 20.1 %collective-permute-start.41 = (bf16[128,2048]{1,0:T(8,128)(2,1)}, bf16[128,2048]{1,0:T(8,128)(2,1)}, u32[]{:S(2)}, u32[]{:S(2)}) collective-permute-start(bf16[128,2048]{1,0:T(8,128)(2,1)} %back_sum.28), channel_id=1, source_target_pairs={{0,8},{1,9},{2,10},{3,11},{4,0},{5,1},{6,2},{7,3},{8,12},{9,13},{1... | collective-permute-start | bytes 1572872 | tf_op jit(solution)/shard_map/ppermute | solution.py:369
  325.5 18.3 %collective-permute-start.38 = (bf16[128,2048]{1,0:T(8,128)(2,1)}, bf16[128,2048]{1,0:T(8,128)(2,1)S(1)}, u32[]{:S(2)}, u32[]{:S(2)}) collective-permute-start(bf16[128,2048]{1,0:T(8,128)(2,1)} %back_sum.25), channel_id=1, source_target_pairs={{0,8},{1,9},{2,10},{3,11},{4,0},{5,1},{6,2},{7,3},{8,12},{9,13},{1... | collective-permute-start | bytes 1572872 | tf_op jit(solution)/shard_map/ppermute | solution.py:369
  326.4 25.4 %collective-permute-start.34 = (bf16[96,4096]{1,0:T(8,128)(2,1)}, bf16[96,4096]{1,0:T(8,128)(2,1)S(1)}, u32[]{:S(2)}, u32[]{:S(2)}) collective-permute-start(bf16[96,4096]{1,0:T(8,128)(2,1)} %tie.41), channel_id=1, source_target_pairs={{0,2},{1,3},{2,0},{3,1},{4,6},{5,7},{6,4},{7,5},{8,10},{9,11},{10,... | collective-permute-start | bytes 2359304 | tf_op jit(solution)/shard_map/ppermute | solution.py:369
  336.0 15.7 %collective-permute-start.42 = (bf16[128,2048]{1,0:T(8,128)(2,1)S(1)}, bf16[128,2048]{1,0:T(8,128)(2,1)S(1)}, u32[]{:S(2)}, u32[]{:S(2)}) collective-permute-start(bf16[128,2048]{1,0:T(8,128)(2,1)S(1)} %back_sum.29), channel_id=1, source_target_pairs={{0,8},{1,9},{2,10},{3,11},{4,0},{5,1},{6,2},{7,3},{8,12},{9,13},{1... | collective-permute-start | bytes 1572872 | tf_op jit(solution)/shard_map/ppermute | solution.py:369
  345.2 9.8 %collective-permute-start.39 = (bf16[128,2048]{1,0:T(8,128)(2,1)S(1)}, bf16[128,2048]{1,0:T(8,128)(2,1)S(1)}, u32[]{:S(2)}, u32[]{:S(2)}) collective-permute-start(bf16[128,2048]{1,0:T(8,128)(2,1)S(1)} %back_sum.26), channel_id=1, source_target_pairs={{0,8},{1,9},{2,10},{3,11},{4,0},{5,1},{6,2},{7,3},{8,12},{9,13},{1... | collective-permute-start | bytes 1572872 | tf_op jit(solution)/shard_map/ppermute | solution.py:369
  (41 other events, 107.0 us)

commit v4 on v3

--- a/solution.py
+++ b/solution.py
@@ -460,7 +460,7 @@
     choose("cot", last, [outs[0]])
     moe_out, steps = combine(outs, True, far)
     deps = [came("y", 2 * zs + 1)] if ys == 2 else []
-    grads = expert_backward(own["cot"] + other["cot"], saved, gate_mats, up_mats, down_mats, cap, deps + steps[0][:1])
+    grads = expert_backward(own["cot"] + other["cot"], saved, gate_mats, up_mats, down_mats, cap, deps + steps[0] + steps[1][:1])
     token_grad, _ = combine(grads, False)
     return (moe_out, token_grad)
 

time: 357 us -> 348 us (0.975)
  waiting for transfers between devices: 184 us -> 177 us
  starting transfers between devices: 47.4 us -> 42.4 us
    ppermute x43, waiting for transfers between devices: 184 us -> 177 us  [permute(): return lax.ppermute(value, 'wide', perm)]
    ppermute x43, starting transfers between devices: 47.4 us -> 42.4 us  [permute(): return lax.ppermute(value, 'wide', perm)]
    unnamed x124 -> x116, local copies, waits for them, and re-layouts: 19.8 us -> 21.7 us
  transfers between devices with their start and end apart: 43 -> 43, of which waited for: 20 -> 19; matrix products, arithmetic and copies ran while one was open for 1% -> 1% of each run, Pallas kernels for 28% -> 29%
where the time goes in v4:
time: 348 us; the launch traced here: 347 us
  waiting for transfers between devices  177 us (51%)
  Pallas kernels  102 us (29%)
  starting transfers between devices  42.4 us (12%)
  local copies, waits for them, and re-layouts  23.1 us (7%)
    ppermute x43, waiting for transfers between devices, permute(): return lax.ppermute(value, 'wide', perm)  177 us
    pallas_call x2, Pallas kernels, expert_call(): pl.pallas_call(body, grid=(2, firsts + seconds), in_specs=specs, out_spec...  60.9 us
    ppermute x43, starting transfers between devices, permute(): return lax.ppermute(value, 'wide', perm)  42.4 us
    pallas_call x16, Pallas kernels, back_sum(): pl.pallas_call(body, grid=(1,), in_specs=specs, out_specs=pl.BlockSpec((r...  28.8 us
    unnamed x116, local copies, waits for them, and re-layouts  21.7 us
  transfers between devices with their start and end apart: 43, of which 19 were waited for; matrix products, arithmetic and copies ran while one was open for 1% of the time, Pallas kernels for 29%

profile of v4, /device:TPU:0, one launch (start us, length us, event | category | flops | bytes accessed | tf_op | source)
XLA Modules:
  0.0 346.6 jit_solution(12190711644979912148)
XLA Ops:
  1.7 1.3 fusion.6
  2.9 2.7 collective-permute-start.1
  7.2 2.1 first_choice.4
  9.4 1.5 collective-permute-start.3
  10.9 8.3 %collective-permute-done.1.refs_1_.refs_0_ = bf16[128,2048]{1,0:T(8,128)(2,1)S(1)} collective-permute-done((bf16[128,2048]{1,0:T(8,128)(2,1)S(1)}, bf16[128,2048]{1,0:T(8,128)(2,1)S(1)}, u32[]{:S(2)}, u32[]{:S(2)}) %collective-permute-start.1) | collective-permute-done | bytes 524320 | tf_op jit(solution)/shard_map/ppermute | solution.py:369
  20.2 1.4 next_choice.4
  21.6 1.0 copy-done.38
  22.6 11.9 %collective-permute-done.refs_0_ = bf16[128,2176]{1,0:T(8,128)(2,1)S(1)} collective-permute-done((bf16[128,2176]{1,0:T(8,128)(2,1)S(1)}, bf16[128,2176]{1,0:T(8,128)(2,1)S(1)}, u32[]{:S(2)}, u32[]{:S(2)}) %collective-permute-start) | collective-permute-done | bytes 557088 | tf_op jit(solution)/shard_map/ppermute | solution.py:369
  34.5 1.4 collective-permute-start.9
  35.8 1.2 first_choice.5
  39.8 3.4 collective-permute-start.7
  43.2 12.4 %collective-permute-done.2.refs_0_ = bf16[128,2176]{1,0:T(8,128)(2,1)S(1)} collective-permute-done((bf16[128,2176]{1,0:T(8,128)(2,1)}, bf16[128,2176]{1,0:T(8,128)(2,1)S(1)}, u32[]{:S(2)}, u32[]{:S(2)}) %collective-permute-start.2) | collective-permute-done | bytes 557088 | tf_op jit(solution)/shard_map/ppermute | solution.py:369
  55.6 8.7 %collective-permute-done.7.refs_1_.refs_0_ = bf16[128,2048]{1,0:T(8,128)(2,1)S(1)} collective-permute-done((bf16[128,2048]{1,0:T(8,128)(2,1)}, bf16[128,2048]{1,0:T(8,128)(2,1)S(1)}, u32[]{:S(2)}, u32[]{:S(2)}) %collective-permute-start.7) | collective-permute-done | bytes 524320 | tf_op jit(solution)/shard_map/ppermute | solution.py:369
  64.3 1.2 first_choice.6
  66.4 0.9 copy-done.55
  68.7 3.3 collective-permute-start.10
  72.0 1.5 collective-permute-start.12
  73.5 18.2 %collective-permute-done.10.refs_1_ = bf16[128,2048]{1,0:T(8,128)(2,1)S(1)} collective-permute-done((bf16[128,2048]{1,0:T(8,128)(2,1)}, bf16[128,2048]{1,0:T(8,128)(2,1)S(1)}, u32[]{:S(2)}, u32[]{:S(2)}) %collective-permute-start.10) | collective-permute-done | bytes 524320 | tf_op jit(solution)/shard_map/ppermute | solution.py:369
  91.7 2.1 first_choice.7
  93.9 0.9 copy-done.14
  95.4 1.1 collective-permute-start.13
  96.9 3.3 collective-permute-start.14
  100.1 12.4 %collective-permute-done.15.refs_1_.refs_0_ = bf16[128,2048]{1,0:T(8,128)(2,1)S(1)} collective-permute-done((bf16[128,2048]{1,0:T(8,128)(2,1)}, bf16[128,2048]{1,0:T(8,128)(2,1)S(1)}, u32[]{:S(2)}, u32[]{:S(2)}) %collective-permute-start.15) | collective-permute-done | bytes 524320 | tf_op jit(solution)/shard_map/ppermute | solution.py:369
  112.5 6.8 %collective-permute-done.14.refs_0_ = bf16[128,2048]{1,0:T(8,128)(2,1)S(1)} collective-permute-done((bf16[128,2048]{1,0:T(8,128)(2,1)}, bf16[128,2048]{1,0:T(8,128)(2,1)S(1)}, u32[]{:S(2)}, u32[]{:S(2)}) %collective-permute-start.14) | collective-permute-done | bytes 524320 | tf_op jit(solution)/shard_map/ppermute | solution.py:369
  121.5 0.9 collective-permute-start.20
  122.4 3.3 collective-permute-start.22
  125.7 30.5 %expert_forward.1 = (bf16[96,4096]{1,0:T(8,128)(2,1)}, bf16[96,4096]{1,0:T(8,128)(2,1)}, bf16[96,4096]{1,0:T(8,128)(2,1)}, bf16[96,4096]{1,0:T(8,128)(2,1)}, bf1...) custom-call(bf16[96,4096]{1,0:T(8,128)(2,1)} %copy-done.50, ...), custom_call_target="tpu_custom_call" | custom-call | flops 14495514624 | bytes 50331648 | tf_op jit(solution)/shard_map/expert_forward/pallas_call | solution.py:225
  160.1 12.9 %collective-permute-done.17.refs_1_ = bf16[96,4096]{1,0:T(8,128)(2,1)S(1)} collective-permute-done((bf16[96,4096]{1,0:T(8,128)(2,1)}, bf16[96,4096]{1,0:T(8,128)(2,1)S(1)}, u32[]{:S(2)}, u32[]{:S(2)}) %collective-permute-start.17) | collective-permute-done | bytes 786464 | tf_op jit(solution)/shard_map/ppermute | solution.py:369
  174.5 1.1 copy-done.5
  177.2 35.5 %collective-permute-done.23.refs_1_ = bf16[128,2048]{1,0:T(8,128)(2,1)} collective-permute-done((bf16[128,2048]{1,0:T(8,128)(2,1)}, bf16[128,2048]{1,0:T(8,128)(2,1)}, u32[]{:S(2)}, u32[]{:S(2)}) %collective-permute-start.23) | collective-permute-done | bytes 524320 | tf_op jit(solution)/shard_map/ppermute | solution.py:369
  213.5 2.6 next_choice.6
  217.1 1.5 collective-permute-start.24
  220.7 1.4 copy-done.20
  222.1 2.6 back_sum.20
  224.7 4.9 %collective-permute-done.24.refs_1_.refs_7_ = bf16[96,4096]{1,0:T(8,128)(2,1)} collective-permute-done((bf16[96,4096]{1,0:T(8,128)(2,1)}, bf16[96,4096]{1,0:T(8,128)(2,1)}, u32[]{:S(2)}, u32[]{:S(2)}) %collective-permute-start.24) | collective-permute-done | bytes 786464 | tf_op jit(solution)/shard_map/ppermute | solution.py:369
  229.6 1.3 collective-permute-start.25
  232.0 1.1 copy-done.21
  233.2 2.6 back_sum.17
  235.8 2.2 collective-permute-done.32.refs_6_
  238.0 30.3 %expert_backward.1 = (bf16[96,4096]{1,0:T(8,128)(2,1)}, bf16[96,4096]{1,0:T(8,128)(2,1)}, bf16[96,4096]{1,0:T(8,128)(2,1)}, bf16[96,4096]{1,0:T(8,128)(2,1)}, bf...) custom-call(bf16[96,4096]{1,0:T(8,128)(2,1)} %copy-done.38, ...), custom_call_target="tpu_custom_call" | custom-call | flops 14495514624 | bytes 50331648 | tf_op jit(solution)/shard_map/expert_backward/pallas_call | solution.py:225
  269.3 1.5 collective-permute-start.35
  270.7 1.1 copy-done.11
  271.9 2.7 back_sum.21
  274.6 2.7 back_sum.18
  278.7 11.2 %collective-permute-done.35.refs_1_ = bf16[96,4096]{1,0:T(8,128)(2,1)S(1)} collective-permute-done((bf16[96,4096]{1,0:T(8,128)(2,1)}, bf16[96,4096]{1,0:T(8,128)(2,1)S(1)}, u32[]{:S(2)}, u32[]{:S(2)}) %collective-permute-start.35) | collective-permute-done | bytes 786464 | tf_op jit(solution)/shard_map/ppermute | solution.py:369
  292.5 8.4 %collective-permute-done.28.refs_2_.refs_1_ = bf16[128,2048]{1,0:T(8,128)(2,1)} collective-permute-done((bf16[128,2048]{1,0:T(8,128)(2,1)}, bf16[128,2048]{1,0:T(8,128)(2,1)}, u32[]{:S(2)}, u32[]{:S(2)}) %collective-permute-start.28) | collective-permute-done | bytes 524320 | tf_op jit(solution)/shard_map/ppermute | solution.py:369
  300.9 0.9 collective-permute-start.37
  302.3 3.1 collective-permute-done.33.refs_1_
  305.4 6.8 %collective-permute-done.40.refs_2_ = bf16[128,2048]{1,0:T(8,128)(2,1)} collective-permute-done((bf16[128,2048]{1,0:T(8,128)(2,1)}, bf16[128,2048]{1,0:T(8,128)(2,1)}, u32[]{:S(2)}, u32[]{:S(2)}) %collective-permute-start.40) | collective-permute-done | bytes 524320 | tf_op jit(solution)/shard_map/ppermute | solution.py:369
  312.1 2.3 back_sum.28
  314.5 0.9 collective-permute-start.41
  315.4 7.0 %collective-permute-done.37.refs_2_ = bf16[128,2048]{1,0:T(8,128)(2,1)} collective-permute-done((bf16[128,2048]{1,0:T(8,128)(2,1)}, bf16[128,2048]{1,0:T(8,128)(2,1)}, u32[]{:S(2)}, u32[]{:S(2)}) %collective-permute-start.37) | collective-permute-done | bytes 524320 | tf_op jit(solution)/shard_map/ppermute | solution.py:369
  322.4 2.4 back_sum.25
  325.5 1.3 collective-permute-start.34
  326.7 1.2 collective-permute-done.41.refs_2_
  328.0 1.7 back_sum.29
  330.5 3.7 %collective-permute-done.38.refs_2_ = bf16[128,2048]{1,0:T(8,128)(2,1)} collective-permute-done((bf16[128,2048]{1,0:T(8,128)(2,1)}, bf16[128,2048]{1,0:T(8,128)(2,1)}, u32[]{:S(2)}, u32[]{:S(2)}) %collective-permute-start.38) | collective-permute-done | bytes 524320 | tf_op jit(solution)/shard_map/ppermute | solution.py:369
  334.2 1.6 back_sum.26
  335.9 1.7 collective-permute-start.39
  337.6 2.6 back_sum.22.refs_3_
  340.2 2.7 back_sum.23
  342.9 1.3 back_sum.30.refs_3_
  344.1 1.2 collective-permute-done.39.refs_2_
  345.3 1.3 back_sum.31
  (194 shorter events, 30.3 us)
Async XLA Ops:
  0.6 39.1 %collective-permute-start.4 = (bf16[4096,768]{1,0:T(8,128)(2,1)}, bf16[4096,768]{1,0:T(8,128)(2,1)}, u32[]{:S(2)}, u32[]{:S(2)}) collective-permute-start(bf16[4096,768]{1,0:T(8,128)(2,1)} %bitcast.9), channel_id=1, source_target_pairs={{0,1},{1,0},{2,3},{3,2},{4,5},{5,4},{6,7},{7,6},{8,9},{9,8},{10,11... | collective-permute-start | bytes 18874376 | tf_op jit(solution)/shard_map/ppermute | solution.py:369
  1.1 38.6 %collective-permute-start.5 = (bf16[4096,768]{1,0:T(8,128)(2,1)}, bf16[4096,768]{1,0:T(8,128)(2,1)}, u32[]{:S(2)}, u32[]{:S(2)}) collective-permute-start(bf16[4096,768]{1,0:T(8,128)(2,1)} %bitcast.12), channel_id=1, source_target_pairs={{0,1},{1,0},{2,3},{3,2},{4,5},{5,4},{6,7},{7,6},{8,9},{9,8},{10,11... | collective-permute-start | bytes 18874376 | tf_op jit(solution)/shard_map/ppermute | solution.py:369
  1.2 38.5 %collective-permute-start.6 = (bf16[768,4096]{1,0:T(8,128)(2,1)}, bf16[768,4096]{1,0:T(8,128)(2,1)}, u32[]{:S(2)}, u32[]{:S(2)}) collective-permute-start(bf16[768,4096]{1,0:T(8,128)(2,1)} %bitcast.15), channel_id=1, source_target_pairs={{0,1},{1,0},{2,3},{3,2},{4,5},{5,4},{6,7},{7,6},{8,9},{9,8},{10,11... | collective-permute-start | bytes 18874376 | tf_op jit(solution)/shard_map/ppermute | solution.py:369
  2.9 16.2 %collective-permute-start.1 = (bf16[128,2048]{1,0:T(8,128)(2,1)S(1)}, bf16[128,2048]{1,0:T(8,128)(2,1)S(1)}, u32[]{:S(2)}, u32[]{:S(2)}) collective-permute-start(bf16[128,2048]{1,0:T(8,128)(2,1)S(1)} %get-tuple-element.88.refs_1_), channel_id=1, source_target_pairs={{0,4},{1,5},{2,6},{3,7},{4,12},{5,13},{6,14},{7,15},{8,0},{9,1},{1... | collective-permute-start | bytes 1572872 | tf_op jit(solution)/shard_map/ppermute | solution.py:369
  5.6 14.4 %copy-start.57 = (bf16[128,4096]{1,0:T(8,128)(2,1)S(1)}, bf16[128,4096]{1,0:T(8,128)(2,1)}, u32[]{:S(2)}) copy-start(bf16[128,4096]{1,0:T(8,128)(2,1)} %param.8) | copy-start | bytes 3145732
  9.3 10.8 %copy-start.50 = (bf16[96,4096]{1,0:T(8,128)(2,1)}, bf16[96,4096]{1,0:T(8,128)(2,1)S(1)}, u32[]{:S(2)}) copy-start(bf16[96,4096]{1,0:T(8,128)(2,1)S(1)} %get-tuple-element.45.refs_0_) | copy-start | bytes 2359300
  9.4 27.7 %copy-start.40 = (bf16[192,128]{1,0:T(8,128)(2,1)}, bf16[192,128]{1,0:T(8,128)(2,1)S(1)}, u32[]{:S(2)}) copy-start(bf16[192,128]{1,0:T(8,128)(2,1)S(1)} %get-tuple-element.47.pick.mix) | copy-start | bytes 147460
  9.4 29.5 %collective-permute-start.3 = (bf16[96,4096]{1,0:T(8,128)(2,1)}, bf16[96,4096]{1,0:T(8,128)(2,1)}, u32[]{:S(2)}, u32[]{:S(2)}) collective-permute-start(bf16[96,4096]{1,0:T(8,128)(2,1)} %get-tuple-element.49), channel_id=1, source_target_pairs={{0,2},{1,3},{2,0},{3,1},{4,6},{5,7},{6,4},{7,5},{8,10},{9,11},{10,... | collective-permute-start | bytes 2359304 | tf_op jit(solution)/shard_map/ppermute | solution.py:369
  19.2 19.7 %copy-start.31 = (bf16[128,2048]{1,0:T(8,128)(2,1)}, bf16[128,2048]{1,0:T(8,128)(2,1)S(1)}, u32[]{:S(2)}) copy-start(bf16[128,2048]{1,0:T(8,128)(2,1)S(1)} %collective-permute-done.1.refs_1_.refs_0_) | copy-start | bytes 1572868
  19.2 15.3 %collective-permute-start = (bf16[128,2176]{1,0:T(8,128)(2,1)S(1)}, bf16[128,2176]{1,0:T(8,128)(2,1)S(1)}, u32[]{:S(2)}, u32[]{:S(2)}) collective-permute-start(bf16[128,2176]{1,0:T(8,128)(2,1)S(1)} %fusion.1.refs_0_), channel_id=1, source_target_pairs={{0,4},{1,5},{2,6},{3,7},{4,12},{5,13},{6,14},{7,15},{8,0},{9,1},{1... | collective-permute-start | bytes 1671176 | tf_op jit(solution)/shard_map/ppermute | solution.py:369
  20.1 19.6 %copy-start.1 = (bf16[128,2048]{1,0:T(8,128)(2,1)}, bf16[128,2048]{1,0:T(8,128)(2,1)S(1)}, u32[]{:S(2)}) copy-start(bf16[128,2048]{1,0:T(8,128)(2,1)S(1)} %get-tuple-element.86.refs_1_.refs_0_) | copy-start | bytes 1572868
  20.1 19.6 %copy-start.13 = (bf16[128,2048]{1,0:T(8,128)(2,1)}, bf16[128,2048]{1,0:T(8,128)(2,1)S(1)}, u32[]{:S(2)}) copy-start(bf16[128,2048]{1,0:T(8,128)(2,1)S(1)} %get-tuple-element.87.refs_0_) | copy-start | bytes 1572868
  34.5 34.3 %collective-permute-start.9 = (bf16[96,4096]{1,0:T(8,128)(2,1)}, bf16[96,4096]{1,0:T(8,128)(2,1)}, u32[]{:S(2)}, u32[]{:S(2)}) collective-permute-start(bf16[96,4096]{1,0:T(8,128)(2,1)} %get-tuple-element.51), channel_id=1, source_target_pairs={{0,2},{1,3},{2,0},{3,1},{4,6},{5,7},{6,4},{7,5},{8,10},{9,11},{10,... | collective-permute-start | bytes 2359304 | tf_op jit(solution)/shard_map/ppermute | solution.py:369
  38.9 80.5 %copy-start.45 = (bf16[192,128]{1,0:T(8,128)(2,1)}, bf16[192,128]{1,0:T(8,128)(2,1)S(1)}, u32[]{:S(2)}) copy-start(bf16[192,128]{1,0:T(8,128)(2,1)S(1)} %get-tuple-element.60.pick.mix) | copy-start | bytes 147460
  38.9 16.7 %collective-permute-start.2 = (bf16[128,2176]{1,0:T(8,128)(2,1)}, bf16[128,2176]{1,0:T(8,128)(2,1)S(1)}, u32[]{:S(2)}, u32[]{:S(2)}) collective-permute-start(bf16[128,2176]{1,0:T(8,128)(2,1)} %tie.23), channel_id=1, source_target_pairs={{0,4},{1,5},{2,6},{3,7},{4,12},{5,13},{6,14},{7,15},{8,0},{9,1},{1... | collective-permute-start | bytes 1671176 | tf_op jit(solution)/shard_map/ppermute | solution.py:369
  39.8 24.5 %collective-permute-start.7 = (bf16[128,2048]{1,0:T(8,128)(2,1)}, bf16[128,2048]{1,0:T(8,128)(2,1)S(1)}, u32[]{:S(2)}, u32[]{:S(2)}) collective-permute-start(bf16[128,2048]{1,0:T(8,128)(2,1)} %tie.24), channel_id=1, source_target_pairs={{0,4},{1,5},{2,6},{3,7},{4,12},{5,13},{6,14},{7,15},{8,0},{9,1},{1... | collective-permute-start | bytes 1572872 | tf_op jit(solution)/shard_map/ppermute | solution.py:369
  55.6 11.7 %copy-start.25 = (bf16[128,2176]{1,0:T(8,128)(2,1)}, bf16[128,2176]{1,0:T(8,128)(2,1)S(1)}, u32[]{:S(2)}) copy-start(bf16[128,2176]{1,0:T(8,128)(2,1)S(1)} %collective-permute-done.2.refs_0_) | copy-start | bytes 1671172
  67.3 89.5 %copy-start.47 = (bf16[192,128]{1,0:T(8,128)(2,1)}, bf16[192,128]{1,0:T(8,128)(2,1)S(1)}, u32[]{:S(2)}) copy-start(bf16[192,128]{1,0:T(8,128)(2,1)S(1)} %get-tuple-element.72.pick.mix) | copy-start | bytes 147460
  67.3 24.4 %collective-permute-start.8 = (bf16[128,2176]{1,0:T(8,128)(2,1)}, bf16[128,2176]{1,0:T(8,128)(2,1)S(1)}, u32[]{:S(2)}, u32[]{:S(2)}) collective-permute-start(bf16[128,2176]{1,0:T(8,128)(2,1)} %tie.25), channel_id=1, source_target_pairs={{0,4},{1,5},{2,6},{3,7},{4,12},{5,13},{6,14},{7,15},{8,0},{9,1},{1... | collective-permute-start | bytes 1671176 | tf_op jit(solution)/shard_map/ppermute | solution.py:369
  68.2 28.3 %collective-permute-start.11 = (bf16[96,4096]{1,0:T(8,128)(2,1)}, bf16[96,4096]{1,0:T(8,128)(2,1)}, u32[]{:S(2)}, u32[]{:S(2)}) collective-permute-start(bf16[96,4096]{1,0:T(8,128)(2,1)} %copy-done.56), channel_id=1, source_target_pairs={{0,2},{1,3},{2,0},{3,1},{4,6},{5,7},{6,4},{7,5},{8,10},{9,11},{10,... | collective-permute-start | bytes 2359304 | tf_op jit(solution)/shard_map/ppermute | solution.py:369
  68.7 23.0 %collective-permute-start.10 = (bf16[128,2048]{1,0:T(8,128)(2,1)}, bf16[128,2048]{1,0:T(8,128)(2,1)S(1)}, u32[]{:S(2)}, u32[]{:S(2)}) collective-permute-start(bf16[128,2048]{1,0:T(8,128)(2,1)} %tie.26), channel_id=1, source_target_pairs={{0,4},{1,5},{2,6},{3,7},{4,12},{5,13},{6,14},{7,15},{8,0},{9,1},{1... | collective-permute-start | bytes 1572872 | tf_op jit(solution)/shard_map/ppermute | solution.py:369
  72.0 50.4 %collective-permute-start.12 = (bf16[96,4096]{1,0:T(8,128)(2,1)}, bf16[96,4096]{1,0:T(8,128)(2,1)}, u32[]{:S(2)}, u32[]{:S(2)}) collective-permute-start(bf16[96,4096]{1,0:T(8,128)(2,1)} %copy-done.55), channel_id=1, source_target_pairs={{0,2},{1,3},{2,0},{3,1},{4,6},{5,7},{6,4},{7,5},{8,10},{9,11},{10,... | collective-permute-start | bytes 2359304 | tf_op jit(solution)/shard_map/ppermute | solution.py:369
  95.4 30.3 %collective-permute-start.13 = (bf16[96,4096]{1,0:T(8,128)(2,1)}, bf16[96,4096]{1,0:T(8,128)(2,1)}, u32[]{:S(2)}, u32[]{:S(2)}) collective-permute-start(bf16[96,4096]{1,0:T(8,128)(2,1)} %get-tuple-element.55), channel_id=1, source_target_pairs={{0,2},{1,3},{2,0},{3,1},{4,6},{5,7},{6,4},{7,5},{8,10},{9,11},{10,... | collective-permute-start | bytes 2359304 | tf_op jit(solution)/shard_map/ppermute | solution.py:369
  96.5 16.0 %collective-permute-start.15 = (bf16[128,2048]{1,0:T(8,128)(2,1)}, bf16[128,2048]{1,0:T(8,128)(2,1)S(1)}, u32[]{:S(2)}, u32[]{:S(2)}) collective-permute-start(bf16[128,2048]{1,0:T(8,128)(2,1)} %tie.29), channel_id=1, source_target_pairs={{0,4},{1,5},{2,6},{3,7},{4,12},{5,13},{6,14},{7,15},{8,0},{9,1},{1... | collective-permute-start | bytes 1572872 | tf_op jit(solution)/shard_map/ppermute | solution.py:369
  96.9 22.5 %collective-permute-start.14 = (bf16[128,2048]{1,0:T(8,128)(2,1)}, bf16[128,2048]{1,0:T(8,128)(2,1)S(1)}, u32[]{:S(2)}, u32[]{:S(2)}) collective-permute-start(bf16[128,2048]{1,0:T(8,128)(2,1)} %tie.27), channel_id=1, source_target_pairs={{0,4},{1,5},{2,6},{3,7},{4,12},{5,13},{6,14},{7,15},{8,0},{9,1},{1... | collective-permute-start | bytes 1572872 | tf_op jit(solution)/shard_map/ppermute | solution.py:369
  112.5 9.8 %copy-start.29 = (bf16[128,2048]{1,0:T(8,128)(2,1)}, bf16[128,2048]{1,0:T(8,128)(2,1)S(1)}, u32[]{:S(2)}) copy-start(bf16[128,2048]{1,0:T(8,128)(2,1)S(1)} %collective-permute-done.15.refs_1_.refs_0_) | copy-start | bytes 1572868
  120.8 35.4 %collective-permute-start.16 = (bf16[96,4096]{1,0:T(8,128)(2,1)S(1)}, bf16[96,4096]{1,0:T(8,128)(2,1)}, u32[]{:S(2)}, u32[]{:S(2)}) collective-permute-start(bf16[96,4096]{1,0:T(8,128)(2,1)S(1)} %get-tuple-element.62), channel_id=1, source_target_pairs={{0,2},{1,3},{2,0},{3,1},{4,6},{5,7},{6,4},{7,5},{8,10},{9,11},{10,... | collective-permute-start | bytes 2359304 | tf_op jit(solution)/shard_map/ppermute | solution.py:369
  121.5 35.3 %collective-permute-start.20 = (bf16[128,2048]{1,0:T(8,128)(2,1)}, bf16[128,2048]{1,0:T(8,128)(2,1)S(1)}, u32[]{:S(2)}, u32[]{:S(2)}) collective-permute-start(bf16[128,2048]{1,0:T(8,128)(2,1)} %tie.33), channel_id=1, source_target_pairs={{0,4},{1,5},{2,6},{3,7},{4,12},{5,13},{6,14},{7,15},{8,0},{9,1},{1... | collective-permute-start | bytes 1572872 | tf_op jit(solution)/shard_map/ppermute | solution.py:369
  122.4 34.4 %collective-permute-start.22 = (bf16[128,2048]{1,0:T(8,128)(2,1)}, bf16[128,2048]{1,0:T(8,128)(2,1)S(1)}, u32[]{:S(2)}, u32[]{:S(2)}) collective-permute-start(bf16[128,2048]{1,0:T(8,128)(2,1)} %tie.35), channel_id=1, source_target_pairs={{0,4},{1,5},{2,6},{3,7},{4,12},{5,13},{6,14},{7,15},{8,0},{9,1},{1... | collective-permute-start | bytes 1572872 | tf_op jit(solution)/shard_map/ppermute | solution.py:369
  156.2 16.8 %collective-permute-start.17 = (bf16[96,4096]{1,0:T(8,128)(2,1)}, bf16[96,4096]{1,0:T(8,128)(2,1)S(1)}, u32[]{:S(2)}, u32[]{:S(2)}) collective-permute-start(bf16[96,4096]{1,0:T(8,128)(2,1)} %tie.30), channel_id=1, source_target_pairs={{0,2},{1,3},{2,0},{3,1},{4,6},{5,7},{6,4},{7,5},{8,10},{9,11},{10,... | collective-permute-start | bytes 2359304 | tf_op jit(solution)/shard_map/ppermute | solution.py:369
  158.4 18.8 %collective-permute-start.21 = (bf16[128,2048]{1,0:T(8,128)(2,1)}, bf16[128,2048]{1,0:T(8,128)(2,1)}, u32[]{:S(2)}, u32[]{:S(2)}) collective-permute-start(bf16[128,2048]{1,0:T(8,128)(2,1)} %tie.34), channel_id=1, source_target_pairs={{0,4},{1,5},{2,6},{3,7},{4,12},{5,13},{6,14},{7,15},{8,0},{9,1},{1... | collective-permute-start | bytes 1572872 | tf_op jit(solution)/shard_map/ppermute | solution.py:369
  159.4 15.1 %copy-start.16 = (bf16[96,4096]{1,0:T(8,128)(2,1)S(1)}, bf16[96,4096]{1,0:T(8,128)(2,1)}, u32[]{:S(2)}) copy-start(bf16[96,4096]{1,0:T(8,128)(2,1)} %get-tuple-element.70.refs_0_) | copy-start | bytes 2359300
  159.4 53.4 %collective-permute-start.23 = (bf16[128,2048]{1,0:T(8,128)(2,1)}, bf16[128,2048]{1,0:T(8,128)(2,1)}, u32[]{:S(2)}, u32[]{:S(2)}) collective-permute-start(bf16[128,2048]{1,0:T(8,128)(2,1)} %tie.36), channel_id=1, source_target_pairs={{0,4},{1,5},{2,6},{3,7},{4,12},{5,13},{6,14},{7,15},{8,0},{9,1},{1... | collective-permute-start | bytes 1572872 | tf_op jit(solution)/shard_map/ppermute | solution.py:369
  173.9 38.9 %copy-start = (bf16[96,4096]{1,0:T(8,128)(2,1)S(1)}, bf16[96,4096]{1,0:T(8,128)(2,1)}, u32[]{:S(2)}) copy-start(bf16[96,4096]{1,0:T(8,128)(2,1)} %get-tuple-element.56.refs_2_.refs_0_) | copy-start | bytes 2359300
  173.9 46.8 %collective-permute-start.18 = (bf16[96,4096]{1,0:T(8,128)(2,1)}, bf16[96,4096]{1,0:T(8,128)(2,1)S(1)}, u32[]{:S(2)}, u32[]{:S(2)}) collective-permute-start(bf16[96,4096]{1,0:T(8,128)(2,1)} %tie.31), channel_id=1, source_target_pairs={{0,2},{1,3},{2,0},{3,1},{4,6},{5,7},{6,4},{7,5},{8,10},{9,11},{10,... | collective-permute-start | bytes 2359304 | tf_op jit(solution)/shard_map/ppermute | solution.py:369
  175.6 43.5 %copy-start.6 = (bf16[96,4096]{1,0:T(8,128)(2,1)S(1)}, bf16[96,4096]{1,0:T(8,128)(2,1)}, u32[]{:S(2)}) copy-start(bf16[96,4096]{1,0:T(8,128)(2,1)} %copy-done.4) | copy-start | bytes 2359300
  177.2 43.4 %collective-permute-start.29 = (bf16[128,2048]{1,0:T(8,128)(2,1)}, bf16[128,2048]{1,0:T(8,128)(2,1)}, u32[]{:S(2)}, u32[]{:S(2)}) collective-permute-start(bf16[128,2048]{1,0:T(8,128)(2,1)} %tie.39), channel_id=1, source_target_pairs={{0,8},{1,9},{2,10},{3,11},{4,0},{5,1},{6,2},{7,3},{8,12},{9,13},{1... | collective-permute-start | bytes 1572872 | tf_op jit(solution)/shard_map/ppermute | solution.py:369
  217.1 12.6 %collective-permute-start.24 = (bf16[96,4096]{1,0:T(8,128)(2,1)}, bf16[96,4096]{1,0:T(8,128)(2,1)}, u32[]{:S(2)}, u32[]{:S(2)}) collective-permute-start(bf16[96,4096]{1,0:T(8,128)(2,1)} %get-tuple-element.67), channel_id=1, source_target_pairs={{0,2},{1,3},{2,0},{3,1},{4,6},{5,7},{6,4},{7,5},{8,10},{9,11},{10,... | collective-permute-start | bytes 2359304 | tf_op jit(solution)/shard_map/ppermute | solution.py:369
  218.6 19.5 %collective-permute-start.32 = (bf16[96,4096]{1,0:T(8,128)(2,1)}, bf16[96,4096]{1,0:T(8,128)(2,1)}, u32[]{:S(2)}, u32[]{:S(2)}) collective-permute-start(bf16[96,4096]{1,0:T(8,128)(2,1)} %copy-done.53), channel_id=1, source_target_pairs={{0,2},{1,3},{2,0},{3,1},{4,6},{5,7},{6,4},{7,5},{8,10},{9,11},{10,... | collective-permute-start | bytes 2359304 | tf_op jit(solution)/shard_map/ppermute | solution.py:369
  220.6 11.0 %collective-permute-start.26 = (bf16[128,2048]{1,0:T(8,128)(2,1)}, bf16[128,2048]{1,0:T(8,128)(2,1)}, u32[]{:S(2)}, u32[]{:S(2)}) collective-permute-start(bf16[128,2048]{1,0:T(8,128)(2,1)} %tie.38), channel_id=1, source_target_pairs={{0,8},{1,9},{2,10},{3,11},{4,0},{5,1},{6,2},{7,3},{8,12},{9,13},{1... | collective-permute-start | bytes 1572872 | tf_op jit(solution)/shard_map/ppermute | solution.py:369
  224.7 13.4 %collective-permute-start.30 = (bf16[128,2048]{1,0:T(8,128)(2,1)}, bf16[128,2048]{1,0:T(8,128)(2,1)}, u32[]{:S(2)}, u32[]{:S(2)}) collective-permute-start(bf16[128,2048]{1,0:T(8,128)(2,1)} %back_sum.20), channel_id=1, source_target_pairs={{0,8},{1,9},{2,10},{3,11},{4,0},{5,1},{6,2},{7,3},{8,12},{9,13},{1... | collective-permute-start | bytes 1572872 | tf_op jit(solution)/shard_map/ppermute | solution.py:369
  229.6 38.8 %collective-permute-start.25 = (bf16[96,4096]{1,0:T(8,128)(2,1)}, bf16[96,4096]{1,0:T(8,128)(2,1)S(1)}, u32[]{:S(2)}, u32[]{:S(2)}) collective-permute-start(bf16[96,4096]{1,0:T(8,128)(2,1)} %tie.37), channel_id=1, source_target_pairs={{0,2},{1,3},{2,0},{3,1},{4,6},{5,7},{6,4},{7,5},{8,10},{9,11},{10,... | collective-permute-start | bytes 2359304 | tf_op jit(solution)/shard_map/ppermute | solution.py:369
  230.9 46.4 %collective-permute-start.19 = (bf16[96,4096]{1,0:T(8,128)(2,1)}, bf16[96,4096]{1,0:T(8,128)(2,1)S(1)}, u32[]{:S(2)}, u32[]{:S(2)}) collective-permute-start(bf16[96,4096]{1,0:T(8,128)(2,1)} %tie.32), channel_id=1, source_target_pairs={{0,2},{1,3},{2,0},{3,1},{4,6},{5,7},{6,4},{7,5},{8,10},{9,11},{10,... | collective-permute-start | bytes 2359304 | tf_op jit(solution)/shard_map/ppermute | solution.py:369
  235.8 38.7 %collective-permute-start.27 = (bf16[128,2048]{1,0:T(8,128)(2,1)}, bf16[128,2048]{1,0:T(8,128)(2,1)}, u32[]{:S(2)}, u32[]{:S(2)}) collective-permute-start(bf16[128,2048]{1,0:T(8,128)(2,1)} %back_sum.17), channel_id=1, source_target_pairs={{0,8},{1,9},{2,10},{3,11},{4,0},{5,1},{6,2},{7,3},{8,12},{9,13},{1... | collective-permute-start | bytes 1572872 | tf_op jit(solution)/shard_map/ppermute | solution.py:369
  269.3 20.7 %collective-permute-start.35 = (bf16[96,4096]{1,0:T(8,128)(2,1)}, bf16[96,4096]{1,0:T(8,128)(2,1)S(1)}, u32[]{:S(2)}, u32[]{:S(2)}) collective-permute-start(bf16[96,4096]{1,0:T(8,128)(2,1)} %tie.42), channel_id=1, source_target_pairs={{0,2},{1,3},{2,0},{3,1},{4,6},{5,7},{6,4},{7,5},{8,10},{9,11},{10,... | collective-permute-start | bytes 2359304 | tf_op jit(solution)/shard_map/ppermute | solution.py:369
  274.5 15.4 %copy-start.17 = (bf16[96,4096]{1,0:T(8,128)(2,1)S(1)}, bf16[96,4096]{1,0:T(8,128)(2,1)}, u32[]{:S(2)}) copy-start(bf16[96,4096]{1,0:T(8,128)(2,1)} %get-tuple-element.85.refs_0_) | copy-start | bytes 2359300
  274.5 15.4 %copy-start.44 = (bf16[192,128]{1,0:T(8,128)(2,1)S(1)}, bf16[192,128]{1,0:T(8,128)(2,1)}, u32[]{:S(2)}) copy-start(bf16[192,128]{1,0:T(8,128)(2,1)} %copy-done.42) | copy-start | bytes 147460
  274.5 16.7 %collective-permute-start.31 = (bf16[128,2048]{1,0:T(8,128)(2,1)}, bf16[128,2048]{1,0:T(8,128)(2,1)}, u32[]{:S(2)}, u32[]{:S(2)}) collective-permute-start(bf16[128,2048]{1,0:T(8,128)(2,1)} %back_sum.21), channel_id=1, source_target_pairs={{0,8},{1,9},{2,10},{3,11},{4,0},{5,1},{6,2},{7,3},{8,12},{9,13},{1... | collective-permute-start | bytes 1572872 | tf_op jit(solution)/shard_map/ppermute | solution.py:369
  277.3 23.6 %collective-permute-start.28 = (bf16[128,2048]{1,0:T(8,128)(2,1)}, bf16[128,2048]{1,0:T(8,128)(2,1)}, u32[]{:S(2)}, u32[]{:S(2)}) collective-permute-start(bf16[128,2048]{1,0:T(8,128)(2,1)} %back_sum.18), channel_id=1, source_target_pairs={{0,8},{1,9},{2,10},{3,11},{4,0},{5,1},{6,2},{7,3},{8,12},{9,13},{1... | collective-permute-start | bytes 1572872 | tf_op jit(solution)/shard_map/ppermute | solution.py:369
  278.1 27.2 %collective-permute-start.33 = (bf16[96,4096]{1,0:T(8,128)(2,1)}, bf16[96,4096]{1,0:T(8,128)(2,1)S(1)}, u32[]{:S(2)}, u32[]{:S(2)}) collective-permute-start(bf16[96,4096]{1,0:T(8,128)(2,1)} %tie.40), channel_id=1, source_target_pairs={{0,2},{1,3},{2,0},{3,1},{4,6},{5,7},{6,4},{7,5},{8,10},{9,11},{10,... | collective-permute-start | bytes 2359304 | tf_op jit(solution)/shard_map/ppermute | solution.py:369
  291.2 20.9 %collective-permute-start.40 = (bf16[128,2048]{1,0:T(8,128)(2,1)}, bf16[128,2048]{1,0:T(8,128)(2,1)}, u32[]{:S(2)}, u32[]{:S(2)}) collective-permute-start(bf16[128,2048]{1,0:T(8,128)(2,1)} %tie.45), channel_id=1, source_target_pairs={{0,8},{1,9},{2,10},{3,11},{4,0},{5,1},{6,2},{7,3},{8,12},{9,13},{1... | collective-permute-start | bytes 1572872 | tf_op jit(solution)/shard_map/ppermute | solution.py:369
  292.5 19.7 %copy-start.23 = (bf16[96,4096]{1,0:T(8,128)(2,1)S(1)}, bf16[96,4096]{1,0:T(8,128)(2,1)}, u32[]{:S(2)}) copy-start(bf16[96,4096]{1,0:T(8,128)(2,1)} %get-tuple-element.84.refs_0_) | copy-start | bytes 2359300
  292.5 19.7 %copy-start.48 = (bf16[192,128]{1,0:T(8,128)(2,1)S(1)}, bf16[192,128]{1,0:T(8,128)(2,1)}, u32[]{:S(2)}) copy-start(bf16[192,128]{1,0:T(8,128)(2,1)} %copy-done.47) | copy-start | bytes 147460
  300.9 21.5 %collective-permute-start.37 = (bf16[128,2048]{1,0:T(8,128)(2,1)}, bf16[128,2048]{1,0:T(8,128)(2,1)}, u32[]{:S(2)}, u32[]{:S(2)}) collective-permute-start(bf16[128,2048]{1,0:T(8,128)(2,1)} %tie.44), channel_id=1, source_target_pairs={{0,8},{1,9},{2,10},{3,11},{4,0},{5,1},{6,2},{7,3},{8,12},{9,13},{1... | collective-permute-start | bytes 1572872 | tf_op jit(solution)/shard_map/ppermute | solution.py:369
  301.8 24.9 %collective-permute-start.36 = (bf16[96,4096]{1,0:T(8,128)(2,1)}, bf16[96,4096]{1,0:T(8,128)(2,1)}, u32[]{:S(2)}, u32[]{:S(2)}) collective-permute-start(bf16[96,4096]{1,0:T(8,128)(2,1)} %tie.43), channel_id=1, source_target_pairs={{0,2},{1,3},{2,0},{3,1},{4,6},{5,7},{6,4},{7,5},{8,10},{9,11},{10,... | collective-permute-start | bytes 2359304 | tf_op jit(solution)/shard_map/ppermute | solution.py:369
  305.3 19.4 %copy-start.12 = (bf16[96,4096]{1,0:T(8,128)(2,1)}, bf16[96,4096]{1,0:T(8,128)(2,1)S(1)}, u32[]{:S(2)}) copy-start(bf16[96,4096]{1,0:T(8,128)(2,1)S(1)} %collective-permute-done.33.refs_1_) | copy-start | bytes 2359300
  314.5 13.5 %copy-start.22 = (bf16[96,4096]{1,0:T(8,128)(2,1)S(1)}, bf16[96,4096]{1,0:T(8,128)(2,1)}, u32[]{:S(2)}) copy-start(bf16[96,4096]{1,0:T(8,128)(2,1)} %get-tuple-element.81.refs_0_) | copy-start | bytes 2359300
  314.5 13.5 %copy-start.46 = (bf16[192,128]{1,0:T(8,128)(2,1)S(1)}, bf16[192,128]{1,0:T(8,128)(2,1)}, u32[]{:S(2)}) copy-start(bf16[192,128]{1,0:T(8,128)(2,1)} %copy-done.45) | copy-start | bytes 147460
  314.5 13.5 %collective-permute-start.41 = (bf16[128,2048]{1,0:T(8,128)(2,1)}, bf16[128,2048]{1,0:T(8,128)(2,1)}, u32[]{:S(2)}, u32[]{:S(2)}) collective-permute-start(bf16[128,2048]{1,0:T(8,128)(2,1)} %back_sum.28), channel_id=1, source_target_pairs={{0,8},{1,9},{2,10},{3,11},{4,0},{5,1},{6,2},{7,3},{8,12},{9,13},{1... | collective-permute-start | bytes 1572872 | tf_op jit(solution)/shard_map/ppermute | solution.py:369
  324.7 9.5 %collective-permute-start.38 = (bf16[128,2048]{1,0:T(8,128)(2,1)}, bf16[128,2048]{1,0:T(8,128)(2,1)}, u32[]{:S(2)}, u32[]{:S(2)}) collective-permute-start(bf16[128,2048]{1,0:T(8,128)(2,1)} %back_sum.25), channel_id=1, source_target_pairs={{0,8},{1,9},{2,10},{3,11},{4,0},{5,1},{6,2},{7,3},{8,12},{9,13},{1... | collective-permute-start | bytes 1572872 | tf_op jit(solution)/shard_map/ppermute | solution.py:369
  325.5 17.4 %collective-permute-start.34 = (bf16[96,4096]{1,0:T(8,128)(2,1)}, bf16[96,4096]{1,0:T(8,128)(2,1)S(1)}, u32[]{:S(2)}, u32[]{:S(2)}) collective-permute-start(bf16[96,4096]{1,0:T(8,128)(2,1)} %tie.41), channel_id=1, source_target_pairs={{0,2},{1,3},{2,0},{3,1},{4,6},{5,7},{6,4},{7,5},{8,10},{9,11},{10,... | collective-permute-start | bytes 2359304 | tf_op jit(solution)/shard_map/ppermute | solution.py:369
  328.0 9.6 %copy-start.3 = (bf16[96,4096]{1,0:T(8,128)(2,1)S(1)}, bf16[96,4096]{1,0:T(8,128)(2,1)}, u32[]{:S(2)}) copy-start(bf16[96,4096]{1,0:T(8,128)(2,1)} %copy-done.2) | copy-start | bytes 2359300
  329.7 13.2 %collective-permute-start.42 = (bf16[128,2048]{1,0:T(8,128)(2,1)S(1)}, bf16[128,2048]{1,0:T(8,128)(2,1)S(1)}, u32[]{:S(2)}, u32[]{:S(2)}) collective-permute-start(bf16[128,2048]{1,0:T(8,128)(2,1)S(1)} %back_sum.29), channel_id=1, source_target_pairs={{0,8},{1,9},{2,10},{3,11},{4,0},{5,1},{6,2},{7,3},{8,12},{9,13},{1... | collective-permute-start | bytes 1572872 | tf_op jit(solution)/shard_map/ppermute | solution.py:369
  335.9 9.5 %collective-permute-start.39 = (bf16[128,2048]{1,0:T(8,128)(2,1)S(1)}, bf16[128,2048]{1,0:T(8,128)(2,1)S(1)}, u32[]{:S(2)}, u32[]{:S(2)}) collective-permute-start(bf16[128,2048]{1,0:T(8,128)(2,1)S(1)} %back_sum.26), channel_id=1, source_target_pairs={{0,8},{1,9},{2,10},{3,11},{4,0},{5,1},{6,2},{7,3},{8,12},{9,13},{1... | collective-permute-start | bytes 1572872 | tf_op jit(solution)/shard_map/ppermute | solution.py:369
  (37 other events, 67.7 us)

commit v5 on v4

--- a/solution.py
+++ b/solution.py
@@ -460,7 +460,7 @@
     choose("cot", last, [outs[0]])
     moe_out, steps = combine(outs, True, far)
     deps = [came("y", 2 * zs + 1)] if ys == 2 else []
-    grads = expert_backward(own["cot"] + other["cot"], saved, gate_mats, up_mats, down_mats, cap, deps + steps[0] + steps[1][:1])
+    grads = expert_backward(own["cot"] + other["cot"], saved, gate_mats, up_mats, down_mats, cap, deps + steps[0] + steps[1])
     token_grad, _ = combine(grads, False)
     return (moe_out, token_grad)
 

time: 348 us -> 349 us (level)
  transfers between devices with their start and end apart: 43 -> 43, of which waited for: 19 -> 20; matrix products, arithmetic and copies ran while one was open for 1% -> 1% of each run, Pallas kernels for 29% -> 28%
where the time goes in v5:
time: 349 us; the launch traced here: 348 us
  waiting for transfers between devices  180 us (52%)
  Pallas kernels  99.8 us (29%)
  starting transfers between devices  44.3 us (13%)
  local copies, waits for them, and re-layouts  21 us (6%)
    ppermute x43, waiting for transfers between devices, permute(): return lax.ppermute(value, 'wide', perm)  180 us
    pallas_call x2, Pallas kernels, expert_call(): pl.pallas_call(body, grid=(2, firsts + seconds), in_specs=specs, out_spec...  60.9 us
    ppermute x43, starting transfers between devices, permute(): return lax.ppermute(value, 'wide', perm)  44.3 us
    pallas_call x16, Pallas kernels, back_sum(): pl.pallas_call(body, grid=(1,), in_specs=specs, out_specs=pl.BlockSpec((r...  27.9 us
    unnamed x116, local copies, waits for them, and re-layouts  19.7 us
  transfers between devices with their start and end apart: 43, of which 20 were waited for; matrix products, arithmetic and copies ran while one was open for 1% of the time, Pallas kernels for 28%

profile of v5, /device:TPU:0, one launch (start us, length us, event | category | flops | bytes accessed | tf_op | source)
XLA Modules:
  0.0 347.6 jit_solution(16640405393760415239)
XLA Ops:
  1.7 1.3 fusion.6
  2.9 2.7 collective-permute-start.1
  7.2 2.1 first_choice.4
  9.4 1.5 collective-permute-start.3
  10.9 8.3 %collective-permute-done.1.refs_1_.refs_0_ = bf16[128,2048]{1,0:T(8,128)(2,1)S(1)} collective-permute-done((bf16[128,2048]{1,0:T(8,128)(2,1)S(1)}, bf16[128,2048]{1,0:T(8,128)(2,1)S(1)}, u32[]{:S(2)}, u32[]{:S(2)}) %collective-permute-start.1) | collective-permute-done | bytes 524320 | tf_op jit(solution)/shard_map/ppermute | solution.py:369
  20.2 1.5 next_choice.4
  21.6 1.0 copy-done.36
  22.6 11.9 %collective-permute-done.refs_0_ = bf16[128,2176]{1,0:T(8,128)(2,1)S(1)} collective-permute-done((bf16[128,2176]{1,0:T(8,128)(2,1)S(1)}, bf16[128,2176]{1,0:T(8,128)(2,1)S(1)}, u32[]{:S(2)}, u32[]{:S(2)}) %collective-permute-start) | collective-permute-done | bytes 557088 | tf_op jit(solution)/shard_map/ppermute | solution.py:369
  34.5 1.4 collective-permute-start.9
  35.8 1.2 first_choice.5
  38.0 0.9 copy-done.54
  39.8 3.4 collective-permute-start.7
  43.2 12.4 %collective-permute-done.2.refs_0_ = bf16[128,2176]{1,0:T(8,128)(2,1)S(1)} collective-permute-done((bf16[128,2176]{1,0:T(8,128)(2,1)}, bf16[128,2176]{1,0:T(8,128)(2,1)S(1)}, u32[]{:S(2)}, u32[]{:S(2)}) %collective-permute-start.2) | collective-permute-done | bytes 557088 | tf_op jit(solution)/shard_map/ppermute | solution.py:369
  55.6 8.7 %collective-permute-done.7.refs_1_.refs_0_ = bf16[128,2048]{1,0:T(8,128)(2,1)S(1)} collective-permute-done((bf16[128,2048]{1,0:T(8,128)(2,1)}, bf16[128,2048]{1,0:T(8,128)(2,1)S(1)}, u32[]{:S(2)}, u32[]{:S(2)}) %collective-permute-start.7) | collective-permute-done | bytes 524320 | tf_op jit(solution)/shard_map/ppermute | solution.py:369
  64.3 1.2 first_choice.6
  66.4 0.9 copy-done.55
  68.7 3.3 collective-permute-start.10
  72.0 1.5 collective-permute-start.12
  73.5 18.2 %collective-permute-done.10.refs_1_ = bf16[128,2048]{1,0:T(8,128)(2,1)S(1)} collective-permute-done((bf16[128,2048]{1,0:T(8,128)(2,1)}, bf16[128,2048]{1,0:T(8,128)(2,1)S(1)}, u32[]{:S(2)}, u32[]{:S(2)}) %collective-permute-start.10) | collective-permute-done | bytes 524320 | tf_op jit(solution)/shard_map/ppermute | solution.py:369
  91.7 2.1 first_choice.7
  93.9 0.9 copy-done.13
  95.4 1.1 collective-permute-start.13
  96.8 3.3 collective-permute-start.14
  100.1 12.4 %collective-permute-done.15.refs_1_.refs_0_ = bf16[128,2048]{1,0:T(8,128)(2,1)S(1)} collective-permute-done((bf16[128,2048]{1,0:T(8,128)(2,1)}, bf16[128,2048]{1,0:T(8,128)(2,1)S(1)}, u32[]{:S(2)}, u32[]{:S(2)}) %collective-permute-start.15) | collective-permute-done | bytes 524320 | tf_op jit(solution)/shard_map/ppermute | solution.py:369
  112.5 6.8 %collective-permute-done.14.refs_0_ = bf16[128,2048]{1,0:T(8,128)(2,1)S(1)} collective-permute-done((bf16[128,2048]{1,0:T(8,128)(2,1)}, bf16[128,2048]{1,0:T(8,128)(2,1)S(1)}, u32[]{:S(2)}, u32[]{:S(2)}) %collective-permute-start.14) | collective-permute-done | bytes 524320 | tf_op jit(solution)/shard_map/ppermute | solution.py:369
  121.4 0.9 collective-permute-start.22
  122.3 3.3 collective-permute-start.20
  125.6 30.5 %expert_forward.1 = (bf16[96,4096]{1,0:T(8,128)(2,1)}, bf16[96,4096]{1,0:T(8,128)(2,1)}, bf16[96,4096]{1,0:T(8,128)(2,1)}, bf16[96,4096]{1,0:T(8,128)(2,1)}, bf1...) custom-call(bf16[96,4096]{1,0:T(8,128)(2,1)} %copy-done.49, ...), custom_call_target="tpu_custom_call" | custom-call | flops 14495514624 | bytes 50331648 | tf_op jit(solution)/shard_map/expert_forward/pallas_call | solution.py:225
  160.1 12.7 %collective-permute-done.17.refs_1_ = bf16[96,4096]{1,0:T(8,128)(2,1)S(1)} collective-permute-done((bf16[96,4096]{1,0:T(8,128)(2,1)}, bf16[96,4096]{1,0:T(8,128)(2,1)S(1)}, u32[]{:S(2)}, u32[]{:S(2)}) %collective-permute-start.17) | collective-permute-done | bytes 786464 | tf_op jit(solution)/shard_map/ppermute | solution.py:369
  174.4 1.1 copy-done.6
  178.6 34.1 %collective-permute-done.23.refs_1_ = bf16[128,2048]{1,0:T(8,128)(2,1)} collective-permute-done((bf16[128,2048]{1,0:T(8,128)(2,1)}, bf16[128,2048]{1,0:T(8,128)(2,1)}, u32[]{:S(2)}, u32[]{:S(2)}) %collective-permute-start.23) | collective-permute-done | bytes 524320 | tf_op jit(solution)/shard_map/ppermute | solution.py:369
  213.6 1.8 next_choice.6
  216.2 1.5 collective-permute-start.24
  218.2 2.9 back_sum.20
  221.1 1.0 collective-permute-done.26.refs_2_.refs_18_
  222.2 1.5 back_sum.17
  223.7 0.9 collective-permute-start.27
  224.6 4.8 %collective-permute-done.24.refs_1_.refs_7_ = bf16[96,4096]{1,0:T(8,128)(2,1)S(1)} collective-permute-done((bf16[96,4096]{1,0:T(8,128)(2,1)S(1)}, bf16[96,4096]{1,0:T(8,128)(2,1)S(1)}, u32[]{:S(2)}, u32[]{:S(2)}) %collective-permute-start.24) | collective-permute-done | bytes 786464 | tf_op jit(solution)/shard_map/ppermute | solution.py:369
  230.8 1.5 collective-permute-start.19
  232.3 5.6 %collective-permute-done.32.refs_6_ = bf16[96,4096]{1,0:T(8,128)(2,1)} collective-permute-done((bf16[96,4096]{1,0:T(8,128)(2,1)}, bf16[96,4096]{1,0:T(8,128)(2,1)}, u32[]{:S(2)}, u32[]{:S(2)}) %collective-permute-start.32) | collective-permute-done | bytes 786464 | tf_op jit(solution)/shard_map/ppermute | solution.py:369
  237.9 30.4 %expert_backward.1 = (bf16[96,4096]{1,0:T(8,128)(2,1)}, bf16[96,4096]{1,0:T(8,128)(2,1)}, bf16[96,4096]{1,0:T(8,128)(2,1)}, bf16[96,4096]{1,0:T(8,128)(2,1)}, bf...) custom-call(bf16[96,4096]{1,0:T(8,128)(2,1)} %copy-done.36, ...), custom_call_target="tpu_custom_call" | custom-call | flops 14495514624 | bytes 50331648 | tf_op jit(solution)/shard_map/expert_backward/pallas_call | solution.py:225
  269.7 1.1 copy-done.10
  270.9 2.7 back_sum.21
  273.7 2.6 back_sum.18
  276.4 1.5 collective-permute-start.28
  279.3 10.6 %collective-permute-done.35.refs_1_ = bf16[96,4096]{1,0:T(8,128)(2,1)S(1)} collective-permute-done((bf16[96,4096]{1,0:T(8,128)(2,1)}, bf16[96,4096]{1,0:T(8,128)(2,1)S(1)}, u32[]{:S(2)}, u32[]{:S(2)}) %collective-permute-start.35) | collective-permute-done | bytes 786464 | tf_op jit(solution)/shard_map/ppermute | solution.py:369
  292.4 7.6 %collective-permute-done.28.refs_2_.refs_1_ = bf16[128,2048]{1,0:T(8,128)(2,1)} collective-permute-done((bf16[128,2048]{1,0:T(8,128)(2,1)}, bf16[128,2048]{1,0:T(8,128)(2,1)}, u32[]{:S(2)}, u32[]{:S(2)}) %collective-permute-start.28) | collective-permute-done | bytes 524320 | tf_op jit(solution)/shard_map/ppermute | solution.py:369
  300.9 1.4 collective-permute-start.36
  302.3 2.9 collective-permute-done.33.refs_1_
  305.2 6.0 %collective-permute-done.40.refs_2_ = bf16[128,2048]{1,0:T(8,128)(2,1)} collective-permute-done((bf16[128,2048]{1,0:T(8,128)(2,1)}, bf16[128,2048]{1,0:T(8,128)(2,1)}, u32[]{:S(2)}, u32[]{:S(2)}) %collective-permute-start.40) | collective-permute-done | bytes 524320 | tf_op jit(solution)/shard_map/ppermute | solution.py:369
  311.3 2.4 back_sum.28
  314.5 7.6 %collective-permute-done.37.refs_2_ = bf16[128,2048]{1,0:T(8,128)(2,1)} collective-permute-done((bf16[128,2048]{1,0:T(8,128)(2,1)}, bf16[128,2048]{1,0:T(8,128)(2,1)}, u32[]{:S(2)}, u32[]{:S(2)}) %collective-permute-start.37) | collective-permute-done | bytes 524320 | tf_op jit(solution)/shard_map/ppermute | solution.py:369
  322.1 2.3 back_sum.25
  326.2 1.5 collective-permute-done.41.refs_2_
  327.7 1.7 back_sum.29
  329.4 0.9 collective-permute-start.42
  330.4 4.2 %collective-permute-done.38.refs_2_ = bf16[128,2048]{1,0:T(8,128)(2,1)} collective-permute-done((bf16[128,2048]{1,0:T(8,128)(2,1)}, bf16[128,2048]{1,0:T(8,128)(2,1)}, u32[]{:S(2)}, u32[]{:S(2)}) %collective-permute-start.38) | collective-permute-done | bytes 524320 | tf_op jit(solution)/shard_map/ppermute | solution.py:369
  334.6 1.6 back_sum.26
  336.2 1.2 collective-permute-start.39
  337.4 2.6 back_sum.22.refs_3_
  340.0 2.7 back_sum.23
  342.7 1.3 back_sum.30.refs_3_
  344.0 2.3 collective-permute-done.39.refs_2_
  346.3 1.3 back_sum.31
  (194 shorter events, 31.9 us)
Async XLA Ops:
  0.6 39.1 %collective-permute-start.4 = (bf16[4096,768]{1,0:T(8,128)(2,1)}, bf16[4096,768]{1,0:T(8,128)(2,1)}, u32[]{:S(2)}, u32[]{:S(2)}) collective-permute-start(bf16[4096,768]{1,0:T(8,128)(2,1)} %bitcast.9), channel_id=1, source_target_pairs={{0,1},{1,0},{2,3},{3,2},{4,5},{5,4},{6,7},{7,6},{8,9},{9,8},{10,11... | collective-permute-start | bytes 18874376 | tf_op jit(solution)/shard_map/ppermute | solution.py:369
  1.1 38.6 %collective-permute-start.5 = (bf16[4096,768]{1,0:T(8,128)(2,1)}, bf16[4096,768]{1,0:T(8,128)(2,1)}, u32[]{:S(2)}, u32[]{:S(2)}) collective-permute-start(bf16[4096,768]{1,0:T(8,128)(2,1)} %bitcast.12), channel_id=1, source_target_pairs={{0,1},{1,0},{2,3},{3,2},{4,5},{5,4},{6,7},{7,6},{8,9},{9,8},{10,11... | collective-permute-start | bytes 18874376 | tf_op jit(solution)/shard_map/ppermute | solution.py:369
  1.2 38.5 %collective-permute-start.6 = (bf16[768,4096]{1,0:T(8,128)(2,1)}, bf16[768,4096]{1,0:T(8,128)(2,1)}, u32[]{:S(2)}, u32[]{:S(2)}) collective-permute-start(bf16[768,4096]{1,0:T(8,128)(2,1)} %bitcast.15), channel_id=1, source_target_pairs={{0,1},{1,0},{2,3},{3,2},{4,5},{5,4},{6,7},{7,6},{8,9},{9,8},{10,11... | collective-permute-start | bytes 18874376 | tf_op jit(solution)/shard_map/ppermute | solution.py:369
  2.9 16.2 %collective-permute-start.1 = (bf16[128,2048]{1,0:T(8,128)(2,1)S(1)}, bf16[128,2048]{1,0:T(8,128)(2,1)S(1)}, u32[]{:S(2)}, u32[]{:S(2)}) collective-permute-start(bf16[128,2048]{1,0:T(8,128)(2,1)S(1)} %get-tuple-element.88.refs_1_), channel_id=1, source_target_pairs={{0,4},{1,5},{2,6},{3,7},{4,12},{5,13},{6,14},{7,15},{8,0},{9,1},{1... | collective-permute-start | bytes 1572872 | tf_op jit(solution)/shard_map/ppermute | solution.py:369
  5.6 14.4 %copy-start.56 = (bf16[128,4096]{1,0:T(8,128)(2,1)S(1)}, bf16[128,4096]{1,0:T(8,128)(2,1)}, u32[]{:S(2)}) copy-start(bf16[128,4096]{1,0:T(8,128)(2,1)} %param.8) | copy-start | bytes 3145732
  9.3 10.8 %copy-start.49 = (bf16[96,4096]{1,0:T(8,128)(2,1)}, bf16[96,4096]{1,0:T(8,128)(2,1)S(1)}, u32[]{:S(2)}) copy-start(bf16[96,4096]{1,0:T(8,128)(2,1)S(1)} %get-tuple-element.45.refs_0_) | copy-start | bytes 2359300
  9.4 27.7 %copy-start.39 = (bf16[192,128]{1,0:T(8,128)(2,1)}, bf16[192,128]{1,0:T(8,128)(2,1)S(1)}, u32[]{:S(2)}) copy-start(bf16[192,128]{1,0:T(8,128)(2,1)S(1)} %get-tuple-element.47.pick.mix) | copy-start | bytes 147460
  9.4 29.5 %collective-permute-start.3 = (bf16[96,4096]{1,0:T(8,128)(2,1)}, bf16[96,4096]{1,0:T(8,128)(2,1)}, u32[]{:S(2)}, u32[]{:S(2)}) collective-permute-start(bf16[96,4096]{1,0:T(8,128)(2,1)} %get-tuple-element.49), channel_id=1, source_target_pairs={{0,2},{1,3},{2,0},{3,1},{4,6},{5,7},{6,4},{7,5},{8,10},{9,11},{10,... | collective-permute-start | bytes 2359304 | tf_op jit(solution)/shard_map/ppermute | solution.py:369
  19.2 19.7 %copy-start.29 = (bf16[128,2048]{1,0:T(8,128)(2,1)}, bf16[128,2048]{1,0:T(8,128)(2,1)S(1)}, u32[]{:S(2)}) copy-start(bf16[128,2048]{1,0:T(8,128)(2,1)S(1)} %collective-permute-done.1.refs_1_.refs_0_) | copy-start | bytes 1572868
  19.2 15.3 %collective-permute-start = (bf16[128,2176]{1,0:T(8,128)(2,1)S(1)}, bf16[128,2176]{1,0:T(8,128)(2,1)S(1)}, u32[]{:S(2)}, u32[]{:S(2)}) collective-permute-start(bf16[128,2176]{1,0:T(8,128)(2,1)S(1)} %fusion.1.refs_0_), channel_id=1, source_target_pairs={{0,4},{1,5},{2,6},{3,7},{4,12},{5,13},{6,14},{7,15},{8,0},{9,1},{1... | collective-permute-start | bytes 1671176 | tf_op jit(solution)/shard_map/ppermute | solution.py:369
  20.1 19.6 %copy-start.1 = (bf16[128,2048]{1,0:T(8,128)(2,1)}, bf16[128,2048]{1,0:T(8,128)(2,1)S(1)}, u32[]{:S(2)}) copy-start(bf16[128,2048]{1,0:T(8,128)(2,1)S(1)} %get-tuple-element.86.refs_1_.refs_0_) | copy-start | bytes 1572868
  20.1 19.6 %copy-start.12 = (bf16[128,2048]{1,0:T(8,128)(2,1)}, bf16[128,2048]{1,0:T(8,128)(2,1)S(1)}, u32[]{:S(2)}) copy-start(bf16[128,2048]{1,0:T(8,128)(2,1)S(1)} %get-tuple-element.87.refs_0_) | copy-start | bytes 1572868
  34.5 34.3 %collective-permute-start.9 = (bf16[96,4096]{1,0:T(8,128)(2,1)}, bf16[96,4096]{1,0:T(8,128)(2,1)}, u32[]{:S(2)}, u32[]{:S(2)}) collective-permute-start(bf16[96,4096]{1,0:T(8,128)(2,1)} %get-tuple-element.51), channel_id=1, source_target_pairs={{0,2},{1,3},{2,0},{3,1},{4,6},{5,7},{6,4},{7,5},{8,10},{9,11},{10,... | collective-permute-start | bytes 2359304 | tf_op jit(solution)/shard_map/ppermute | solution.py:369
  38.9 80.4 %copy-start.44 = (bf16[192,128]{1,0:T(8,128)(2,1)}, bf16[192,128]{1,0:T(8,128)(2,1)S(1)}, u32[]{:S(2)}) copy-start(bf16[192,128]{1,0:T(8,128)(2,1)S(1)} %get-tuple-element.60.pick.mix) | copy-start | bytes 147460
  38.9 16.7 %collective-permute-start.2 = (bf16[128,2176]{1,0:T(8,128)(2,1)}, bf16[128,2176]{1,0:T(8,128)(2,1)S(1)}, u32[]{:S(2)}, u32[]{:S(2)}) collective-permute-start(bf16[128,2176]{1,0:T(8,128)(2,1)} %tie.23), channel_id=1, source_target_pairs={{0,4},{1,5},{2,6},{3,7},{4,12},{5,13},{6,14},{7,15},{8,0},{9,1},{1... | collective-permute-start | bytes 1671176 | tf_op jit(solution)/shard_map/ppermute | solution.py:369
  39.8 24.5 %collective-permute-start.7 = (bf16[128,2048]{1,0:T(8,128)(2,1)}, bf16[128,2048]{1,0:T(8,128)(2,1)S(1)}, u32[]{:S(2)}, u32[]{:S(2)}) collective-permute-start(bf16[128,2048]{1,0:T(8,128)(2,1)} %tie.24), channel_id=1, source_target_pairs={{0,4},{1,5},{2,6},{3,7},{4,12},{5,13},{6,14},{7,15},{8,0},{9,1},{1... | collective-permute-start | bytes 1572872 | tf_op jit(solution)/shard_map/ppermute | solution.py:369
  55.6 11.7 %copy-start.23 = (bf16[128,2176]{1,0:T(8,128)(2,1)}, bf16[128,2176]{1,0:T(8,128)(2,1)S(1)}, u32[]{:S(2)}) copy-start(bf16[128,2176]{1,0:T(8,128)(2,1)S(1)} %collective-permute-done.2.refs_0_) | copy-start | bytes 1671172
  67.3 89.4 %copy-start.46 = (bf16[192,128]{1,0:T(8,128)(2,1)}, bf16[192,128]{1,0:T(8,128)(2,1)S(1)}, u32[]{:S(2)}) copy-start(bf16[192,128]{1,0:T(8,128)(2,1)S(1)} %get-tuple-element.72.pick.mix) | copy-start | bytes 147460
  67.3 24.4 %collective-permute-start.8 = (bf16[128,2176]{1,0:T(8,128)(2,1)}, bf16[128,2176]{1,0:T(8,128)(2,1)S(1)}, u32[]{:S(2)}, u32[]{:S(2)}) collective-permute-start(bf16[128,2176]{1,0:T(8,128)(2,1)} %tie.25), channel_id=1, source_target_pairs={{0,4},{1,5},{2,6},{3,7},{4,12},{5,13},{6,14},{7,15},{8,0},{9,1},{1... | collective-permute-start | bytes 1671176 | tf_op jit(solution)/shard_map/ppermute | solution.py:369
  68.2 28.3 %collective-permute-start.11 = (bf16[96,4096]{1,0:T(8,128)(2,1)}, bf16[96,4096]{1,0:T(8,128)(2,1)}, u32[]{:S(2)}, u32[]{:S(2)}) collective-permute-start(bf16[96,4096]{1,0:T(8,128)(2,1)} %copy-done.54), channel_id=1, source_target_pairs={{0,2},{1,3},{2,0},{3,1},{4,6},{5,7},{6,4},{7,5},{8,10},{9,11},{10,... | collective-permute-start | bytes 2359304 | tf_op jit(solution)/shard_map/ppermute | solution.py:369
  68.7 23.0 %collective-permute-start.10 = (bf16[128,2048]{1,0:T(8,128)(2,1)}, bf16[128,2048]{1,0:T(8,128)(2,1)S(1)}, u32[]{:S(2)}, u32[]{:S(2)}) collective-permute-start(bf16[128,2048]{1,0:T(8,128)(2,1)} %tie.26), channel_id=1, source_target_pairs={{0,4},{1,5},{2,6},{3,7},{4,12},{5,13},{6,14},{7,15},{8,0},{9,1},{1... | collective-permute-start | bytes 1572872 | tf_op jit(solution)/shard_map/ppermute | solution.py:369
  72.0 49.4 %collective-permute-start.12 = (bf16[96,4096]{1,0:T(8,128)(2,1)}, bf16[96,4096]{1,0:T(8,128)(2,1)}, u32[]{:S(2)}, u32[]{:S(2)}) collective-permute-start(bf16[96,4096]{1,0:T(8,128)(2,1)} %copy-done.55), channel_id=1, source_target_pairs={{0,2},{1,3},{2,0},{3,1},{4,6},{5,7},{6,4},{7,5},{8,10},{9,11},{10,... | collective-permute-start | bytes 2359304 | tf_op jit(solution)/shard_map/ppermute | solution.py:369
  95.4 30.2 %collective-permute-start.13 = (bf16[96,4096]{1,0:T(8,128)(2,1)}, bf16[96,4096]{1,0:T(8,128)(2,1)}, u32[]{:S(2)}, u32[]{:S(2)}) collective-permute-start(bf16[96,4096]{1,0:T(8,128)(2,1)} %get-tuple-element.55), channel_id=1, source_target_pairs={{0,2},{1,3},{2,0},{3,1},{4,6},{5,7},{6,4},{7,5},{8,10},{9,11},{10,... | collective-permute-start | bytes 2359304 | tf_op jit(solution)/shard_map/ppermute | solution.py:369
  96.5 16.0 %collective-permute-start.15 = (bf16[128,2048]{1,0:T(8,128)(2,1)}, bf16[128,2048]{1,0:T(8,128)(2,1)S(1)}, u32[]{:S(2)}, u32[]{:S(2)}) collective-permute-start(bf16[128,2048]{1,0:T(8,128)(2,1)} %tie.29), channel_id=1, source_target_pairs={{0,4},{1,5},{2,6},{3,7},{4,12},{5,13},{6,14},{7,15},{8,0},{9,1},{1... | collective-permute-start | bytes 1572872 | tf_op jit(solution)/shard_map/ppermute | solution.py:369
  96.8 22.5 %collective-permute-start.14 = (bf16[128,2048]{1,0:T(8,128)(2,1)}, bf16[128,2048]{1,0:T(8,128)(2,1)S(1)}, u32[]{:S(2)}, u32[]{:S(2)}) collective-permute-start(bf16[128,2048]{1,0:T(8,128)(2,1)} %tie.27), channel_id=1, source_target_pairs={{0,4},{1,5},{2,6},{3,7},{4,12},{5,13},{6,14},{7,15},{8,0},{9,1},{1... | collective-permute-start | bytes 1572872 | tf_op jit(solution)/shard_map/ppermute | solution.py:369
  112.5 8.9 %copy-start.27 = (bf16[128,2048]{1,0:T(8,128)(2,1)}, bf16[128,2048]{1,0:T(8,128)(2,1)S(1)}, u32[]{:S(2)}) copy-start(bf16[128,2048]{1,0:T(8,128)(2,1)S(1)} %collective-permute-done.15.refs_1_.refs_0_) | copy-start | bytes 1572868
  120.7 35.3 %collective-permute-start.16 = (bf16[96,4096]{1,0:T(8,128)(2,1)S(1)}, bf16[96,4096]{1,0:T(8,128)(2,1)}, u32[]{:S(2)}, u32[]{:S(2)}) collective-permute-start(bf16[96,4096]{1,0:T(8,128)(2,1)S(1)} %get-tuple-element.62), channel_id=1, source_target_pairs={{0,2},{1,3},{2,0},{3,1},{4,6},{5,7},{6,4},{7,5},{8,10},{9,11},{10,... | collective-permute-start | bytes 2359304 | tf_op jit(solution)/shard_map/ppermute | solution.py:369
  121.4 35.3 %collective-permute-start.22 = (bf16[128,2048]{1,0:T(8,128)(2,1)}, bf16[128,2048]{1,0:T(8,128)(2,1)S(1)}, u32[]{:S(2)}, u32[]{:S(2)}) collective-permute-start(bf16[128,2048]{1,0:T(8,128)(2,1)} %tie.35), channel_id=1, source_target_pairs={{0,4},{1,5},{2,6},{3,7},{4,12},{5,13},{6,14},{7,15},{8,0},{9,1},{1... | collective-permute-start | bytes 1572872 | tf_op jit(solution)/shard_map/ppermute | solution.py:369
  122.3 34.4 %collective-permute-start.20 = (bf16[128,2048]{1,0:T(8,128)(2,1)}, bf16[128,2048]{1,0:T(8,128)(2,1)S(1)}, u32[]{:S(2)}, u32[]{:S(2)}) collective-permute-start(bf16[128,2048]{1,0:T(8,128)(2,1)} %tie.33), channel_id=1, source_target_pairs={{0,4},{1,5},{2,6},{3,7},{4,12},{5,13},{6,14},{7,15},{8,0},{9,1},{1... | collective-permute-start | bytes 1572872 | tf_op jit(solution)/shard_map/ppermute | solution.py:369
  156.1 16.8 %collective-permute-start.17 = (bf16[96,4096]{1,0:T(8,128)(2,1)}, bf16[96,4096]{1,0:T(8,128)(2,1)S(1)}, u32[]{:S(2)}, u32[]{:S(2)}) collective-permute-start(bf16[96,4096]{1,0:T(8,128)(2,1)} %tie.30), channel_id=1, source_target_pairs={{0,2},{1,3},{2,0},{3,1},{4,6},{5,7},{6,4},{7,5},{8,10},{9,11},{10,... | collective-permute-start | bytes 2359304 | tf_op jit(solution)/shard_map/ppermute | solution.py:369
  158.5 18.6 %collective-permute-start.21 = (bf16[128,2048]{1,0:T(8,128)(2,1)}, bf16[128,2048]{1,0:T(8,128)(2,1)}, u32[]{:S(2)}, u32[]{:S(2)}) collective-permute-start(bf16[128,2048]{1,0:T(8,128)(2,1)} %tie.34), channel_id=1, source_target_pairs={{0,4},{1,5},{2,6},{3,7},{4,12},{5,13},{6,14},{7,15},{8,0},{9,1},{1... | collective-permute-start | bytes 1572872 | tf_op jit(solution)/shard_map/ppermute | solution.py:369
  159.4 15.0 %copy-start.16 = (bf16[96,4096]{1,0:T(8,128)(2,1)S(1)}, bf16[96,4096]{1,0:T(8,128)(2,1)}, u32[]{:S(2)}) copy-start(bf16[96,4096]{1,0:T(8,128)(2,1)} %get-tuple-element.70.refs_0_) | copy-start | bytes 2359300
  159.4 53.3 %collective-permute-start.23 = (bf16[128,2048]{1,0:T(8,128)(2,1)}, bf16[128,2048]{1,0:T(8,128)(2,1)}, u32[]{:S(2)}, u32[]{:S(2)}) collective-permute-start(bf16[128,2048]{1,0:T(8,128)(2,1)} %tie.36), channel_id=1, source_target_pairs={{0,4},{1,5},{2,6},{3,7},{4,12},{5,13},{6,14},{7,15},{8,0},{9,1},{1... | collective-permute-start | bytes 1572872 | tf_op jit(solution)/shard_map/ppermute | solution.py:369
  173.8 44.5 %collective-permute-start.18 = (bf16[96,4096]{1,0:T(8,128)(2,1)}, bf16[96,4096]{1,0:T(8,128)(2,1)S(1)}, u32[]{:S(2)}, u32[]{:S(2)}) collective-permute-start(bf16[96,4096]{1,0:T(8,128)(2,1)} %tie.31), channel_id=1, source_target_pairs={{0,2},{1,3},{2,0},{3,1},{4,6},{5,7},{6,4},{7,5},{8,10},{9,11},{10,... | collective-permute-start | bytes 2359304 | tf_op jit(solution)/shard_map/ppermute | solution.py:369
  177.1 35.7 %copy-start = (bf16[96,4096]{1,0:T(8,128)(2,1)S(1)}, bf16[96,4096]{1,0:T(8,128)(2,1)}, u32[]{:S(2)}) copy-start(bf16[96,4096]{1,0:T(8,128)(2,1)} %get-tuple-element.56.refs_2_.refs_0_) | copy-start | bytes 2359300
  177.1 41.2 %collective-permute-start.29 = (bf16[128,2048]{1,0:T(8,128)(2,1)}, bf16[128,2048]{1,0:T(8,128)(2,1)}, u32[]{:S(2)}, u32[]{:S(2)}) collective-permute-start(bf16[128,2048]{1,0:T(8,128)(2,1)} %tie.39), channel_id=1, source_target_pairs={{0,8},{1,9},{2,10},{3,11},{4,0},{5,1},{6,2},{7,3},{8,12},{9,13},{1... | collective-permute-start | bytes 1572872 | tf_op jit(solution)/shard_map/ppermute | solution.py:369
  178.6 39.6 %copy-start.19 = (bf16[96,4096]{1,0:T(8,128)(2,1)S(1)}, bf16[96,4096]{1,0:T(8,128)(2,1)}, u32[]{:S(2)}) copy-start(bf16[96,4096]{1,0:T(8,128)(2,1)} %get-tuple-element.69.refs_0_) | copy-start | bytes 2359300
  212.8 9.4 %collective-permute-start.26 = (bf16[128,2048]{1,0:T(8,128)(2,1)}, bf16[128,2048]{1,0:T(8,128)(2,1)S(1)}, u32[]{:S(2)}, u32[]{:S(2)}) collective-permute-start(bf16[128,2048]{1,0:T(8,128)(2,1)} %tie.38), channel_id=1, source_target_pairs={{0,8},{1,9},{2,10},{3,11},{4,0},{5,1},{6,2},{7,3},{8,12},{9,13},{1... | collective-permute-start | bytes 1572872 | tf_op jit(solution)/shard_map/ppermute | solution.py:369
  216.2 13.2 %collective-permute-start.24 = (bf16[96,4096]{1,0:T(8,128)(2,1)S(1)}, bf16[96,4096]{1,0:T(8,128)(2,1)S(1)}, u32[]{:S(2)}, u32[]{:S(2)}) collective-permute-start(bf16[96,4096]{1,0:T(8,128)(2,1)S(1)} %get-tuple-element.67), channel_id=1, source_target_pairs={{0,2},{1,3},{2,0},{3,1},{4,6},{5,7},{6,4},{7,5},{8,10},{9,11},{10,... | collective-permute-start | bytes 2359304 | tf_op jit(solution)/shard_map/ppermute | solution.py:369
  217.7 20.2 %collective-permute-start.32 = (bf16[96,4096]{1,0:T(8,128)(2,1)}, bf16[96,4096]{1,0:T(8,128)(2,1)}, u32[]{:S(2)}, u32[]{:S(2)}) collective-permute-start(bf16[96,4096]{1,0:T(8,128)(2,1)} %copy-done.52), channel_id=1, source_target_pairs={{0,2},{1,3},{2,0},{3,1},{4,6},{5,7},{6,4},{7,5},{8,10},{9,11},{10,... | collective-permute-start | bytes 2359304 | tf_op jit(solution)/shard_map/ppermute | solution.py:369
  221.1 16.8 %collective-permute-start.30 = (bf16[128,2048]{1,0:T(8,128)(2,1)}, bf16[128,2048]{1,0:T(8,128)(2,1)}, u32[]{:S(2)}, u32[]{:S(2)}) collective-permute-start(bf16[128,2048]{1,0:T(8,128)(2,1)} %back_sum.20), channel_id=1, source_target_pairs={{0,8},{1,9},{2,10},{3,11},{4,0},{5,1},{6,2},{7,3},{8,12},{9,13},{1... | collective-permute-start | bytes 1572872 | tf_op jit(solution)/shard_map/ppermute | solution.py:369
  223.7 14.2 %collective-permute-start.27 = (bf16[128,2048]{1,0:T(8,128)(2,1)}, bf16[128,2048]{1,0:T(8,128)(2,1)}, u32[]{:S(2)}, u32[]{:S(2)}) collective-permute-start(bf16[128,2048]{1,0:T(8,128)(2,1)} %back_sum.17), channel_id=1, source_target_pairs={{0,8},{1,9},{2,10},{3,11},{4,0},{5,1},{6,2},{7,3},{8,12},{9,13},{1... | collective-permute-start | bytes 1572872 | tf_op jit(solution)/shard_map/ppermute | solution.py:369
  230.3 38.1 %collective-permute-start.25 = (bf16[96,4096]{1,0:T(8,128)(2,1)}, bf16[96,4096]{1,0:T(8,128)(2,1)S(1)}, u32[]{:S(2)}, u32[]{:S(2)}) collective-permute-start(bf16[96,4096]{1,0:T(8,128)(2,1)} %tie.37), channel_id=1, source_target_pairs={{0,2},{1,3},{2,0},{3,1},{4,6},{5,7},{6,4},{7,5},{8,10},{9,11},{10,... | collective-permute-start | bytes 2359304 | tf_op jit(solution)/shard_map/ppermute | solution.py:369
  230.8 47.1 %collective-permute-start.19 = (bf16[96,4096]{1,0:T(8,128)(2,1)}, bf16[96,4096]{1,0:T(8,128)(2,1)S(1)}, u32[]{:S(2)}, u32[]{:S(2)}) collective-permute-start(bf16[96,4096]{1,0:T(8,128)(2,1)} %tie.32), channel_id=1, source_target_pairs={{0,2},{1,3},{2,0},{3,1},{4,6},{5,7},{6,4},{7,5},{8,10},{9,11},{10,... | collective-permute-start | bytes 2359304 | tf_op jit(solution)/shard_map/ppermute | solution.py:369
  269.2 20.7 %collective-permute-start.35 = (bf16[96,4096]{1,0:T(8,128)(2,1)}, bf16[96,4096]{1,0:T(8,128)(2,1)S(1)}, u32[]{:S(2)}, u32[]{:S(2)}) collective-permute-start(bf16[96,4096]{1,0:T(8,128)(2,1)} %tie.42), channel_id=1, source_target_pairs={{0,2},{1,3},{2,0},{3,1},{4,6},{5,7},{6,4},{7,5},{8,10},{9,11},{10,... | collective-permute-start | bytes 2359304 | tf_op jit(solution)/shard_map/ppermute | solution.py:369
  273.6 16.4 %copy-start.15 = (bf16[96,4096]{1,0:T(8,128)(2,1)S(1)}, bf16[96,4096]{1,0:T(8,128)(2,1)}, u32[]{:S(2)}) copy-start(bf16[96,4096]{1,0:T(8,128)(2,1)} %get-tuple-element.85.refs_0_) | copy-start | bytes 2359300
  273.6 16.4 %copy-start.43 = (bf16[192,128]{1,0:T(8,128)(2,1)S(1)}, bf16[192,128]{1,0:T(8,128)(2,1)}, u32[]{:S(2)}) copy-start(bf16[192,128]{1,0:T(8,128)(2,1)} %copy-done.41) | copy-start | bytes 147460
  273.6 17.6 %collective-permute-start.31 = (bf16[128,2048]{1,0:T(8,128)(2,1)}, bf16[128,2048]{1,0:T(8,128)(2,1)}, u32[]{:S(2)}, u32[]{:S(2)}) collective-permute-start(bf16[128,2048]{1,0:T(8,128)(2,1)} %back_sum.21), channel_id=1, source_target_pairs={{0,8},{1,9},{2,10},{3,11},{4,0},{5,1},{6,2},{7,3},{8,12},{9,13},{1... | collective-permute-start | bytes 1572872 | tf_op jit(solution)/shard_map/ppermute | solution.py:369
  276.4 23.6 %collective-permute-start.28 = (bf16[128,2048]{1,0:T(8,128)(2,1)}, bf16[128,2048]{1,0:T(8,128)(2,1)}, u32[]{:S(2)}, u32[]{:S(2)}) collective-permute-start(bf16[128,2048]{1,0:T(8,128)(2,1)} %back_sum.18), channel_id=1, source_target_pairs={{0,8},{1,9},{2,10},{3,11},{4,0},{5,1},{6,2},{7,3},{8,12},{9,13},{1... | collective-permute-start | bytes 1572872 | tf_op jit(solution)/shard_map/ppermute | solution.py:369
  278.8 26.4 %collective-permute-start.33 = (bf16[96,4096]{1,0:T(8,128)(2,1)}, bf16[96,4096]{1,0:T(8,128)(2,1)S(1)}, u32[]{:S(2)}, u32[]{:S(2)}) collective-permute-start(bf16[96,4096]{1,0:T(8,128)(2,1)} %tie.40), channel_id=1, source_target_pairs={{0,2},{1,3},{2,0},{3,1},{4,6},{5,7},{6,4},{7,5},{8,10},{9,11},{10,... | collective-permute-start | bytes 2359304 | tf_op jit(solution)/shard_map/ppermute | solution.py:369
  291.2 20.1 %collective-permute-start.40 = (bf16[128,2048]{1,0:T(8,128)(2,1)}, bf16[128,2048]{1,0:T(8,128)(2,1)}, u32[]{:S(2)}, u32[]{:S(2)}) collective-permute-start(bf16[128,2048]{1,0:T(8,128)(2,1)} %tie.45), channel_id=1, source_target_pairs={{0,8},{1,9},{2,10},{3,11},{4,0},{5,1},{6,2},{7,3},{8,12},{9,13},{1... | collective-permute-start | bytes 1572872 | tf_op jit(solution)/shard_map/ppermute | solution.py:369
  292.4 18.8 %copy-start.21 = (bf16[96,4096]{1,0:T(8,128)(2,1)S(1)}, bf16[96,4096]{1,0:T(8,128)(2,1)}, u32[]{:S(2)}) copy-start(bf16[96,4096]{1,0:T(8,128)(2,1)} %get-tuple-element.84.refs_0_) | copy-start | bytes 2359300
  292.4 18.8 %copy-start.47 = (bf16[192,128]{1,0:T(8,128)(2,1)S(1)}, bf16[192,128]{1,0:T(8,128)(2,1)}, u32[]{:S(2)}) copy-start(bf16[192,128]{1,0:T(8,128)(2,1)} %copy-done.46) | copy-start | bytes 147460
  300.0 22.1 %collective-permute-start.37 = (bf16[128,2048]{1,0:T(8,128)(2,1)}, bf16[128,2048]{1,0:T(8,128)(2,1)}, u32[]{:S(2)}, u32[]{:S(2)}) collective-permute-start(bf16[128,2048]{1,0:T(8,128)(2,1)} %tie.44), channel_id=1, source_target_pairs={{0,8},{1,9},{2,10},{3,11},{4,0},{5,1},{6,2},{7,3},{8,12},{9,13},{1... | collective-permute-start | bytes 1572872 | tf_op jit(solution)/shard_map/ppermute | solution.py:369
  300.9 25.3 %collective-permute-start.36 = (bf16[96,4096]{1,0:T(8,128)(2,1)}, bf16[96,4096]{1,0:T(8,128)(2,1)}, u32[]{:S(2)}, u32[]{:S(2)}) collective-permute-start(bf16[96,4096]{1,0:T(8,128)(2,1)} %tie.43), channel_id=1, source_target_pairs={{0,2},{1,3},{2,0},{3,1},{4,6},{5,7},{6,4},{7,5},{8,10},{9,11},{10,... | collective-permute-start | bytes 2359304 | tf_op jit(solution)/shard_map/ppermute | solution.py:369
  305.2 19.2 %copy-start.11 = (bf16[96,4096]{1,0:T(8,128)(2,1)}, bf16[96,4096]{1,0:T(8,128)(2,1)S(1)}, u32[]{:S(2)}) copy-start(bf16[96,4096]{1,0:T(8,128)(2,1)S(1)} %collective-permute-done.33.refs_1_) | copy-start | bytes 2359300
  313.6 14.1 %copy-start.20 = (bf16[96,4096]{1,0:T(8,128)(2,1)S(1)}, bf16[96,4096]{1,0:T(8,128)(2,1)}, u32[]{:S(2)}) copy-start(bf16[96,4096]{1,0:T(8,128)(2,1)} %get-tuple-element.81.refs_0_) | copy-start | bytes 2359300
  313.6 14.1 %copy-start.45 = (bf16[192,128]{1,0:T(8,128)(2,1)S(1)}, bf16[192,128]{1,0:T(8,128)(2,1)}, u32[]{:S(2)}) copy-start(bf16[192,128]{1,0:T(8,128)(2,1)} %copy-done.44) | copy-start | bytes 147460
  313.6 14.1 %collective-permute-start.41 = (bf16[128,2048]{1,0:T(8,128)(2,1)}, bf16[128,2048]{1,0:T(8,128)(2,1)}, u32[]{:S(2)}, u32[]{:S(2)}) collective-permute-start(bf16[128,2048]{1,0:T(8,128)(2,1)} %back_sum.28), channel_id=1, source_target_pairs={{0,8},{1,9},{2,10},{3,11},{4,0},{5,1},{6,2},{7,3},{8,12},{9,13},{1... | collective-permute-start | bytes 1572872 | tf_op jit(solution)/shard_map/ppermute | solution.py:369
  324.4 10.1 %collective-permute-start.38 = (bf16[128,2048]{1,0:T(8,128)(2,1)}, bf16[128,2048]{1,0:T(8,128)(2,1)}, u32[]{:S(2)}, u32[]{:S(2)}) collective-permute-start(bf16[128,2048]{1,0:T(8,128)(2,1)} %back_sum.25), channel_id=1, source_target_pairs={{0,8},{1,9},{2,10},{3,11},{4,0},{5,1},{6,2},{7,3},{8,12},{9,13},{1... | collective-permute-start | bytes 1572872 | tf_op jit(solution)/shard_map/ppermute | solution.py:369
  325.3 17.4 %collective-permute-start.34 = (bf16[96,4096]{1,0:T(8,128)(2,1)}, bf16[96,4096]{1,0:T(8,128)(2,1)S(1)}, u32[]{:S(2)}, u32[]{:S(2)}) collective-permute-start(bf16[96,4096]{1,0:T(8,128)(2,1)} %tie.41), channel_id=1, source_target_pairs={{0,2},{1,3},{2,0},{3,1},{4,6},{5,7},{6,4},{7,5},{8,10},{9,11},{10,... | collective-permute-start | bytes 2359304 | tf_op jit(solution)/shard_map/ppermute | solution.py:369
  327.7 9.7 %copy-start.3 = (bf16[96,4096]{1,0:T(8,128)(2,1)S(1)}, bf16[96,4096]{1,0:T(8,128)(2,1)}, u32[]{:S(2)}) copy-start(bf16[96,4096]{1,0:T(8,128)(2,1)} %copy-done.2) | copy-start | bytes 2359300
  329.4 13.3 %collective-permute-start.42 = (bf16[128,2048]{1,0:T(8,128)(2,1)S(1)}, bf16[128,2048]{1,0:T(8,128)(2,1)S(1)}, u32[]{:S(2)}, u32[]{:S(2)}) collective-permute-start(bf16[128,2048]{1,0:T(8,128)(2,1)S(1)} %back_sum.29), channel_id=1, source_target_pairs={{0,8},{1,9},{2,10},{3,11},{4,0},{5,1},{6,2},{7,3},{8,12},{9,13},{1... | collective-permute-start | bytes 1572872 | tf_op jit(solution)/shard_map/ppermute | solution.py:369
  336.2 10.1 %collective-permute-start.39 = (bf16[128,2048]{1,0:T(8,128)(2,1)S(1)}, bf16[128,2048]{1,0:T(8,128)(2,1)S(1)}, u32[]{:S(2)}, u32[]{:S(2)}) collective-permute-start(bf16[128,2048]{1,0:T(8,128)(2,1)S(1)} %back_sum.26), channel_id=1, source_target_pairs={{0,8},{1,9},{2,10},{3,11},{4,0},{5,1},{6,2},{7,3},{8,12},{9,13},{1... | collective-permute-start | bytes 1572872 | tf_op jit(solution)/shard_map/ppermute | solution.py:369
  (37 other events, 71.3 us)
